TPU v7x, 128 devices: a whole 4x4x4 slice. The times are simulated.
128 devices in a mesh: row: 8 (over z, y_lo), col: 16 (over y_hi, x, core).
Axes of the slice: x: 4, y: 4 (y_hi: 2, y_lo: 2; y = y_hi * 2 + y_lo), z: 4, core: 2. Of those that a mesh axis runs over, the one named last changes fastest.
Arguments:
- integrals: float32 [3072, 16384], P('row', 'col'), may hold values from -0.046875 to 0.046875
- amplitudes: float32 [32, 512, 8, 512], P('row', 'col'), may hold values from -6 to 6
- driver: float32 [3072, 4096], P('row', 'col'), may hold values from -6 to 6
- occ_rows: float32 [6], replicated, may hold values from -2 to -0.5
- occ_cols: float32 [8], replicated, may hold values from -2 to -0.5
- virtual: float32 [512], replicated, may hold values from 0.2 to 3
Outputs:
- updated: float32 [3072, 4096], P('row', 'col')
All inputs are finite; a program needn't handle non-finite values.
Results may differ from a plain program's by a relative error of at most 0.000062.
Values sent between devices are 32-bit elements; how exact they have to be, the bound alone decides.
No kernel may reach another device: no remote copies, remote signals or barrier semaphores. Data moves between devices by JAX's collectives and lax.ppermute only.
A program may use at most 128 MiB of HBM per device.

v0:
```python
import jax
import jax.numpy as jnp
from jax import lax
from jax.sharding import PartitionSpec as P


def shards(integrals, amplitudes, driver, occ_rows, occ_cols, virtual):
    k_local, c_local, occ_j, virt_b = amplitudes.shape
    flat = amplitudes.reshape(k_local, c_local, occ_j * virt_b)
    height = driver.shape[0]
    width = driver.shape[1]
    moved = lax.all_to_all(flat, "col", split_axis=2, concat_axis=1, tiled=True)
    panel = moved.reshape(moved.shape[0] * moved.shape[1], moved.shape[2])
    column_panel = lax.all_gather(panel, "row", axis=0, tiled=True)
    cycle = jnp.dot(
        lax.all_gather(integrals, "col", axis=1, tiled=True),
        column_panel,
        precision=lax.Precision.HIGHEST,
        preferred_element_type=jnp.float32,
    )
    row_energy = (occ_rows[:, None] - virtual[None, :]).reshape(-1)
    col_energy = (occ_cols[:, None] - virtual[None, :]).reshape(-1)
    row_part = lax.dynamic_slice_in_dim(row_energy, lax.axis_index("row") * height, height, 0)
    col_part = lax.dynamic_slice_in_dim(col_energy, lax.axis_index("col") * width, width, 0)
    denominator = row_part[:, None] + col_part[None, :]
    return (driver + cycle) / denominator


def solution(mesh):
    in_specs = (P("row", "col"), P("row", "col", None, None), P("row", "col"), P(), P(), P())
    out_specs = P("row", "col")
    return jax.shard_map(shards, mesh=mesh, in_specs=in_specs, out_specs=out_specs, check_vma=False)
```

profile of v0, /device:TPU:1, one launch (start us, length us, event | category | flops | bytes accessed | tf_op | source)
XLA Modules:
  0.0 589.5 jit_solution(12810584391186417538)
XLA Ops:
  6.5 0.0 all-gather.5.cloned.1.call-start
  6.5 6.3 %copy.8 = f32[4,32,8,512]{1,0,3,2:T(4,128)} copy(f32[4,32,8,512]{3,2,1,0:T(8,128)} %param.7) | data formatting | bytes 4194304 | tf_op args[1]
  12.8 8.5 %reshape.22 = f32[16,1,32768]{2,1,0:T(1,128)S(1)} reshape(f32[4096,4,32]{2,1,0:T(4,128)} %bitcast.14) | data formatting | bytes 4194304
  21.3 0.0 copy-start.1
  21.3 0.0 copy-start.2
  21.3 0.0 copy-start.3
  21.3 0.0 copy-start
  21.3 36.7 %all_to_all.15 = f32[16,1,32768]{2,1,0:T(1,128)} all-to-all(f32[16,1,32768]{2,1,0:T(1,128)S(1)} %reshape.22), channel_id=1, replica_groups=mesh['row'=8,'col'=16] {'col'}, dimensions={0} | all-to-all | bytes 4194304 | tf_op jit(solution)/shard_map/all_to_all | solution.py:12
  58.1 0.5 broadcast.9
  58.6 7.3 %reduce = f32[16,32768]{1,0:T(8,128)S(1)} reduce(f32[16,1,32768]{2,1,0:T(1,128)} %all_to_all.15, f32[]{:T(128)} %broadcast.9), dimensions={1}, to_apply=%all_to_all.11.reduce_sub_computation | reduce | bytes 4194308 | tf_op jit(solution)/shard_map/all_to_all | solution.py:12
  65.9 6.3 %reshape.23 = f32[4096,4,32]{2,1,0:T(4,128)} reshape(f32[16,32768]{1,0:T(8,128)S(1)} %reduce) | data formatting | bytes 4194304
  72.2 8.0 %copy.12 = f32[4,32,16,256]{3,1,2,0:T(8,128)} copy(f32[4,32,16,256]{1,0,3,2:T(4,128)} %bitcast.13) | data formatting | bytes 4194304 | tf_op jit(solution)/shard_map/all_to_all | solution.py:12
  80.2 0.0 all-gather.5.cloned.1.call-update
  80.2 0.2 all-gather.3.cloned.1.call-start
  80.5 0.5 all-gather.3.cloned.1.call-update
  81.0 0.0 copy-done.1
  81.0 0.0 copy-done.2
  81.0 0.1 subtract_bitcast_fusion
  81.1 0.0 copy-done.3
  81.1 0.1 broadcast_subtract_fusion
  81.2 0.1 dynamic_slice.7
  81.2 0.1 dynamic_slice.6
  81.3 322.8 %all-gather.5.cloned.1.call-done = f32[16384,256]{1,0:T(8,128)} async-done(((f32[2048,256]{1,0:T(8,128)}), f32[16384,256]{1,0:T(8,128)}) %all-gather.5.cloned.1.call-update) | async-done | bytes 16777232 | tf_op jit(solution)/shard_map/all_gather | solution.py:14
  404.1 152.9 %all-gather.3.cloned.1.call-done = f32[384,16384]{1,0:T(8,128)} async-done(((f32[384,1024]{1,0:T(8,128)}), f32[384,16384]{1,0:T(8,128)}) %all-gather.3.cloned.1.call-update) | async-done | bytes 25165840 | tf_op jit(solution)/shard_map/all_gather | solution.py:16
  557.0 0.0 copy-done
  557.0 25.6 %fusion = f32[384,256]{1,0:T(8,128)} fusion(f32[384,256]{1,0:T(8,128)S(1)} %copy-done, f32[384,16384]{1,0:T(8,128)} %all-gather.3.cloned.1.call-done, f32[16384,256]{1,0:T(8,128)} %all-gather.5.cloned.1.call-done, f32[256]{0:T(256)S(1)} %dynamic_slice.7, f32[384]{0:T(512)S(1)} %dynamic_slice.6), kind=kOutput, calls=%fused_computation.1 | convolution fusion | flops 19327647744 | bytes 42732032 | tf_op jit(solution)/shard_map/dot_general | solution.py:15
  (2 shorter events, 0.0 us)
Async XLA Ops:
  6.5 397.6 %all-gather.5.cloned.1.call-start = ((), (), s32[]{:S(2)}) async-start(), calls=%async_computation.2 | async-start | bytes 18874368 | tf_op jit(solution)/shard_map/all_gather | solution.py:14
  21.3 59.7 %copy-start.1 = (f32[512]{0:T(512)S(1)}, f32[512]{0:T(512)}, u32[]{:S(2)}) copy-start(f32[512]{0:T(512)} %param.11) | copy-start | bytes 6148
  21.3 59.7 %copy-start.2 = (f32[8]{0:T(128)S(1)}, f32[8]{0:T(128)}, u32[]{:S(2)}) copy-start(f32[8]{0:T(128)} %param.10) | copy-start | bytes 100
  21.3 59.8 %copy-start.3 = (f32[6]{0:T(128)S(1)}, f32[6]{0:T(128)}, u32[]{:S(2)}) copy-start(f32[6]{0:T(128)} %param.9) | copy-start | bytes 76
  21.3 535.7 %copy-start = (f32[384,256]{1,0:T(8,128)S(1)}, f32[384,256]{1,0:T(8,128)}, u32[]{:S(2)}) copy-start(f32[384,256]{1,0:T(8,128)} %param.8) | copy-start | bytes 1179652
  80.2 476.8 %all-gather.3.cloned.1.call-start = ((), (), s32[]{:S(2)}) async-start(), calls=%async_computation.1 | async-start | bytes 26738688 | tf_op jit(solution)/shard_map/all_gather | solution.py:16
Sparse Core Ops, SparseCore 0:
  80.3 323.7 all-gather.4
  406.6 150.3 all-gather.2
where the time goes:
time: 590 us; the launch traced here: 589 us
  waiting for transfers between devices  476 us (81%)
  blocking collectives  36.7 us (6%)
  local copies, waits for them, and re-layouts  29.8 us (5%)
  matrix products  25.6 us (4%)
  between operations  13.5 us (2%)
  other arithmetic  7.43 us (1%)
    all_gather x1, waiting for transfers between devices, shards(): column_panel = lax.all_gather(panel, 'row', axis=0, tiled=True)  323 us
    all_gather x1, waiting for transfers between devices, shards(): lax.all_gather(integrals, 'col', axis=1, tiled=True)  153 us
    all_to_all x1, blocking collectives, shards(): moved = lax.all_to_all(flat, 'col', split_axis=2, concat_axis=1, tiled=True)  36.7 us
    dot_general x1, matrix products, shards(): jnp.dot(lax.all_gather(integrals, 'col', axis=1, tiled=True), column_pane...  25.6 us
    unnamed x12, local copies, waits for them, and re-layouts  21.1 us
  transfers between devices with their start and end apart: 2, of which 2 were waited for; matrix products, arithmetic and copies ran while one was open for 0% of the time, Pallas kernels for 0%

commit v1 on v0

v1 whole, which is shorter than its diff:
```python
import jax
import jax.numpy as jnp
from jax import lax
from jax.sharding import Mesh, PartitionSpec as P

AXES = ("z", "yl", "yh", "x", "core")
SIZES = (4, 2, 2, 4, 2)


def device_index(z, y, x, core):
    return (((z * 2 + y % 2) * 2 + y // 2) * 4 + x) * 2 + core


def moves(target):
    pairs = []
    for z in range(4):
        for y in range(4):
            for x in range(4):
                for core in range(2):
                    pairs.append((device_index(z, y, x, core), device_index(*target(z, y, x, core))))
    return pairs


RING_Z = moves(lambda z, y, x, core: ((z + 1 - 2 * core) % 4, y, x, core))
RING_Y = moves(lambda z, y, x, core: (z, (y + 1 - 2 * core) % 4, x, core))
SWAP = moves(lambda z, y, x, core: (z, y, x, 1 - core))


def ring(own, pairs):
    held = [own]
    for _ in range(3):
        held.append(lax.ppermute(held[-1], AXES, pairs))
    return held


def in_order(held, position, core):
    step = 1 - 2 * core
    stacked = jnp.stack(held)
    return jnp.take(stacked, (step * (position - jnp.arange(4))) % 4, axis=0)


def shards(integrals, amplitudes, driver, occ_rows, occ_cols, virtual):
    z, yl, yh, x, core = (lax.axis_index(axis) for axis in AXES)
    y = yh * 2 + yl
    rows = driver.shape[0]
    amp = amplitudes.reshape(4, 32, 2, 4, 2, 2, 128).transpose(2, 5, 4, 0, 1, 3, 6).reshape(4, 2, 128, 512)
    amp = lax.all_to_all(amp, ("yh", "yl"), 0, 0, tiled=True)
    ints = integrals.reshape(rows, 2, 2, 4, 2, 32).transpose(3, 4, 0, 1, 2, 5).reshape(8, rows, 128)
    ints = lax.all_to_all(ints, ("x", "core"), 0, 0, tiled=True)
    amp = in_order(ring(amp, RING_Z), z, core)
    ints = in_order(ring(ints, RING_Y), y, core)
    lhs = ints.reshape(2, 2, 8, rows, 128).transpose(1, 3, 0, 2, 4).reshape(2 * rows, 2048)
    rhs = amp.reshape(4, 2, 2, 2, 4, 32, 512).transpose(0, 2, 4, 1, 5, 3, 6).reshape(2048, 1024)
    part = jnp.dot(lhs, rhs, precision=lax.Precision.HIGH, preferred_element_type=jnp.float32)
    part = part.reshape(2, rows, 2, 4, 128)
    other = lax.dynamic_index_in_dim(part, 1 - core, 2, keepdims=False)
    mine = lax.dynamic_index_in_dim(part, core, 2, keepdims=False)
    mine = mine + lax.ppermute(other, AXES, SWAP)
    mine = mine.transpose(0, 2, 1, 3).reshape(8, rows, 128)
    mine = lax.all_to_all(mine, ("yl", "x"), 0, 0, tiled=True)
    cycle = mine.reshape(2, 4, rows, 128).sum(axis=1).transpose(1, 0, 2).reshape(rows, 256)
    row_energy = (occ_rows[:, None] - virtual[None, :]).reshape(-1)
    col_energy = (occ_cols[:, None] - virtual[None, :]).reshape(-1)
    row_part = lax.dynamic_slice_in_dim(row_energy, (z * 2 + yl) * rows, rows, 0)
    col_part = lax.dynamic_slice_in_dim(col_energy, ((yh * 4 + x) * 2 + core) * 256, 256, 0)
    denominator = row_part[:, None] + col_part[None, :]
    return (driver + cycle) / denominator


def solution(mesh):
    fine = Mesh(mesh.devices.reshape(SIZES), AXES)
    row, col = ("z", "yl"), ("yh", "x", "core")
    in_specs = (P(row, col), P(row, col, None, None), P(row, col), P(), P(), P())
    return jax.shard_map(shards, mesh=fine, in_specs=in_specs, out_specs=P(row, col), check_vma=False)
```

time: 590 us -> 262 us (0.44)
  waiting for transfers between devices: 476 us -> 108 us
  local copies, waits for them, and re-layouts: 29.8 us -> 67.7 us
  starting transfers between devices: 0.22 us -> 37.4 us
  blocking collectives: 36.7 us -> 0 us
  other arithmetic: 7.43 us -> 24.5 us
  between operations: 13.5 us -> 0.17 us
    all_gather x2 -> x0, waiting for transfers between devices: 476 us -> none  [the longest x1 323 us: shards(): column_panel = lax.all_gather(panel, 'row', axis=0, tiled=True)]
    all_to_all x0 -> x3, waiting for transfers between devices: none -> 57.7 us  [the longest x1 20.9 us: shards(): mine = lax.all_to_all(mine, ('yl', 'x'), 0, 0, tiled=True)]
    ppermute x0 -> x7, waiting for transfers between devices: none -> 50.7 us  [the longest x6 47.4 us: ring(): held.append(lax.ppermute(held[-1], AXES, pairs))]
    all_to_all x1 -> x0, blocking collectives: 36.7 us -> none  [shards(): moved = lax.all_to_all(flat, 'col', split_axis=2, concat_axis=1, tiled=True)]
    ppermute x0 -> x7, starting transfers between devices: none -> 22.7 us  [the longest x6 16.5 us: ring(): held.append(lax.ppermute(held[-1], AXES, pairs))]
    gather x0 -> x3, local copies, waits for them, and re-layouts: none -> 20.6 us  [in_order(): return jnp.take(stacked, step * (position - jnp.arange(4)) % 4, axis=0)]
    transpose x0 -> x4, local copies, waits for them, and re-layouts: none -> 18.3 us  [the longest x1 8.8 us: shards(): amp.reshape(4, 2, 2, 2, 4, 32, 512).transpose(0, 2, 4, 1, 5, 3, 6)]
    all_to_all x0 -> x3, starting transfers between devices: none -> 14.8 us  [the longest x1 6.16 us: shards(): ints = lax.all_to_all(ints, ('x', 'core'), 0, 0, tiled=True)]
  transfers between devices with their start and end apart: 2 -> 10, of which waited for: 2 -> 8; matrix products, arithmetic and copies ran while one was open for 0% -> 14% of each run, Pallas kernels for 0% -> 0%
where the time goes in v1:
time: 262 us; the launch traced here: 261 us
  waiting for transfers between devices  108 us (41%)
  local copies, waits for them, and re-layouts  67.7 us (26%)
  starting transfers between devices  37.4 us (14%)
  other arithmetic  24.5 us (9%)
  matrix products  23 us (9%)
    ppermute x6, waiting for transfers between devices, ring(): held.append(lax.ppermute(held[-1], AXES, pairs))  47.4 us
    dot_general x1, matrix products, shards(): jnp.dot(lhs, rhs, precision=lax.Precision.HIGH, preferred_element_type=jn...  23 us
    all_to_all x1, waiting for transfers between devices, shards(): mine = lax.all_to_all(mine, ('yl', 'x'), 0, 0, tiled=True)  20.9 us
    gather x3, local copies, waits for them, and re-layouts, in_order(): return jnp.take(stacked, step * (position - jnp.arange(4)) % 4, axis=0)  20.6 us
    all_to_all x1, waiting for transfers between devices, shards(): amp = lax.all_to_all(amp, ('yh', 'yl'), 0, 0, tiled=True)  19.7 us
    all_to_all x1, waiting for transfers between devices, shards(): ints = lax.all_to_all(ints, ('x', 'core'), 0, 0, tiled=True)  17.1 us
    ppermute x6, starting transfers between devices, ring(): held.append(lax.ppermute(held[-1], AXES, pairs))  16.5 us
    another operation x2, other arithmetic, in_order(): stacked = jnp.stack(held)  10.6 us
  transfers between devices with their start and end apart: 10, of which 8 were waited for; matrix products, arithmetic and copies ran while one was open for 14% of the time, Pallas kernels for 0%

profile of v1, /device:TPU:1, one launch (start us, length us, event | category | flops | bytes accessed | tf_op | source)
XLA Modules:
  0.0 261.2 jit_solution(5128984307651132529)
XLA Ops:
  0.0 3.5 %reshape.164 = f32[4,32,2,4,2,2,128]{6,5,4,3,2,1,0:T(2,128)} reshape(f32[4,32,8,512]{3,2,1,0:T(8,128)} %param.7) | data formatting | bytes 4194304 | tf_op jit(solution)/shard_map/reshape | solution.py:46
  7.5 5.0 %all-to-all-start.1 = ((f32[4,2,128,512]{3,2,1,0:T(8,128)}), f32[4,2,128,512]{3,2,1,0:T(8,128)S(1)}, u32[]{:S(2)}, u32[]{:S(2)}) async-start(f32[4,2,128,512]{3,2,1,0:T(8,128)} %reshape.165), calls=%async_computation.1 | async-start | bytes 4194304 | tf_op jit(solution)/shard_map/all_to_all | solution.py:47
  12.5 3.0 %copy.29 = f32[384,1024]{0,1:T(8,128)} copy(f32[384,1024]{1,0:T(8,128)} %param.6) | data formatting | bytes 3145728 | tf_op args[0]
  15.6 2.7 %copy.30 = f32[4,2,384,2,2,32]{2,5,4,3,1,0:T(8,128)} copy(f32[4,2,384,2,2,32]{2,5,1,0,4,3:T(8,128)} %bitcast.68) | data formatting | bytes 3145728 | tf_op jit(solution)/shard_map/transpose | solution.py:48
  18.3 19.7 %all-to-all-done.1 = f32[4,2,128,512]{3,2,1,0:T(8,128)S(1)} async-done(((f32[4,2,128,512]{3,2,1,0:T(8,128)}), f32[4,2,128,512]{3,2,1,0:T(8,128)S(1)}, u32[]{:S(2)}, u32[]{:S(2)}) %all-to-all-start.1) | async-done | bytes 2097184 | tf_op jit(solution)/shard_map/all_to_all | solution.py:47
  38.0 6.2 %all-to-all-start = ((f32[8,384,128]{1,2,0:T(8,128)}), f32[8,384,128]{1,2,0:T(8,128)}, u32[]{:S(2)}, u32[]{:S(2)}) async-start(f32[8,384,128]{1,2,0:T(8,128)} %bitcast.67), calls=%async_computation | async-start | bytes 3145728 | tf_op jit(solution)/shard_map/all_to_all | solution.py:49
  44.1 3.8 %collective-permute-start.3 = (f32[4,2,128,512]{3,2,1,0:T(8,128)S(1)}, f32[4,2,128,512]{3,2,1,0:T(8,128)}, u32[]{:S(2)}, u32[]{:S(2)}) collective-permute-start(f32[4,2,128,512]{3,2,1,0:T(8,128)S(1)} %all-to-all-done.1), channel_id=1, source_target_pairs={{0,32},{1,97},{2,34},{3,99},{4,36},{5,101},{6,38},{7,103},{16,48},... | collective-permute-start | bytes 6291464 | tf_op jit(solution)/shard_map/ppermute | solution.py:32
  47.9 17.1 %all-to-all-done = f32[8,384,128]{1,2,0:T(8,128)} async-done(((f32[8,384,128]{1,2,0:T(8,128)}), f32[8,384,128]{1,2,0:T(8,128)}, u32[]{:S(2)}, u32[]{:S(2)}) %all-to-all-start) | async-done | bytes 1572896 | tf_op jit(solution)/shard_map/all_to_all | solution.py:49
  65.8 5.0 %collective-permute-done.3 = f32[4,2,128,512]{3,2,1,0:T(8,128)} collective-permute-done((f32[4,2,128,512]{3,2,1,0:T(8,128)S(1)}, f32[4,2,128,512]{3,2,1,0:T(8,128)}, u32[]{:S(2)}, u32[]{:S(2)}) %collective-permute-start.3) | collective-permute-done | bytes 2097184 | tf_op jit(solution)/shard_map/ppermute | solution.py:32
  70.9 3.4 %collective-permute-start.4 = (f32[4,2,128,512]{3,2,1,0:T(8,128)}, f32[4,2,128,512]{3,2,1,0:T(8,128)}, u32[]{:S(2)}, u32[]{:S(2)}) collective-permute-start(f32[4,2,128,512]{3,2,1,0:T(8,128)} %collective-permute-done.3), channel_id=1, source_target_pairs={{0,32},{1,97},{2,34},{3,99},{4,36},{5,101},{6,38},{7,103},{16,48},... | collective-permute-start | bytes 6291464 | tf_op jit(solution)/shard_map/ppermute | solution.py:32
  74.3 10.6 %collective-permute-done = f32[8,384,128]{1,2,0:T(8,128)S(1)} collective-permute-done((f32[8,384,128]{1,2,0:T(8,128)}, f32[8,384,128]{1,2,0:T(8,128)S(1)}, u32[]{:S(2)}, u32[]{:S(2)}) %collective-permute-start) | collective-permute-done | bytes 1572896 | tf_op jit(solution)/shard_map/ppermute | solution.py:32
  88.1 17.6 %collective-permute-done.1 = f32[8,384,128]{1,2,0:T(8,128)} collective-permute-done((f32[8,384,128]{1,2,0:T(8,128)S(1)}, f32[8,384,128]{1,2,0:T(8,128)}, u32[]{:S(2)}, u32[]{:S(2)}) %collective-permute-start.1) | collective-permute-done | bytes 1572896 | tf_op jit(solution)/shard_map/ppermute | solution.py:32
  105.7 3.0 %collective-permute-start.2 = (f32[8,384,128]{1,2,0:T(8,128)}, f32[8,384,128]{1,2,0:T(8,128)}, u32[]{:S(2)}, u32[]{:S(2)}) collective-permute-start(f32[8,384,128]{1,2,0:T(8,128)} %collective-permute-done.1), channel_id=1, source_target_pairs={{0,16},{1,25},{2,18},{3,27},{4,20},{5,29},{6,22},{7,31},{16,8},{17... | collective-permute-start | bytes 4718600 | tf_op jit(solution)/shard_map/ppermute | solution.py:32
  108.7 3.4 %collective-permute-start.5 = (f32[4,2,128,512]{3,2,1,0:T(8,128)}, f32[4,2,128,512]{3,2,1,0:T(8,128)}, u32[]{:S(2)}, u32[]{:S(2)}) collective-permute-start(f32[4,2,128,512]{3,2,1,0:T(8,128)} %collective-permute-done.4), channel_id=1, source_target_pairs={{0,32},{1,97},{2,34},{3,99},{4,36},{5,101},{6,38},{7,103},{16,48},... | collective-permute-start | bytes 6291464 | tf_op jit(solution)/shard_map/ppermute | solution.py:32
  112.1 14.2 %collective-permute-done.2 = f32[8,384,128]{1,2,0:T(8,128)} collective-permute-done((f32[8,384,128]{1,2,0:T(8,128)}, f32[8,384,128]{1,2,0:T(8,128)}, u32[]{:S(2)}, u32[]{:S(2)}) %collective-permute-start.2) | collective-permute-done | bytes 1572896 | tf_op jit(solution)/shard_map/ppermute | solution.py:32
  126.4 4.8 %pad_maximum_fusion.1 = f32[4,8,384,128]{2,3,1,0:T(8,128)} fusion(f32[1,8,384,128]{2,3,1,0:T(8,128)} %bitcast.6, f32[1,8,384,128]{2,3,1,0:T(8,128)} %bitcast.5, f32[1,8,384,128]{2,3,1,0:T(8,128)} %bitcast.69, f32[1,8,384,128]{2,3,1,0:T(8,128)} %bitcast.3), kind=kLoop, calls=%fused_computation.4 | loop fusion | flops 4718592 | bytes 12582912 | tf_op jit(solution)/shard_map/stack | solution.py:38
  131.2 6.4 %gather_fusion = f32[4,8,384,128]{2,3,1,0:T(8,128)} fusion(f32[4,8,384,128]{2,3,1,0:T(8,128)} %pad_maximum_fusion.1, s32[1024]{0:T(1024)S(1)} %pad_clamp_fusion.1), kind=kCustom, calls=%fused_computation | custom fusion | bytes 12582928 | tf_op jit(solution)/shard_map/jit(_take)/gather | solution.py:39
  137.5 6.6 %copy.31 = f32[4,8,384,128]{3,2,1,0:T(8,128)} copy(f32[4,8,384,128]{2,3,1,0:T(8,128)} %gather_fusion) | data formatting | bytes 12582912 | tf_op jit(solution)/shard_map/jit(_take)/gather | solution.py:39
  144.1 6.3 %select_bitcast_fusion.1 = f32[2,384,2,8,128]{4,1,3,0,2:T(8,128)} fusion(f32[2,2,8,384,128]{4,3,2,1,0:T(8,128)} %bitcast.62, pred[2,2]{1,0:T(4,128)(4,1)S(1)} %compare_and_fusion.1), kind=kLoop, calls=%fused_computation.5 | loop fusion | flops 1572864 | bytes 12582916 | tf_op jit(solution)/shard_map/transpose | solution.py:52
  150.4 6.6 %copy.32 = f32[2,384,2,8,128]{1,4,3,2,0:T(8,128)} copy(f32[2,384,2,8,128]{4,1,3,0,2:T(8,128)} %select_bitcast_fusion.1) | data formatting | bytes 12582912 | tf_op jit(solution)/shard_map/transpose | solution.py:52
  157.0 5.8 %pad_maximum_fusion = f32[4,4,2,128,512]{4,3,2,1,0:T(8,128)} fusion(f32[1,4,2,128,512]{4,3,2,1,0:T(8,128)} %bitcast.16, f32[1,4,2,128,512]{4,3,2,1,0:T(8,128)} %bitcast.15, f32[1,4,2,128,512]{4,3,2,1,0:T(8,128)} %bitcast.14, f32[1,4,2,128,512]{4,3,2,1,0:T(8,128)S(1)} %bitcast.65), kind=kLoop, calls=%fused_computation.2 | loop fusion | flops 6291456 | bytes 16777216 | tf_op jit(solution)/shard_map/stack | solution.py:38
  162.7 7.7 %gather_fusion.1 = f32[4,4,2,128,512]{4,3,2,1,0:T(8,128)} fusion(f32[4,4,2,128,512]{4,3,2,1,0:T(8,128)} %pad_maximum_fusion, s32[1024]{0:T(1024)S(1)} %pad_clamp_fusion), kind=kCustom, calls=%fused_computation.1 | custom fusion | bytes 16777232 | tf_op jit(solution)/shard_map/jit(_take)/gather | solution.py:39
  170.4 4.5 %select_bitcast_fusion = f32[4,2,4,2,32,2,512]{6,4,2,5,1,3,0:T(8,128)S(1)} fusion(f32[4,2,2,2,4,32,512]{6,5,4,3,2,1,0:T(8,128)} %bitcast.59, pred[4]{0:T(512)(128)(4,1)S(1)} %compare_and_fusion), kind=kLoop, calls=%fused_computation.3 | loop fusion | flops 2097152 | bytes 16777220 | tf_op jit(solution)/shard_map/transpose | solution.py:53
  175.0 8.8 %copy.34 = f32[4,2,4,2,32,2,512]{6,5,4,3,2,1,0:T(2,128)S(1)} copy(f32[4,2,4,2,32,2,512]{6,4,2,5,1,3,0:T(8,128)S(1)} %select_bitcast_fusion) | data formatting | bytes 16777216 | tf_op jit(solution)/shard_map/transpose | solution.py:53
  183.8 5.3 %copy.44 = f32[256,8,2,512]{3,1,2,0:T(8,128)} copy(f32[256,8,2,512]{3,2,1,0:T(2,128)S(1)} %bitcast.60) | data formatting | bytes 16777216
  189.1 9.2 %copy.43 = f32[1024,2048]{1,0:T(8,128)} copy(f32[1024,2048]{0,1:T(8,128)} %bitcast.61) | data formatting | bytes 16777216 | tf_op jit(solution)/shard_map/dot_general | solution.py:54
  198.3 23.0 %fusion.7 = f32[2,384,2,4,128]{4,1,3,2,0:T(8,128)S(1)} fusion(f32[2,384,2048,1,1]{1,2,4,3,0:T(8,128)} %bitcast.66, f32[2,4,128,2048,1]{3,2,1,0,4:T(8,128)} %bitcast.63), kind=kOutput, calls=%fused_computation.40 | convolution fusion | flops 9663676416 | bytes 17825792 | tf_op jit(solution)/shard_map/dot_general | solution.py:54
  222.6 6.1 %collective-permute-start.6 = (f32[2,384,4,128]{3,1,2,0:T(8,128)}, f32[2,384,4,128]{3,1,2,0:T(8,128)}, u32[]{:S(2)}, u32[]{:S(2)}) collective-permute-start(f32[2,384,4,128]{3,1,2,0:T(8,128)} %dynamic-slice_bitcast_fusion), channel_id=1, source_target_pairs={{0,1},{1,0},{2,3},{3,2},{4,5},{5,4},{6,7},{7,6},{16,17},{17,16},{1... | collective-permute-start | bytes 4718600 | tf_op jit(solution)/shard_map/ppermute | solution.py:58
  228.8 3.4 %collective-permute-done.6 = f32[2,384,4,128]{3,1,2,0:T(8,128)} collective-permute-done((f32[2,384,4,128]{3,1,2,0:T(8,128)}, f32[2,384,4,128]{3,1,2,0:T(8,128)}, u32[]{:S(2)}, u32[]{:S(2)}) %collective-permute-start.6) | collective-permute-done | bytes 1572896 | tf_op jit(solution)/shard_map/ppermute | solution.py:58
  232.1 2.7 %bitcast_add_fusion = f32[2,384,4,128]{3,1,2,0:T(8,128)} fusion(f32[2,384,4,128]{3,1,2,0:T(8,128)} %collective-permute-done.6, f32[2,384,2,4,128]{4,1,3,2,0:T(8,128)S(1)} %fusion.7, s32[]{:T(128)S(6)} %select_n.99), kind=kLoop, calls=%fused_computation.8 | loop fusion | flops 393216 | bytes 4718596 | tf_op jit(solution)/shard_map/add | solution.py:58
  234.8 3.6 %all-to-all-start.2 = ((f32[8,384,128]{2,1,0:T(8,128)}), f32[8,384,128]{2,1,0:T(8,128)S(1)}, u32[]{:S(2)}, u32[]{:S(2)}) async-start(f32[8,384,128]{2,1,0:T(8,128)} %bitcast.26), calls=%async_computation.2 | async-start | bytes 3145728 | tf_op jit(solution)/shard_map/all_to_all | solution.py:60
  239.0 20.9 %all-to-all-done.2 = f32[8,384,128]{2,1,0:T(8,128)S(1)} async-done(((f32[8,384,128]{2,1,0:T(8,128)}), f32[8,384,128]{2,1,0:T(8,128)S(1)}, u32[]{:S(2)}, u32[]{:S(2)}) %all-to-all-start.2) | async-done | bytes 1572896 | tf_op jit(solution)/shard_map/all_to_all | solution.py:60
  (34 shorter events, 11.3 us)
Async XLA Ops:
  7.5 30.4 %all-to-all-start.1 = ((f32[4,2,128,512]{3,2,1,0:T(8,128)}), f32[4,2,128,512]{3,2,1,0:T(8,128)S(1)}, u32[]{:S(2)}, u32[]{:S(2)}) async-start(f32[4,2,128,512]{3,2,1,0:T(8,128)} %reshape.165), calls=%async_computation.1 | async-start | bytes 4194304 | tf_op jit(solution)/shard_map/all_to_all | solution.py:47
  38.0 27.0 %all-to-all-start = ((f32[8,384,128]{1,2,0:T(8,128)}), f32[8,384,128]{1,2,0:T(8,128)}, u32[]{:S(2)}, u32[]{:S(2)}) async-start(f32[8,384,128]{1,2,0:T(8,128)} %bitcast.67), calls=%async_computation | async-start | bytes 3145728 | tf_op jit(solution)/shard_map/all_to_all | solution.py:49
  44.1 26.7 %collective-permute-start.3 = (f32[4,2,128,512]{3,2,1,0:T(8,128)S(1)}, f32[4,2,128,512]{3,2,1,0:T(8,128)}, u32[]{:S(2)}, u32[]{:S(2)}) collective-permute-start(f32[4,2,128,512]{3,2,1,0:T(8,128)S(1)} %all-to-all-done.1), channel_id=1, source_target_pairs={{0,32},{1,97},{2,34},{3,99},{4,36},{5,101},{6,38},{7,103},{16,48},... | collective-permute-start | bytes 6291464 | tf_op jit(solution)/shard_map/ppermute | solution.py:32
  65.0 19.9 %collective-permute-start = (f32[8,384,128]{1,2,0:T(8,128)}, f32[8,384,128]{1,2,0:T(8,128)S(1)}, u32[]{:S(2)}, u32[]{:S(2)}) collective-permute-start(f32[8,384,128]{1,2,0:T(8,128)} %all-to-all-done), channel_id=1, source_target_pairs={{0,16},{1,25},{2,18},{3,27},{4,20},{5,29},{6,22},{7,31},{16,8},{17... | collective-permute-start | bytes 4718600 | tf_op jit(solution)/shard_map/ppermute | solution.py:32
  70.9 37.8 %collective-permute-start.4 = (f32[4,2,128,512]{3,2,1,0:T(8,128)}, f32[4,2,128,512]{3,2,1,0:T(8,128)}, u32[]{:S(2)}, u32[]{:S(2)}) collective-permute-start(f32[4,2,128,512]{3,2,1,0:T(8,128)} %collective-permute-done.3), channel_id=1, source_target_pairs={{0,32},{1,97},{2,34},{3,99},{4,36},{5,101},{6,38},{7,103},{16,48},... | collective-permute-start | bytes 6291464 | tf_op jit(solution)/shard_map/ppermute | solution.py:32
  84.8 1.2 copy-start
  86.0 19.7 %collective-permute-start.1 = (f32[8,384,128]{1,2,0:T(8,128)S(1)}, f32[8,384,128]{1,2,0:T(8,128)}, u32[]{:S(2)}, u32[]{:S(2)}) collective-permute-start(f32[8,384,128]{1,2,0:T(8,128)S(1)} %collective-permute-done), channel_id=1, source_target_pairs={{0,16},{1,25},{2,18},{3,27},{4,20},{5,29},{6,22},{7,31},{16,8},{17... | collective-permute-start | bytes 4718600 | tf_op jit(solution)/shard_map/ppermute | solution.py:32
  105.7 20.7 %collective-permute-start.2 = (f32[8,384,128]{1,2,0:T(8,128)}, f32[8,384,128]{1,2,0:T(8,128)}, u32[]{:S(2)}, u32[]{:S(2)}) collective-permute-start(f32[8,384,128]{1,2,0:T(8,128)} %collective-permute-done.1), channel_id=1, source_target_pairs={{0,16},{1,25},{2,18},{3,27},{4,20},{5,29},{6,22},{7,31},{16,8},{17... | collective-permute-start | bytes 4718600 | tf_op jit(solution)/shard_map/ppermute | solution.py:32
  108.7 48.3 %collective-permute-start.5 = (f32[4,2,128,512]{3,2,1,0:T(8,128)}, f32[4,2,128,512]{3,2,1,0:T(8,128)}, u32[]{:S(2)}, u32[]{:S(2)}) collective-permute-start(f32[4,2,128,512]{3,2,1,0:T(8,128)} %collective-permute-done.4), channel_id=1, source_target_pairs={{0,32},{1,97},{2,34},{3,99},{4,36},{5,101},{6,38},{7,103},{16,48},... | collective-permute-start | bytes 6291464 | tf_op jit(solution)/shard_map/ppermute | solution.py:32
  221.3 17.1 %copy-start.2 = (f32[512]{0:T(512)S(1)}, f32[512]{0:T(512)}, u32[]{:S(2)}) copy-start(f32[512]{0:T(512)} %param.11) | copy-start | bytes 6148
  221.3 17.1 %copy-start.3 = (f32[8]{0:T(128)S(1)}, f32[8]{0:T(128)}, u32[]{:S(2)}) copy-start(f32[8]{0:T(128)} %param.10) | copy-start | bytes 100
  221.3 17.2 %copy-start.4 = (f32[6]{0:T(128)S(1)}, f32[6]{0:T(128)}, u32[]{:S(2)}) copy-start(f32[6]{0:T(128)} %param.9) | copy-start | bytes 76
  221.4 17.3 %copy-start.1 = (f32[384,256]{1,0:T(8,128)S(1)}, f32[384,256]{1,0:T(8,128)}, u32[]{:S(2)}) copy-start(f32[384,256]{1,0:T(8,128)} %param.8) | copy-start | bytes 1179652
  222.6 9.5 %collective-permute-start.6 = (f32[2,384,4,128]{3,1,2,0:T(8,128)}, f32[2,384,4,128]{3,1,2,0:T(8,128)}, u32[]{:S(2)}, u32[]{:S(2)}) collective-permute-start(f32[2,384,4,128]{3,1,2,0:T(8,128)} %dynamic-slice_bitcast_fusion), channel_id=1, source_target_pairs={{0,1},{1,0},{2,3},{3,2},{4,5},{5,4},{6,7},{7,6},{16,17},{17,16},{1... | collective-permute-start | bytes 4718600 | tf_op jit(solution)/shard_map/ppermute | solution.py:58
  234.8 25.0 %all-to-all-start.2 = ((f32[8,384,128]{2,1,0:T(8,128)}), f32[8,384,128]{2,1,0:T(8,128)S(1)}, u32[]{:S(2)}, u32[]{:S(2)}) async-start(f32[8,384,128]{2,1,0:T(8,128)} %bitcast.26), calls=%async_computation.2 | async-start | bytes 3145728 | tf_op jit(solution)/shard_map/all_to_all | solution.py:60

commit v2 on v1

v2 whole, which is shorter than its diff:
```python
import functools

import jax
import jax.numpy as jnp
from jax import lax
from jax.experimental import pallas as pl
from jax.experimental.pallas import tpu as pltpu
from jax.sharding import Mesh, PartitionSpec as P

AXES = ("z", "yl", "yh", "x", "core")
SIZES = (4, 2, 2, 4, 2)
F32, BF16 = jnp.float32, jnp.bfloat16


def device_index(z, y, x, core):
    return (((z * 2 + y % 2) * 2 + y // 2) * 4 + x) * 2 + core


def moves(target):
    pairs = []
    for z in range(4):
        for y in range(4):
            for x in range(4):
                for core in range(2):
                    pairs.append((device_index(z, y, x, core), device_index(*target(z, y, x, core))))
    return pairs


Z_ON = [moves(lambda z, y, x, core, d=d: ((z + d * (1 - 2 * core)) % 4, y, x, core)) for d in range(4)]
Y_ON = [moves(lambda z, y, x, core, d=d: (z, (y + d * (1 - 2 * core)) % 4, x, core)) for d in range(4)]
SWAP = moves(lambda z, y, x, core: (z, y, x, 1 - core))


def call(body, grid, in_specs, out_specs, out_shape, scalars, operands, scratch=(), aliases=None, flops=0, vmem=8 << 20):
    nbytes = sum(4 * o.size for o in operands[:1])
    return pl.pallas_call(
        body,
        grid_spec=pltpu.PrefetchScalarGridSpec(
            num_scalar_prefetch=1, grid=grid, in_specs=in_specs, out_specs=out_specs, scratch_shapes=list(scratch)
        ),
        out_shape=out_shape,
        input_output_aliases=aliases or {},
        cost_estimate=pl.CostEstimate(flops=flops, bytes_accessed=2 * nbytes, transcendentals=0),
        compiler_params=pltpu.CompilerParams(vmem_limit_bytes=vmem),
    )(scalars, *operands)


def split_amplitudes(amplitudes, targets):
    def body(target, src, *refs):
        outs, turned = refs[:4], refs[4]
        turned[...] = jnp.swapaxes(src[0], 0, 1)
        for out, slot in zip(outs, range(4)):
            y = target[slot]
            yh, yl = y // 2, y % 2
            for half in range(2):
                lanes = pl.ds(pl.multiple_of(half * 256 + yl * 128, 128), 128)
                for x in range(4):
                    out[half, :, x * 128 : (x + 1) * 128] = turned[yh * 4 + x, :, lanes]

    return call(
        body,
        (4,),
        [pl.BlockSpec((1, 32, 8, 512), lambda k, t: (k, 0, 0, 0))],
        [pl.BlockSpec((2, 32, 512), lambda k, t: (0, k, 0))] * 4,
        [jax.ShapeDtypeStruct((2, 128, 512), F32)] * 4,
        targets,
        (amplitudes,),
        scratch=[pltpu.VMEM((8, 32, 512), F32)],
    )


def split_integrals(integrals):
    rows = integrals.shape[0]
    step = rows // 3

    def body(unused, src, out):
        lane = lax.broadcasted_iota(jnp.int32, (step, 128), 1) // 32
        for h in range(2):
            tiles = [src[:, (e * 4 + yh * 2 + h) * 128 :][:, :128] for yh in range(2) for e in range(2)]
            for j in range(4):
                made = None
                for s in range(4):
                    turn = (s - j) % 4 * 32
                    moved = pltpu.roll(tiles[s], turn, 1) if turn else tiles[s]
                    made = moved if made is None else jnp.where(lane == s, moved, made)
                out[h * 4 + j] = made

    return call(
        body,
        (3,),
        [pl.BlockSpec((step, 1024), lambda r, t: (r, 0))],
        pl.BlockSpec((8, step, 128), lambda r, t: (0, r, 0)),
        jax.ShapeDtypeStruct((8, rows, 128), F32),
        jnp.zeros((1,), jnp.int32),
        (integrals,),
    )


def two_parts(value):
    high = value.astype(BF16)
    return high, (value - high.astype(F32)).astype(BF16)


def laid_out(src, rows):
    first = lax.broadcasted_iota(jnp.int32, (rows, 128), 1) < 64
    for z0 in range(src.shape[0] // 4):
        for yb in range(2):
            one, two = src[z0 * 4 + yb * 2], src[z0 * 4 + yb * 2 + 1]
            yield (z0 * 2 + 0) * 2 + yb, jnp.where(first, one, pltpu.roll(two, 64, 1))
            yield (z0 * 2 + 1) * 2 + yb, jnp.where(first, pltpu.roll(one, 64, 1), two)


def product(ah, al, bh, bl):
    dot = functools.partial(jnp.dot, preferred_element_type=F32)
    return dot(ah, bh) + (dot(ah, bl) + dot(al, bh))


ANY = pl.BlockSpec(memory_space=pl.ANY)
VMEM_FIRST, VMEM_LAST = 56 << 20, 20 << 20
SMALL = pl.BlockSpec(memory_space=pltpu.SMEM)


def first_products(place, ints, own, near):
    rows = ints[0].shape[1]

    def body(at, *refs):
        src_a, src_own, src_near = refs[:3], refs[3:7], refs[7:10]
        out_a, out_b, sums = refs[10:12], refs[12:14], refs[14:16]
        raw_a, raw_own, raw_near, a, b, total, sem, done = refs[16:]
        core, z, y = at[0], at[1], at[2]
        way = 1 - 2 * core
        yl, yh = y & 1, y // 2
        zh, z0 = ((z + 2) & 3) // 2, z & 1
        halves = (1 - core, core)
        loads_a = [pltpu.make_async_copy(src_a[n], raw_a.at[n], sem.at[n]) for n in range(3)]
        loads_b = []
        for n, half in enumerate(halves):
            loads_b.append(
                [pltpu.make_async_copy(src_own[s].at[half], raw_own.at[n, s], sem.at[3 + n * 7 + s]) for s in range(4)]
                + [pltpu.make_async_copy(src_near[s].at[half], raw_near.at[n, s], sem.at[7 + n * 7 + s]) for s in range(3)]
            )
        for copy in loads_a + loads_b[0] + loads_b[1]:
            copy.start()
        stores = []

        def store(source, target):
            stores.append(pltpu.make_async_copy(source, target, done.at[len(stores)]))
            stores[-1].start()

        steps = (0, 1, 3)
        for n, step in enumerate(steps):
            loads_a[n].wait()
            slot = (y - step * way) & 3
            for tile, value in laid_out(raw_a.at[n], rows):
                lanes = slice(tile % 4 * 128, tile % 4 * 128 + 128)
                a[slot, tile // 4, 0, :, lanes], a[slot, tile // 4, 1, :, lanes] = two_parts(value)
        store(a.at[y, z0], out_a[0])
        store(a.at[zh * 2 + 1 - yl, z0], out_a[1])
        for n, half in enumerate(halves):
            for copy in loads_b[n]:
                copy.wait()
            for s in range(4):
                slot = (z - s * way) & 3
                b[n, slot, 0, y], b[n, slot, 1, y] = two_parts(raw_own[n, s])
            for m, back in enumerate((1, 3, 2)):
                part = (y - back * way) & 3
                for k, step in enumerate(steps):
                    slot = (z - step * way) & 3
                    b[n, slot, 0, part], b[n, slot, 1, part] = two_parts(raw_near[n, k, m])
                empty = jnp.zeros((128, 512), BF16)
                b[n, (z + 2) & 3, 0, part], b[n, (z + 2) & 3, 1, part] = empty, empty
            store(b.at[n, pl.ds((1 - yh) * 2, 2)], out_b[n])
            for group, chosen in ((yl, (0,)), (1 - yl, (1, 3))):
                value = None
                for step in chosen:
                    slot = (y - step * way) & 3
                    for k in range(2):
                        bh, bl = (b[n, slot // 2 * 2 + k, p].reshape(512, 512) for p in range(2))
                        part = product(a[slot, k, 0], a[slot, k, 1], bh, bl)
                        value = part if value is None else value + part
                total[n, group] = value
            store(total.at[n], sums[n])
        for copy in stores:
            copy.wait()

    return pl.pallas_call(
        body,
        in_specs=[SMALL] + [ANY] * 10,
        out_specs=[ANY] * 6,
        out_shape=[jax.ShapeDtypeStruct((2, rows, 512), BF16)] * 2
        + [jax.ShapeDtypeStruct((2, 2, 4, 128, 512), BF16)] * 2
        + [jax.ShapeDtypeStruct((2, rows, 512), F32)] * 2,
        scratch_shapes=[
            pltpu.VMEM((3, 8, rows, 128), F32),
            pltpu.VMEM((2, 4, 128, 512), F32),
            pltpu.VMEM((2, 3, 3, 128, 512), F32),
            pltpu.VMEM((4, 2, 2, rows, 512), BF16),
            pltpu.VMEM((2, 4, 2, 4, 128, 512), BF16),
            pltpu.VMEM((2, 2, rows, 512), F32),
            pltpu.SemaphoreType.DMA((17,)),
            pltpu.SemaphoreType.DMA((6,)),
        ],
        cost_estimate=pl.CostEstimate(flops=18 * rows * 2048 * 512, bytes_accessed=24 << 20, transcendentals=0),
        compiler_params=pltpu.CompilerParams(vmem_limit_bytes=VMEM_FIRST),
    )(place, *ints, *own, *near)


def last_products(place, sums, ints, near, own_a, other_a, far_b):
    rows = sums.shape[1]

    def body(at, src_sum, src_far, src_near, src_own, src_other, src_b, out, *refs):
        total, raw, raw_near, own, other, far, b, late, sem = refs
        half, z, y, core = at[0], at[1], at[2], at[3]
        way = 1 - 2 * core
        yl, yh = y & 1, y // 2
        zh, z0 = ((z + 2) & 3) // 2, z & 1
        pairs = (src_near.at[half], raw_near), (src_far, raw), (src_other, other), (src_sum, total), (src_own, own), (src_b, b)
        copies = [pltpu.make_async_copy(*pair, sem.at[n]) for n, pair in enumerate(pairs)]
        for copy in copies:
            copy.start()
        copies[0].wait()
        empty = jnp.zeros((128, 512), BF16)
        late[0, y], late[1, y] = empty, empty
        for m, back in enumerate((1, 3, 2)):
            slot = (y - back * way) & 3
            late[0, slot], late[1, slot] = two_parts(raw_near[m])
        bh, bl = late[0].reshape(512, 512), late[1].reshape(512, 512)
        copies[1].wait()
        for tile, value in laid_out(raw, rows):
            lanes = slice(tile % 4 * 128, tile % 4 * 128 + 128)
            far[tile // 4, 0, :, lanes], far[tile // 4, 1, :, lanes] = two_parts(value)
        for copy in copies[2:5]:
            copy.wait()
        value = total[1 - yl] + product(other[0], other[1], bh, bl)
        for x in range(4):
            out[(1 - yl) * 4 + x] = value[:, x * 128 : x * 128 + 128]

        @pl.when(yh != zh)
        def _():
            own[...] = far[z0]

        value = total[yl] + product(own[0], own[1], bh, bl)
        copies[5].wait()
        for k in range(2):
            value = value + product(far[k, 0], far[k, 1], *(b[k, p].reshape(512, 512) for p in range(2)))
        for x in range(4):
            out[yl * 4 + x] = value[:, x * 128 : x * 128 + 128]

    return pl.pallas_call(
        body,
        in_specs=[SMALL] + [ANY] * 6,
        out_specs=pl.BlockSpec(memory_space=pltpu.VMEM),
        out_shape=jax.ShapeDtypeStruct((8, rows, 128), F32),
        scratch_shapes=[
            pltpu.VMEM((2, rows, 512), F32),
            pltpu.VMEM((8, rows, 128), F32),
            pltpu.VMEM((3, 128, 512), F32),
            pltpu.VMEM((2, rows, 512), BF16),
            pltpu.VMEM((2, rows, 512), BF16),
            pltpu.VMEM((2, 2, rows, 512), BF16),
            pltpu.VMEM((2, 2, 4, 128, 512), BF16),
            pltpu.VMEM((2, 4, 128, 512), BF16),
            pltpu.SemaphoreType.DMA((6,)),
        ],
        cost_estimate=pl.CostEstimate(flops=6 * rows * 2048 * 512, bytes_accessed=8 << 20, transcendentals=0),
        compiler_params=pltpu.CompilerParams(vmem_limit_bytes=VMEM_LAST),
    )(place, sums, ints, near, own_a, other_a, far_b)


def total_of(one, two):
    def body(a, b, out):
        out[...] = a[...] + b[...]

    whole = pl.BlockSpec(memory_space=pltpu.VMEM)
    return pl.pallas_call(
        body,
        in_specs=[whole] * 2,
        out_specs=whole,
        out_shape=jax.ShapeDtypeStruct(one.shape, F32),
        compiler_params=pltpu.CompilerParams(vmem_limit_bytes=4 << 20),
    )(one, two)


def finish(parts, driver, row_part, col_part):
    rows = driver.shape[0]
    step = rows // 3

    def body(unused, part, given, row, col, out):
        for yl in range(2):
            lanes = slice(yl * 128, (yl + 1) * 128)
            cycle = (part[yl * 4] + part[yl * 4 + 1]) + (part[yl * 4 + 2] + part[yl * 4 + 3])
            out[:, lanes] = (given[:, lanes] + cycle) / (row[...] + col[:, lanes])

    return call(
        body,
        (3,),
        [
            pl.BlockSpec((8, step, 128), lambda r, t: (0, r, 0)),
            pl.BlockSpec((step, 256), lambda r, t: (r, 0)),
            pl.BlockSpec((step, 1), lambda r, t: (r, 0)),
            pl.BlockSpec((1, 256), lambda r, t: (0, 0)),
        ],
        pl.BlockSpec((step, 256), lambda r, t: (r, 0)),
        jax.ShapeDtypeStruct((rows, 256), F32),
        jnp.zeros((1,), jnp.int32),
        (parts, driver, row_part, col_part),
    )


def shards(integrals, amplitudes, driver, occ_rows, occ_cols, virtual):
    z, yl, yh, x, core = (lax.axis_index(axis) for axis in AXES)
    y = yh * 2 + yl
    way = 1 - 2 * core
    rows = driver.shape[0]
    number = lambda *v: jnp.stack([jnp.asarray(i, jnp.int32) for i in v])

    ints = split_integrals(integrals)
    amplitudes, ints = lax.optimization_barrier((amplitudes, ints))
    parts = split_amplitudes(amplitudes, number(*((y + d * way) % 4 for d in range(4))))
    on_z = lambda v, d: lax.ppermute(v, AXES, Z_ON[d])
    on_y = lambda v, d: lax.ppermute(v, AXES, Y_ON[d])
    wave = lambda *v: list(lax.optimization_barrier(v))
    ints = lax.all_to_all(ints, ("x", "core"), 0, 0, tiled=True)
    b, c, d = on_y(parts[1], 1), on_y(parts[3], 3), on_y(parts[2], 2)
    own = [parts[0]] + [on_z(parts[0], step) for step in (1, 2, 3)]
    ints, b, c, d, *own[1:] = wave(ints, b, c, d, *own[1:])
    bcd = jnp.stack([b, c, d], axis=1)
    bcd1, bcd3, ints1, ints3 = wave(on_z(bcd, 1), on_z(bcd, 3), on_y(ints, 1), on_y(ints, 3))
    bcd2, ints2 = on_z(bcd1, 1), on_y(ints1, 1)
    own_a, other_a, far_other, far_mine, sum_other, sum_mine = first_products(
        number(core, z, y), (ints, ints1, ints3), own, (bcd, bcd1, bcd3)
    )
    bcd2, ints2 = wave(bcd2, ints2)
    other = last_products(number(1 - core, z, y, core), sum_other, ints2, bcd2, own_a, other_a, far_other)
    mine = last_products(number(core, z, y, core), sum_mine, ints2, bcd2, own_a, other_a, far_mine)
    mine = total_of(mine, lax.ppermute(other, AXES, SWAP))
    mine = lax.all_to_all(mine, ("yl", "x"), 0, 0, tiled=True)
    row_energy = (occ_rows[:, None] - virtual[None, :]).reshape(-1)
    col_energy = (occ_cols[:, None] - virtual[None, :]).reshape(-1)
    row_part = lax.dynamic_slice_in_dim(row_energy, (z * 2 + yl) * rows, rows, 0)
    col_part = lax.dynamic_slice_in_dim(col_energy, ((yh * 4 + x) * 2 + core) * 256, 256, 0)
    return finish(mine, driver, row_part[:, None], col_part[None, :])


def solution(mesh):
    fine = Mesh(mesh.devices.reshape(SIZES), AXES)
    row, col = ("z", "yl"), ("yh", "x", "core")
    in_specs = (P(row, col), P(row, col, None, None), P(row, col), P(), P(), P())
    return jax.shard_map(shards, mesh=fine, in_specs=in_specs, out_specs=P(row, col), check_vma=False)
```

time: 262 us -> 152 us (0.58)
  local copies, waits for them, and re-layouts: 67.7 us -> 8.58 us
  Pallas kernels: 0 us -> 30.6 us
  waiting for transfers between devices: 108 us -> 79.2 us
  other arithmetic: 24.5 us -> 1.19 us
  matrix products: 23 us -> 0 us
  starting transfers between devices: 37.4 us -> 32.2 us
    pallas_call x0 -> x7, Pallas kernels: none -> 30.6 us  [the longest x1 14.2 us: first_products(): pl.pallas_call(body, in_specs=[SMALL] + [ANY] * 10, out_specs=[ANY] * 6,...]
    dot_general x1 -> x0, matrix products: 23 us -> none  [shards(): jnp.dot(lhs, rhs, precision=lax.Precision.HIGH, preferred_element_type=jn...]
    gather x3 -> x0, local copies, waits for them, and re-layouts: 20.6 us -> none  [in_order(): return jnp.take(stacked, step * (position - jnp.arange(4)) % 4, axis=0)]
    all_to_all x1 -> x0, waiting for transfers between devices: 19.7 us -> none  [shards(): amp = lax.all_to_all(amp, ('yh', 'yl'), 0, 0, tiled=True)]
    transpose x4 -> x0, local copies, waits for them, and re-layouts: 18.3 us -> none  [the longest x1 8.8 us: shards(): amp.reshape(4, 2, 2, 2, 4, 32, 512).transpose(0, 2, 4, 1, 5, 3, 6)]
    all_to_all x1, waiting for transfers between devices: 17.1 us -> 0.01 us  [shards(): ints = lax.all_to_all(ints, ('x', 'core'), 0, 0, tiled=True)]
    transpose x2 -> x0, other arithmetic: 10.8 us -> none  [the longest x1 6.29 us: shards(): ints.reshape(2, 2, 8, rows, 128).transpose(1, 3, 0, 2, 4)]
    another operation x2 -> x5, other arithmetic: 10.6 us -> 1.04 us  [the longest x4 0.85 us: shards(): number = lambda *v: jnp.stack([jnp.asarray(i, jnp.int32) for i in v])]
  transfers between devices with their start and end apart: 10 -> 15, of which waited for: 8 -> 9; matrix products, arithmetic and copies ran while one was open for 14% -> 1% of each run, Pallas kernels for 0% -> 13%
where the time goes in v2:
time: 152 us
  waiting for transfers between devices  79.2 us (52%)
  starting transfers between devices  32.2 us (21%)
  Pallas kernels  30.6 us (20%)
  local copies, waits for them, and re-layouts  8.58 us (6%)
    ppermute x6, waiting for transfers between devices, shards(): on_z = lambda v, d: lax.ppermute(v, AXES, Z_ON[d])  34.5 us
    ppermute x6, waiting for transfers between devices, shards(): on_y = lambda v, d: lax.ppermute(v, AXES, Y_ON[d])  23.6 us
    all_to_all x1, waiting for transfers between devices, shards(): mine = lax.all_to_all(mine, ('yl', 'x'), 0, 0, tiled=True)  21.1 us
    pallas_call x1, Pallas kernels, first_products(): pl.pallas_call(body, in_specs=[SMALL] + [ANY] * 10, out_specs=[ANY] * 6,...  14.2 us
    ppermute x6, starting transfers between devices, shards(): on_y = lambda v, d: lax.ppermute(v, AXES, Y_ON[d])  11.8 us
    ppermute x6, starting transfers between devices, shards(): on_z = lambda v, d: lax.ppermute(v, AXES, Z_ON[d])  9.54 us
    pallas_call x2, Pallas kernels, last_products(): pl.pallas_call(body, in_specs=[SMALL] + [ANY] * 6, out_specs=pl.BlockSpec...  9.4 us
    unnamed x37, local copies, waits for them, and re-layouts  8.32 us
  transfers between devices with their start and end apart: 15, of which 9 were waited for; matrix products, arithmetic and copies ran while one was open for 1% of the time, Pallas kernels for 13%

profile of v2, /device:TPU:1, one launch (start us, length us, event | category | flops | bytes accessed | tf_op | source)
XLA Modules:
  0.0 151.9 jit_solution(11347231712820257666)
XLA Ops:
  0.0 1.4 copy-done.7
  1.4 2.6 %shard_map.64 = f32[8,384,128]{2,1,0:T(8,128)} custom-call(s32[1]{0:T(128)} %constant.46.clone.1.unused, f32[384,1024]{1,0:T(8,128)S(1)} %copy-done.7), custom_call_target="tpu_custom_call" | custom-call | bytes 3145728 | tf_op jit(solution)/shard_map/pallas_call | solution.py:36
  4.0 5.9 %all-to-all-start = ((f32[8,384,128]{2,1,0:T(8,128)}), f32[8,384,128]{2,1,0:T(8,128)}, u32[]{:S(2)}, u32[]{:S(2)}) async-start(f32[8,384,128]{2,1,0:T(8,128)} %shard_map.64), calls=%async_computation | async-start | bytes 3145728 | tf_op jit(solution)/shard_map/all_to_all | solution.py:323
  10.0 1.4 shard_map.65
  11.4 2.8 %collective-permute-start = (f32[2,128,512]{2,1,0:T(8,128)S(1)}, f32[2,128,512]{2,1,0:T(8,128)S(1)}, u32[]{:S(2)}, u32[]{:S(2)}) collective-permute-start(f32[2,128,512]{2,1,0:T(8,128)S(1)} %get-tuple-element.32), channel_id=1, source_target_pairs={{0,16},{1,25},{2,18},{3,27},{4,20},{5,29},{6,22},{7,31},{16,8},{17... | collective-permute-start | bytes 1572872 | tf_op jit(solution)/shard_map/ppermute | solution.py:321
  14.3 1.6 %collective-permute-start.2 = (f32[2,128,512]{2,1,0:T(8,128)S(1)}, f32[2,128,512]{2,1,0:T(8,128)S(1)}, u32[]{:S(2)}, u32[]{:S(2)}) collective-permute-start(f32[2,128,512]{2,1,0:T(8,128)S(1)} %get-tuple-element.34), channel_id=1, source_target_pairs={{0,8},{1,9},{2,10},{3,11},{4,12},{5,13},{6,14},{7,15},{16,24},{17,... | collective-permute-start | bytes 1572872 | tf_op jit(solution)/shard_map/ppermute | solution.py:321
  15.9 3.8 %collective-permute-start.3 = (f32[2,128,512]{2,1,0:T(8,128)S(1)}, f32[2,128,512]{2,1,0:T(8,128)S(1)}, u32[]{:S(2)}, u32[]{:S(2)}) collective-permute-start(f32[2,128,512]{2,1,0:T(8,128)S(1)} %get-tuple-element.35.refs_3_), channel_id=1, source_target_pairs={{0,32},{1,97},{2,34},{3,99},{4,36},{5,101},{6,38},{7,103},{16,48},... | collective-permute-start | bytes 1572872 | tf_op jit(solution)/shard_map/ppermute | solution.py:320
  19.7 16.8 %collective-permute-done = f32[2,128,512]{2,1,0:T(8,128)S(1)} collective-permute-done((f32[2,128,512]{2,1,0:T(8,128)S(1)}, f32[2,128,512]{2,1,0:T(8,128)S(1)}, u32[]{:S(2)}, u32[]{:S(2)}) %collective-permute-start) | collective-permute-done | bytes 524320 | tf_op jit(solution)/shard_map/ppermute | solution.py:321
  36.5 1.6 %collective-permute-start.5 = (f32[2,128,512]{2,1,0:T(8,128)S(1)}, f32[2,128,512]{2,1,0:T(8,128)}, u32[]{:S(2)}, u32[]{:S(2)}) collective-permute-start(f32[2,128,512]{2,1,0:T(8,128)S(1)} %get-tuple-element.35.refs_3_), channel_id=1, source_target_pairs={{0,96},{1,33},{2,98},{3,35},{4,100},{5,37},{6,102},{7,39},{16,112}... | collective-permute-start | bytes 1572872 | tf_op jit(solution)/shard_map/ppermute | solution.py:320
  38.0 1.5 collective-permute-done.2
  39.5 0.8 copy-done.16
  40.4 0.8 copy-done.17
  41.1 5.7 %collective-permute-done.5.refs_6_ = f32[2,128,512]{2,1,0:T(8,128)} collective-permute-done((f32[2,128,512]{2,1,0:T(8,128)S(1)}, f32[2,128,512]{2,1,0:T(8,128)}, u32[]{:S(2)}, u32[]{:S(2)}) %collective-permute-start.5) | collective-permute-done | bytes 524320 | tf_op jit(solution)/shard_map/ppermute | solution.py:320
  47.0 1.5 %collective-permute-start.6 = (f32[2,3,128,512]{3,2,1,0:T(8,128)S(1)}, f32[2,3,128,512]{3,2,1,0:T(8,128)}, u32[]{:S(2)}, u32[]{:S(2)}) collective-permute-start(f32[2,3,128,512]{3,2,1,0:T(8,128)S(1)} %pad_maximum_fusion.refs_7_), channel_id=1, source_target_pairs={{0,32},{1,97},{2,34},{3,99},{4,36},{5,101},{6,38},{7,103},{16,48},... | collective-permute-start | bytes 4718600 | tf_op jit(solution)/shard_map/ppermute | solution.py:320
  48.6 5.2 %collective-permute-start.8 = (f32[8,384,128]{2,1,0:T(8,128)}, f32[8,384,128]{2,1,0:T(8,128)}, u32[]{:S(2)}, u32[]{:S(2)}) collective-permute-start(f32[8,384,128]{2,1,0:T(8,128)} %all-to-all-done.refs_0_), channel_id=1, source_target_pairs={{0,16},{1,25},{2,18},{3,27},{4,20},{5,29},{6,22},{7,31},{16,8},{17... | collective-permute-start | bytes 4718600 | tf_op jit(solution)/shard_map/ppermute | solution.py:321
  53.8 28.2 %collective-permute-done.6.refs_8_ = f32[2,3,128,512]{3,2,1,0:T(8,128)} collective-permute-done((f32[2,3,128,512]{3,2,1,0:T(8,128)S(1)}, f32[2,3,128,512]{3,2,1,0:T(8,128)}, u32[]{:S(2)}, u32[]{:S(2)}) %collective-permute-start.6) | collective-permute-done | bytes 1572896 | tf_op jit(solution)/shard_map/ppermute | solution.py:320
  82.0 3.1 %collective-permute-done.8.refs_1_ = f32[8,384,128]{2,1,0:T(8,128)} collective-permute-done((f32[8,384,128]{2,1,0:T(8,128)}, f32[8,384,128]{2,1,0:T(8,128)}, u32[]{:S(2)}, u32[]{:S(2)}) %collective-permute-start.8) | collective-permute-done | bytes 1572896 | tf_op jit(solution)/shard_map/ppermute | solution.py:321
  85.2 2.7 %collective-permute-start.10 = (f32[2,3,128,512]{3,2,1,0:T(8,128)}, f32[2,3,128,512]{3,2,1,0:T(8,128)S(1)}, u32[]{:S(2)}, u32[]{:S(2)}) collective-permute-start(f32[2,3,128,512]{3,2,1,0:T(8,128)} %collective-permute-done.6.refs_8_), channel_id=1, source_target_pairs={{0,32},{1,97},{2,34},{3,99},{4,36},{5,101},{6,38},{7,103},{16,48},... | collective-permute-start | bytes 4718600 | tf_op jit(solution)/shard_map/ppermute | solution.py:320
  87.9 2.1 %collective-permute-start.11 = (f32[8,384,128]{2,1,0:T(8,128)}, f32[8,384,128]{2,1,0:T(8,128)S(1)}, u32[]{:S(2)}, u32[]{:S(2)}) collective-permute-start(f32[8,384,128]{2,1,0:T(8,128)} %collective-permute-done.8.refs_1_), channel_id=1, source_target_pairs={{0,16},{1,25},{2,18},{3,27},{4,20},{5,29},{6,22},{7,31},{16,8},{17... | collective-permute-start | bytes 4718600 | tf_op jit(solution)/shard_map/ppermute | solution.py:321
  90.7 14.2 %shard_map.66 = (bf16[2,384,512]{2,1,0:T(8,128)(2,1)}, bf16[2,384,512]{2,1,0:T(8,128)(2,1)}, bf16[2,2,4,128,512]{4,3,2,1,0:T(8,128)(2,1)}, bf16[2,2,4,128,512]{4...) custom-call(s32[3]{0:T(128)} %pad_add_fusion.at, f32[8,384,128]{2,1,0:T(8,128)} %all-to-all-done.refs_0_, ...), custom_call_target="tpu_custom_call" | custom-call | flops 7247757312 | bytes 25165824 | tf_op jit(solution)/shard_map/pallas_call | solution.py:186
  105.6 2.1 %collective-permute-done.11.src_far = f32[8,384,128]{2,1,0:T(8,128)S(1)} collective-permute-done((f32[8,384,128]{2,1,0:T(8,128)}, f32[8,384,128]{2,1,0:T(8,128)S(1)}, u32[]{:S(2)}, u32[]{:S(2)}) %collective-permute-start.11) | collective-permute-done | bytes 1572896 | tf_op jit(solution)/shard_map/ppermute | solution.py:321
  107.7 1.1 copy-done
  108.8 1.1 copy-done.1
  110.0 1.6 %copy-done.3 = bf16[2,2,4,128,512]{4,3,2,1,0:T(8,128)(2,1)S(1)} copy-done((bf16[2,2,4,128,512]{4,3,2,1,0:T(8,128)(2,1)S(1)}, bf16[2,2,4,128,512]{4,3,2,1,0:T(8,128)(2,1)}, u32[]{:S(2)}) %copy-start.3) | copy-done | bytes 2097176
  111.5 1.4 copy-done.6
  113.0 4.7 %shard_map.68 = f32[8,384,128]{2,1,0:T(8,128)S(1)} custom-call(s32[4]{0:T(128)S(1)} %add_add_fusion.1.at, f32[2,384,512]{2,1,0:T(8,128)S(1)} %copy-done.6, f32[8,384,128]{2,1,0:T(8,128)S(1)} %collective-permute-done.11.src_far, f32[2,3,128,512]{3,2,1,0:T(8,128)S(1)} %collective-permute-done.10.src_near, bf16[2,384,512]{2,1,0:T(8,128)(2,1)S(1)} %copy-done, ...), custom_call_target="tpu_custom_call" | custom-call | flops 2415919104 | bytes 8388608 | tf_op jit(solution)/shard_map/pallas_call | solution.py:249
  117.7 1.0 collective-permute-start.12
  118.7 4.7 %shard_map.67.a = f32[8,384,128]{2,1,0:T(8,128)S(1)} custom-call(s32[4]{0:T(128)S(1)} %add_add_fusion.at, f32[2,384,512]{2,1,0:T(8,128)S(1)} %copy-done.5, f32[8,384,128]{2,1,0:T(8,128)S(1)} %collective-permute-done.11.src_far, f32[2,3,128,512]{3,2,1,0:T(8,128)S(1)} %collective-permute-done.10.src_near, bf16[2,384,512]{2,1,0:T(8,128)(2,1)S(1)} %copy-done, ...), custom_call_target="tpu_custom_call" | custom-call | flops 2415919104 | bytes 8388608 | tf_op jit(solution)/shard_map/pallas_call | solution.py:249
  123.4 1.3 shard_map.69
  124.8 4.0 %all-to-all-start.1 = ((f32[8,384,128]{2,1,0:T(8,128)}), f32[8,384,128]{2,1,0:T(8,128)S(1)}, u32[]{:S(2)}, u32[]{:S(2)}) async-start(f32[8,384,128]{2,1,0:T(8,128)} %shard_map.69), calls=%async_computation.1 | async-start | bytes 3145728 | tf_op jit(solution)/shard_map/all_to_all | solution.py:337
  129.2 21.1 %all-to-all-done.1.part = f32[8,384,128]{2,1,0:T(8,128)S(1)} async-done(((f32[8,384,128]{2,1,0:T(8,128)}), f32[8,384,128]{2,1,0:T(8,128)S(1)}, u32[]{:S(2)}, u32[]{:S(2)}) %all-to-all-start.1) | async-done | bytes 1572896 | tf_op jit(solution)/shard_map/all_to_all | solution.py:337
  150.3 1.6 %shard_map.70 = f32[384,256]{1,0:T(8,128)} custom-call(s32[1]{0:T(128)} %constant.46.clone.1.unused, f32[8,384,128]{2,1,0:T(8,128)S(1)} %all-to-all-done.1.part, f32[384,256]{1,0:T(8,128)S(1)} %copy-done.8, f32[384,1]{1,0:T(8,128)S(1)} %broadcast_in_dim.12.row, f32[1,256]{1,0:T(1,128)S(1)} %bitcast.15), custom_call_target="tpu_custom_call" | custom-call | bytes 3145728 | tf_op jit(solution)/shard_map/pallas_call | solution.py:36
  (53 shorter events, 2.2 us)
Async XLA Ops:
  0.0 1.4 copy-start.7
  4.0 6.0 %copy-start.4 = (f32[4,32,8,512]{3,2,1,0:T(8,128)S(1)}, f32[4,32,8,512]{3,2,1,0:T(8,128)}, u32[]{:S(2)}) copy-start(f32[4,32,8,512]{3,2,1,0:T(8,128)} %src.2) | copy-start | bytes 6291460
  4.0 42.8 %all-to-all-start = ((f32[8,384,128]{2,1,0:T(8,128)}), f32[8,384,128]{2,1,0:T(8,128)}, u32[]{:S(2)}, u32[]{:S(2)}) async-start(f32[8,384,128]{2,1,0:T(8,128)} %shard_map.64), calls=%async_computation | async-start | bytes 3145728 | tf_op jit(solution)/shard_map/all_to_all | solution.py:323
  11.4 25.0 %copy-start.9 = (f32[2,128,512]{2,1,0:T(8,128)}, f32[2,128,512]{2,1,0:T(8,128)S(1)}, u32[]{:S(2)}) copy-start(f32[2,128,512]{2,1,0:T(8,128)S(1)} %get-tuple-element.35.refs_3_) | copy-start | bytes 1572868
  11.4 25.0 %collective-permute-start = (f32[2,128,512]{2,1,0:T(8,128)S(1)}, f32[2,128,512]{2,1,0:T(8,128)S(1)}, u32[]{:S(2)}, u32[]{:S(2)}) collective-permute-start(f32[2,128,512]{2,1,0:T(8,128)S(1)} %get-tuple-element.32), channel_id=1, source_target_pairs={{0,16},{1,25},{2,18},{3,27},{4,20},{5,29},{6,22},{7,31},{16,8},{17... | collective-permute-start | bytes 1572872 | tf_op jit(solution)/shard_map/ppermute | solution.py:321
  14.3 23.8 %collective-permute-start.1 = (f32[2,128,512]{2,1,0:T(8,128)S(1)}, f32[2,128,512]{2,1,0:T(8,128)S(1)}, u32[]{:S(2)}, u32[]{:S(2)}) collective-permute-start(f32[2,128,512]{2,1,0:T(8,128)S(1)} %get-tuple-element.33), channel_id=1, source_target_pairs={{0,24},{1,17},{2,26},{3,19},{4,28},{5,21},{6,30},{7,23},{16,0},{17... | collective-permute-start | bytes 1572872 | tf_op jit(solution)/shard_map/ppermute | solution.py:321
  14.3 25.3 %collective-permute-start.2 = (f32[2,128,512]{2,1,0:T(8,128)S(1)}, f32[2,128,512]{2,1,0:T(8,128)S(1)}, u32[]{:S(2)}, u32[]{:S(2)}) collective-permute-start(f32[2,128,512]{2,1,0:T(8,128)S(1)} %get-tuple-element.34), channel_id=1, source_target_pairs={{0,8},{1,9},{2,10},{3,11},{4,12},{5,13},{6,14},{7,15},{16,24},{17,... | collective-permute-start | bytes 1572872 | tf_op jit(solution)/shard_map/ppermute | solution.py:321
  15.9 23.6 %collective-permute-start.3 = (f32[2,128,512]{2,1,0:T(8,128)S(1)}, f32[2,128,512]{2,1,0:T(8,128)S(1)}, u32[]{:S(2)}, u32[]{:S(2)}) collective-permute-start(f32[2,128,512]{2,1,0:T(8,128)S(1)} %get-tuple-element.35.refs_3_), channel_id=1, source_target_pairs={{0,32},{1,97},{2,34},{3,99},{4,36},{5,101},{6,38},{7,103},{16,48},... | collective-permute-start | bytes 1572872 | tf_op jit(solution)/shard_map/ppermute | solution.py:320
  19.7 19.9 %collective-permute-start.4 = (f32[2,128,512]{2,1,0:T(8,128)S(1)}, f32[2,128,512]{2,1,0:T(8,128)S(1)}, u32[]{:S(2)}, u32[]{:S(2)}) collective-permute-start(f32[2,128,512]{2,1,0:T(8,128)S(1)} %get-tuple-element.35.refs_3_), channel_id=1, source_target_pairs={{0,64},{1,65},{2,66},{3,67},{4,68},{5,69},{6,70},{7,71},{16,80},{1... | collective-permute-start | bytes 1572872 | tf_op jit(solution)/shard_map/ppermute | solution.py:320
  36.5 10.3 %collective-permute-start.5 = (f32[2,128,512]{2,1,0:T(8,128)S(1)}, f32[2,128,512]{2,1,0:T(8,128)}, u32[]{:S(2)}, u32[]{:S(2)}) collective-permute-start(f32[2,128,512]{2,1,0:T(8,128)S(1)} %get-tuple-element.35.refs_3_), channel_id=1, source_target_pairs={{0,96},{1,33},{2,98},{3,35},{4,100},{5,37},{6,102},{7,39},{16,112}... | collective-permute-start | bytes 1572872 | tf_op jit(solution)/shard_map/ppermute | solution.py:320
  39.5 0.8 copy-start.16
  47.0 38.2 %copy-start.10 = (f32[2,3,128,512]{3,2,1,0:T(8,128)}, f32[2,3,128,512]{3,2,1,0:T(8,128)S(1)}, u32[]{:S(2)}) copy-start(f32[2,3,128,512]{3,2,1,0:T(8,128)S(1)} %pad_maximum_fusion.refs_7_) | copy-start | bytes 4718596
  47.0 35.0 %collective-permute-start.6 = (f32[2,3,128,512]{3,2,1,0:T(8,128)S(1)}, f32[2,3,128,512]{3,2,1,0:T(8,128)}, u32[]{:S(2)}, u32[]{:S(2)}) collective-permute-start(f32[2,3,128,512]{3,2,1,0:T(8,128)S(1)} %pad_maximum_fusion.refs_7_), channel_id=1, source_target_pairs={{0,32},{1,97},{2,34},{3,99},{4,36},{5,101},{6,38},{7,103},{16,48},... | collective-permute-start | bytes 4718600 | tf_op jit(solution)/shard_map/ppermute | solution.py:320
  48.6 33.4 %collective-permute-start.7 = (f32[2,3,128,512]{3,2,1,0:T(8,128)S(1)}, f32[2,3,128,512]{3,2,1,0:T(8,128)S(1)}, u32[]{:S(2)}, u32[]{:S(2)}) collective-permute-start(f32[2,3,128,512]{3,2,1,0:T(8,128)S(1)} %pad_maximum_fusion.refs_7_), channel_id=1, source_target_pairs={{0,96},{1,33},{2,98},{3,35},{4,100},{5,37},{6,102},{7,39},{16,112}... | collective-permute-start | bytes 4718600 | tf_op jit(solution)/shard_map/ppermute | solution.py:320
  48.6 36.6 %collective-permute-start.8 = (f32[8,384,128]{2,1,0:T(8,128)}, f32[8,384,128]{2,1,0:T(8,128)}, u32[]{:S(2)}, u32[]{:S(2)}) collective-permute-start(f32[8,384,128]{2,1,0:T(8,128)} %all-to-all-done.refs_0_), channel_id=1, source_target_pairs={{0,16},{1,25},{2,18},{3,27},{4,20},{5,29},{6,22},{7,31},{16,8},{17... | collective-permute-start | bytes 4718600 | tf_op jit(solution)/shard_map/ppermute | solution.py:321
  53.8 31.4 %collective-permute-start.9 = (f32[8,384,128]{2,1,0:T(8,128)}, f32[8,384,128]{2,1,0:T(8,128)S(1)}, u32[]{:S(2)}, u32[]{:S(2)}) collective-permute-start(f32[8,384,128]{2,1,0:T(8,128)} %all-to-all-done.refs_0_), channel_id=1, source_target_pairs={{0,24},{1,17},{2,26},{3,19},{4,28},{5,21},{6,30},{7,23},{16,0},{17... | collective-permute-start | bytes 4718600 | tf_op jit(solution)/shard_map/ppermute | solution.py:321
  82.0 5.9 %copy-start.14 = (f32[2,3,128,512]{3,2,1,0:T(8,128)}, f32[2,3,128,512]{3,2,1,0:T(8,128)S(1)}, u32[]{:S(2)}) copy-start(f32[2,3,128,512]{3,2,1,0:T(8,128)S(1)} %collective-permute-done.7.refs_9_) | copy-start | bytes 4718596
  85.2 2.7 %copy-start.15 = (f32[8,384,128]{2,1,0:T(8,128)}, f32[8,384,128]{2,1,0:T(8,128)S(1)}, u32[]{:S(2)}) copy-start(f32[8,384,128]{2,1,0:T(8,128)S(1)} %collective-permute-done.9.refs_2_) | copy-start | bytes 4718596
  85.2 20.4 %collective-permute-start.10 = (f32[2,3,128,512]{3,2,1,0:T(8,128)}, f32[2,3,128,512]{3,2,1,0:T(8,128)S(1)}, u32[]{:S(2)}, u32[]{:S(2)}) collective-permute-start(f32[2,3,128,512]{3,2,1,0:T(8,128)} %collective-permute-done.6.refs_8_), channel_id=1, source_target_pairs={{0,32},{1,97},{2,34},{3,99},{4,36},{5,101},{6,38},{7,103},{16,48},... | collective-permute-start | bytes 4718600 | tf_op jit(solution)/shard_map/ppermute | solution.py:320
  87.9 19.8 %collective-permute-start.11 = (f32[8,384,128]{2,1,0:T(8,128)}, f32[8,384,128]{2,1,0:T(8,128)S(1)}, u32[]{:S(2)}, u32[]{:S(2)}) collective-permute-start(f32[8,384,128]{2,1,0:T(8,128)} %collective-permute-done.8.refs_1_), channel_id=1, source_target_pairs={{0,16},{1,25},{2,18},{3,27},{4,20},{5,29},{6,22},{7,31},{16,8},{17... | collective-permute-start | bytes 4718600 | tf_op jit(solution)/shard_map/ppermute | solution.py:321
  107.7 1.1 copy-start
  108.8 1.1 copy-start.1
  110.0 1.6 %copy-start.3 = (bf16[2,2,4,128,512]{4,3,2,1,0:T(8,128)(2,1)S(1)}, bf16[2,2,4,128,512]{4,3,2,1,0:T(8,128)(2,1)}, u32[]{:S(2)}) copy-start(bf16[2,2,4,128,512]{4,3,2,1,0:T(8,128)(2,1)} %get-tuple-element.54.src_b) | copy-start | bytes 6291460
  111.5 1.4 copy-start.6
  113.0 5.8 %copy-start.2 = (bf16[2,2,4,128,512]{4,3,2,1,0:T(8,128)(2,1)S(1)}, bf16[2,2,4,128,512]{4,3,2,1,0:T(8,128)(2,1)}, u32[]{:S(2)}) copy-start(bf16[2,2,4,128,512]{4,3,2,1,0:T(8,128)(2,1)} %get-tuple-element.52.src_b) | copy-start | bytes 6291460
  113.0 5.8 %copy-start.5 = (f32[2,384,512]{2,1,0:T(8,128)S(1)}, f32[2,384,512]{2,1,0:T(8,128)}, u32[]{:S(2)}) copy-start(f32[2,384,512]{2,1,0:T(8,128)} %get-tuple-element.47.src_sum) | copy-start | bytes 4718596
  117.7 5.8 %collective-permute-start.12 = (f32[8,384,128]{2,1,0:T(8,128)S(1)}, f32[8,384,128]{2,1,0:T(8,128)S(1)}, u32[]{:S(2)}, u32[]{:S(2)}) collective-permute-start(f32[8,384,128]{2,1,0:T(8,128)S(1)} %shard_map.68), channel_id=1, source_target_pairs={{0,1},{1,0},{2,3},{3,2},{4,5},{5,4},{6,7},{7,6},{16,17},{17,16},{1... | collective-permute-start | bytes 4718600 | tf_op jit(solution)/shard_map/ppermute | solution.py:336
  124.8 4.0 %copy-start.11 = (f32[512]{0:T(512)S(1)}, f32[512]{0:T(512)}, u32[]{:S(2)}) copy-start(f32[512]{0:T(512)} %param.11) | copy-start | bytes 6148
  124.8 4.0 %copy-start.12 = (f32[6]{0:T(128)S(1)}, f32[6]{0:T(128)}, u32[]{:S(2)}) copy-start(f32[6]{0:T(128)} %param.9) | copy-start | bytes 76
  124.8 4.3 %copy-start.13 = (f32[8]{0:T(128)S(1)}, f32[8]{0:T(128)}, u32[]{:S(2)}) copy-start(f32[8]{0:T(128)} %param.10) | copy-start | bytes 100
  124.8 25.5 %copy-start.8 = (f32[384,256]{1,0:T(8,128)S(1)}, f32[384,256]{1,0:T(8,128)}, u32[]{:S(2)}) copy-start(f32[384,256]{1,0:T(8,128)} %given.1) | copy-start | bytes 1179652
  124.8 25.5 %all-to-all-start.1 = ((f32[8,384,128]{2,1,0:T(8,128)}), f32[8,384,128]{2,1,0:T(8,128)S(1)}, u32[]{:S(2)}, u32[]{:S(2)}) async-start(f32[8,384,128]{2,1,0:T(8,128)} %shard_map.69), calls=%async_computation.1 | async-start | bytes 3145728 | tf_op jit(solution)/shard_map/all_to_all | solution.py:337
  (1 other events, 0.8 us)

commit v3 on v2

--- a/solution.py
+++ b/solution.py
@@ -126,7 +126,8 @@
     def body(at, *refs):
         src_a, src_own, src_near = refs[:3], refs[3:7], refs[7:10]
         out_a, out_b, sums = refs[10:12], refs[12:14], refs[14:16]
-        raw_a, raw_own, raw_near, a, b, total, sem, done = refs[16:]
+        raw_a, raw_own, raw_near, a, b, total, sem, done = refs[17:]
+        refs[16][...] = jnp.zeros((8, 128), F32)
         core, z, y = at[0], at[1], at[2]
         way = 1 - 2 * core
         yl, yh = y & 1, y // 2
@@ -139,7 +140,7 @@
                 [pltpu.make_async_copy(src_own[s].at[half], raw_own.at[n, s], sem.at[3 + n * 7 + s]) for s in range(4)]
                 + [pltpu.make_async_copy(src_near[s].at[half], raw_near.at[n, s], sem.at[7 + n * 7 + s]) for s in range(3)]
             )
-        for copy in loads_a + loads_b[0] + loads_b[1]:
+        for copy in loads_a + loads_b[0]:
             copy.start()
         stores = []
 
@@ -159,6 +160,9 @@
         for n, half in enumerate(halves):
             for copy in loads_b[n]:
                 copy.wait()
+            if n == 0:
+                for copy in loads_b[1]:
+                    copy.start()
             for s in range(4):
                 slot = (z - s * way) & 3
                 b[n, slot, 0, y], b[n, slot, 1, y] = two_parts(raw_own[n, s])
@@ -186,10 +190,11 @@
     return pl.pallas_call(
         body,
         in_specs=[SMALL] + [ANY] * 10,
-        out_specs=[ANY] * 6,
+        out_specs=[ANY] * 6 + [pl.BlockSpec(memory_space=pltpu.VMEM)],
         out_shape=[jax.ShapeDtypeStruct((2, rows, 512), BF16)] * 2
         + [jax.ShapeDtypeStruct((2, 2, 4, 128, 512), BF16)] * 2
-        + [jax.ShapeDtypeStruct((2, rows, 512), F32)] * 2,
+        + [jax.ShapeDtypeStruct((2, rows, 512), F32)] * 2
+        + [jax.ShapeDtypeStruct((8, 128), F32)],
         scratch_shapes=[
             pltpu.VMEM((3, 8, rows, 128), F32),
             pltpu.VMEM((2, 4, 128, 512), F32),
@@ -205,10 +210,10 @@
     )(place, *ints, *own, *near)
 
 
-def last_products(place, sums, ints, near, own_a, other_a, far_b):
+def last_products(place, sums, ints, near, own_a, other_a, far_b, ended):
     rows = sums.shape[1]
 
-    def body(at, src_sum, src_far, src_near, src_own, src_other, src_b, out, *refs):
+    def body(at, src_sum, src_far, src_near, src_own, src_other, src_b, unused, out, *refs):
         total, raw, raw_near, own, other, far, b, late, sem = refs
         half, z, y, core = at[0], at[1], at[2], at[3]
         way = 1 - 2 * core
@@ -248,7 +253,7 @@
 
     return pl.pallas_call(
         body,
-        in_specs=[SMALL] + [ANY] * 6,
+        in_specs=[SMALL] + [ANY] * 7,
         out_specs=pl.BlockSpec(memory_space=pltpu.VMEM),
         out_shape=jax.ShapeDtypeStruct((8, rows, 128), F32),
         scratch_shapes=[
@@ -264,7 +269,19 @@
         ],
         cost_estimate=pl.CostEstimate(flops=6 * rows * 2048 * 512, bytes_accessed=8 << 20, transcendentals=0),
         compiler_params=pltpu.CompilerParams(vmem_limit_bytes=VMEM_LAST),
-    )(place, sums, ints, near, own_a, other_a, far_b)
+    )(place, sums, ints, near, own_a, other_a, far_b, ended)
+
+
+def passed(ended):
+    def body(a, b):
+        b[...] = a[...]
+
+    return pl.pallas_call(
+        body,
+        out_shape=jax.ShapeDtypeStruct(ended.shape, F32),
+        cost_estimate=pl.CostEstimate(flops=12 * 10**9, bytes_accessed=8192, transcendentals=0),
+        compiler_params=pltpu.CompilerParams(vmem_limit_bytes=4 << 20),
+    )(ended)
 
 
 def total_of(one, two):
@@ -283,28 +300,18 @@
 
 def finish(parts, driver, row_part, col_part):
     rows = driver.shape[0]
-    step = rows // 3
-
-    def body(unused, part, given, row, col, out):
+
+    def body(part, given, row, col, out):
         for yl in range(2):
             lanes = slice(yl * 128, (yl + 1) * 128)
             cycle = (part[yl * 4] + part[yl * 4 + 1]) + (part[yl * 4 + 2] + part[yl * 4 + 3])
             out[:, lanes] = (given[:, lanes] + cycle) / (row[...] + col[:, lanes])
 
-    return call(
-        body,
-        (3,),
-        [
-            pl.BlockSpec((8, step, 128), lambda r, t: (0, r, 0)),
-            pl.BlockSpec((step, 256), lambda r, t: (r, 0)),
-            pl.BlockSpec((step, 1), lambda r, t: (r, 0)),
-            pl.BlockSpec((1, 256), lambda r, t: (0, 0)),
-        ],
-        pl.BlockSpec((step, 256), lambda r, t: (r, 0)),
-        jax.ShapeDtypeStruct((rows, 256), F32),
-        jnp.zeros((1,), jnp.int32),
-        (parts, driver, row_part, col_part),
-    )
+    return pl.pallas_call(
+        body,
+        out_shape=jax.ShapeDtypeStruct((rows, 256), F32),
+        compiler_params=pltpu.CompilerParams(vmem_limit_bytes=8 << 20),
+    )(parts, driver, row_part, col_part)
 
 
 def shards(integrals, amplitudes, driver, occ_rows, occ_cols, virtual):
@@ -321,18 +328,24 @@
     on_y = lambda v, d: lax.ppermute(v, AXES, Y_ON[d])
     wave = lambda *v: list(lax.optimization_barrier(v))
     ints = lax.all_to_all(ints, ("x", "core"), 0, 0, tiled=True)
-    b, c, d = on_y(parts[1], 1), on_y(parts[3], 3), on_y(parts[2], 2)
-    own = [parts[0]] + [on_z(parts[0], step) for step in (1, 2, 3)]
+    b = on_y(parts[1], 1)
+    own2 = on_z(parts[0], 2)
+    d = on_y(parts[2], 2)
+    own1 = on_z(parts[0], 1)
+    c = on_y(parts[3], 3)
+    own3 = on_z(parts[0], 3)
+    own = [parts[0], own1, own2, own3]
     ints, b, c, d, *own[1:] = wave(ints, b, c, d, *own[1:])
     bcd = jnp.stack([b, c, d], axis=1)
-    bcd1, bcd3, ints1, ints3 = wave(on_z(bcd, 1), on_z(bcd, 3), on_y(ints, 1), on_y(ints, 3))
+    bcd1, bcd3 = on_z(bcd, 1), on_z(bcd, 3)
+    ints1, ints3 = on_y(ints, 1), on_y(ints, 3)
     bcd2, ints2 = on_z(bcd1, 1), on_y(ints1, 1)
-    own_a, other_a, far_other, far_mine, sum_other, sum_mine = first_products(
+    own_a, other_a, far_other, far_mine, sum_other, sum_mine, ended = first_products(
         number(core, z, y), (ints, ints1, ints3), own, (bcd, bcd1, bcd3)
     )
-    bcd2, ints2 = wave(bcd2, ints2)
-    other = last_products(number(1 - core, z, y, core), sum_other, ints2, bcd2, own_a, other_a, far_other)
-    mine = last_products(number(core, z, y, core), sum_mine, ints2, bcd2, own_a, other_a, far_mine)
+    bcd2, ints2, ended = wave(bcd2, ints2, passed(ended))
+    other = last_products(number(1 - core, z, y, core), sum_other, ints2, bcd2, own_a, other_a, far_other, ended)
+    mine = last_products(number(core, z, y, core), sum_mine, ints2, bcd2, own_a, other_a, far_mine, ended)
     mine = total_of(mine, lax.ppermute(other, AXES, SWAP))
     mine = lax.all_to_all(mine, ("yl", "x"), 0, 0, tiled=True)
     row_energy = (occ_rows[:, None] - virtual[None, :]).reshape(-1)

time: 152 us -> 146 us (0.961)
  local copies, waits for them, and re-layouts: 8.58 us -> 3.14 us
  starting transfers between devices: 32.2 us -> 30.6 us
    unnamed x37 -> x39, local copies, waits for them, and re-layouts: 8.32 us -> 2.86 us
    ppermute x6, waiting for transfers between devices: 23.6 us -> 20.3 us  [shards(): on_y = lambda v, d: lax.ppermute(v, AXES, Y_ON[d])]
    ppermute x6, waiting for transfers between devices: 34.5 us -> 37.2 us  [shards(): on_z = lambda v, d: lax.ppermute(v, AXES, Z_ON[d])]
    pallas_call x3 -> x2, Pallas kernels: 5.63 us -> 4 us  [call(): pl.pallas_call(body, grid_spec=pltpu.PrefetchScalarGridSpec(num_scalar_pr...]
    pallas_call x3 -> x5, Pallas kernels: 23.6 us -> 25.2 us  [the longest x1 14.8 us: first_products(): pl.pallas_call(body, in_specs=[SMALL] + [ANY] * 10, out_specs=[ANY] * 6 +...]
  transfers between devices with their start and end apart: 15 -> 15, of which waited for: 9 -> 7; matrix products, arithmetic and copies ran while one was open for 1% -> 1% of each run, Pallas kernels for 13% -> 14%
where the time goes in v3:
time: 146 us; the launch traced here: 145 us
  waiting for transfers between devices  78.5 us (54%)
  starting transfers between devices  30.6 us (21%)
  Pallas kernels  30.5 us (21%)
  local copies, waits for them, and re-layouts  3.14 us (2%)
  other arithmetic  2.25 us (2%)
    ppermute x6, waiting for transfers between devices, shards(): on_z = lambda v, d: lax.ppermute(v, AXES, Z_ON[d])  37.2 us
    all_to_all x1, waiting for transfers between devices, shards(): mine = lax.all_to_all(mine, ('yl', 'x'), 0, 0, tiled=True)  21 us
    ppermute x6, waiting for transfers between devices, shards(): on_y = lambda v, d: lax.ppermute(v, AXES, Y_ON[d])  20.3 us
    pallas_call x1, Pallas kernels, first_products(): pl.pallas_call(body, in_specs=[SMALL] + [ANY] * 10, out_specs=[ANY] * 6 +...  14.8 us
    ppermute x6, starting transfers between devices, shards(): on_y = lambda v, d: lax.ppermute(v, AXES, Y_ON[d])  11.4 us
    pallas_call x2, Pallas kernels, last_products(): pl.pallas_call(body, in_specs=[SMALL] + [ANY] * 7, out_specs=pl.BlockSpec...  9.4 us
    ppermute x6, starting transfers between devices, shards(): on_z = lambda v, d: lax.ppermute(v, AXES, Z_ON[d])  8.9 us
    all_to_all x1, starting transfers between devices, shards(): ints = lax.all_to_all(ints, ('x', 'core'), 0, 0, tiled=True)  5.93 us
  transfers between devices with their start and end apart: 15, of which 7 were waited for; matrix products, arithmetic and copies ran while one was open for 1% of the time, Pallas kernels for 14%

profile of v3, /device:TPU:1, one launch (start us, length us, event | category | flops | bytes accessed | tf_op | source)
XLA Modules:
  0.0 145.2 jit_solution(14534567880740158931)
XLA Ops:
  0.0 1.4 copy-done.7
  1.4 2.6 %shard_map.64 = f32[8,384,128]{2,1,0:T(8,128)} custom-call(s32[1]{0:T(128)} %constant.51.clone.1.unused, f32[384,1024]{1,0:T(8,128)S(1)} %copy-done.7), custom_call_target="tpu_custom_call" | custom-call | bytes 3145728 | tf_op jit(solution)/shard_map/pallas_call | solution.py:36
  4.0 5.9 %all-to-all-start = ((f32[8,384,128]{2,1,0:T(8,128)}), f32[8,384,128]{2,1,0:T(8,128)}, u32[]{:S(2)}, u32[]{:S(2)}) async-start(f32[8,384,128]{2,1,0:T(8,128)} %shard_map.64), calls=%async_computation | async-start | bytes 3145728 | tf_op jit(solution)/shard_map/all_to_all | solution.py:330
  10.0 1.4 shard_map.65
  11.4 2.8 %collective-permute-start = (f32[2,128,512]{2,1,0:T(8,128)S(1)}, f32[2,128,512]{2,1,0:T(8,128)S(1)}, u32[]{:S(2)}, u32[]{:S(2)}) collective-permute-start(f32[2,128,512]{2,1,0:T(8,128)S(1)} %get-tuple-element.30), channel_id=1, source_target_pairs={{0,16},{1,25},{2,18},{3,27},{4,20},{5,29},{6,22},{7,31},{16,8},{17... | collective-permute-start | bytes 1572872 | tf_op jit(solution)/shard_map/ppermute | solution.py:328
  14.3 1.6 %collective-permute-start.2 = (f32[2,128,512]{2,1,0:T(8,128)S(1)}, f32[2,128,512]{2,1,0:T(8,128)S(1)}, u32[]{:S(2)}, u32[]{:S(2)}) collective-permute-start(f32[2,128,512]{2,1,0:T(8,128)S(1)} %get-tuple-element.32), channel_id=1, source_target_pairs={{0,8},{1,9},{2,10},{3,11},{4,12},{5,13},{6,14},{7,15},{16,24},{17,... | collective-permute-start | bytes 1572872 | tf_op jit(solution)/shard_map/ppermute | solution.py:328
  15.9 3.8 %collective-permute-start.3 = (f32[2,128,512]{2,1,0:T(8,128)S(1)}, f32[2,128,512]{2,1,0:T(8,128)S(1)}, u32[]{:S(2)}, u32[]{:S(2)}) collective-permute-start(f32[2,128,512]{2,1,0:T(8,128)S(1)} %get-tuple-element.33.refs_3_), channel_id=1, source_target_pairs={{0,32},{1,97},{2,34},{3,99},{4,36},{5,101},{6,38},{7,103},{16,48},... | collective-permute-start | bytes 1572872 | tf_op jit(solution)/shard_map/ppermute | solution.py:327
  19.7 16.8 %collective-permute-done = f32[2,128,512]{2,1,0:T(8,128)S(1)} collective-permute-done((f32[2,128,512]{2,1,0:T(8,128)S(1)}, f32[2,128,512]{2,1,0:T(8,128)S(1)}, u32[]{:S(2)}, u32[]{:S(2)}) %collective-permute-start) | collective-permute-done | bytes 524320 | tf_op jit(solution)/shard_map/ppermute | solution.py:328
  36.5 1.6 %collective-permute-start.5 = (f32[2,128,512]{2,1,0:T(8,128)S(1)}, f32[2,128,512]{2,1,0:T(8,128)}, u32[]{:S(2)}, u32[]{:S(2)}) collective-permute-start(f32[2,128,512]{2,1,0:T(8,128)S(1)} %get-tuple-element.33.refs_3_), channel_id=1, source_target_pairs={{0,96},{1,33},{2,98},{3,35},{4,100},{5,37},{6,102},{7,39},{16,112}... | collective-permute-start | bytes 1572872 | tf_op jit(solution)/shard_map/ppermute | solution.py:327
  38.0 1.5 %collective-permute-done.2 = f32[2,128,512]{2,1,0:T(8,128)S(1)} collective-permute-done((f32[2,128,512]{2,1,0:T(8,128)S(1)}, f32[2,128,512]{2,1,0:T(8,128)S(1)}, u32[]{:S(2)}, u32[]{:S(2)}) %collective-permute-start.2) | collective-permute-done | bytes 524320 | tf_op jit(solution)/shard_map/ppermute | solution.py:328
  39.5 7.3 %collective-permute-done.5.refs_6_ = f32[2,128,512]{2,1,0:T(8,128)} collective-permute-done((f32[2,128,512]{2,1,0:T(8,128)S(1)}, f32[2,128,512]{2,1,0:T(8,128)}, u32[]{:S(2)}, u32[]{:S(2)}) %collective-permute-start.5) | collective-permute-done | bytes 524320 | tf_op jit(solution)/shard_map/ppermute | solution.py:327
  46.8 1.2 pad_maximum_fusion.refs_7_
  48.1 1.5 %collective-permute-start.8 = (f32[2,3,128,512]{3,2,1,0:T(8,128)S(1)}, f32[2,3,128,512]{3,2,1,0:T(8,128)}, u32[]{:S(2)}, u32[]{:S(2)}) collective-permute-start(f32[2,3,128,512]{3,2,1,0:T(8,128)S(1)} %pad_maximum_fusion.refs_7_), channel_id=1, source_target_pairs={{0,32},{1,97},{2,34},{3,99},{4,36},{5,101},{6,38},{7,103},{16,48},... | collective-permute-start | bytes 4718600 | tf_op jit(solution)/shard_map/ppermute | solution.py:327
  49.6 3.7 %collective-permute-start.6 = (f32[8,384,128]{2,1,0:T(8,128)}, f32[8,384,128]{2,1,0:T(8,128)S(1)}, u32[]{:S(2)}, u32[]{:S(2)}) collective-permute-start(f32[8,384,128]{2,1,0:T(8,128)} %all-to-all-done.refs_0_), channel_id=1, source_target_pairs={{0,16},{1,25},{2,18},{3,27},{4,20},{5,29},{6,22},{7,31},{16,8},{17... | collective-permute-start | bytes 4718600 | tf_op jit(solution)/shard_map/ppermute | solution.py:328
  53.3 0.5 collective-permute-start.9
  53.8 0.7 pad_add_fusion.at
  54.5 29.9 %collective-permute-done.8.refs_8_ = f32[2,3,128,512]{3,2,1,0:T(8,128)} collective-permute-done((f32[2,3,128,512]{3,2,1,0:T(8,128)S(1)}, f32[2,3,128,512]{3,2,1,0:T(8,128)}, u32[]{:S(2)}, u32[]{:S(2)}) %collective-permute-start.8) | collective-permute-done | bytes 1572896 | tf_op jit(solution)/shard_map/ppermute | solution.py:327
  84.5 1.5 %collective-permute-start.10 = (f32[2,3,128,512]{3,2,1,0:T(8,128)}, f32[2,3,128,512]{3,2,1,0:T(8,128)S(1)}, u32[]{:S(2)}, u32[]{:S(2)}) collective-permute-start(f32[2,3,128,512]{3,2,1,0:T(8,128)} %collective-permute-done.8.refs_8_), channel_id=1, source_target_pairs={{0,32},{1,97},{2,34},{3,99},{4,36},{5,101},{6,38},{7,103},{16,48},... | collective-permute-start | bytes 4718600 | tf_op jit(solution)/shard_map/ppermute | solution.py:327
  86.0 0.2 collective-permute-done.6.refs_1_
  86.2 3.3 %collective-permute-start.11 = (f32[8,384,128]{2,1,0:T(8,128)S(1)}, f32[8,384,128]{2,1,0:T(8,128)S(1)}, u32[]{:S(2)}, u32[]{:S(2)}) collective-permute-start(f32[8,384,128]{2,1,0:T(8,128)S(1)} %collective-permute-done.6.refs_1_), channel_id=1, source_target_pairs={{0,16},{1,25},{2,18},{3,27},{4,20},{5,29},{6,22},{7,31},{16,8},{17... | collective-permute-start | bytes 4718600 | tf_op jit(solution)/shard_map/ppermute | solution.py:328
  89.5 14.8 %shard_map.66 = (bf16[2,384,512]{2,1,0:T(8,128)(2,1)}, bf16[2,384,512]{2,1,0:T(8,128)(2,1)}, bf16[2,2,4,128,512]{4,3,2,1,0:T(8,128)(2,1)}, bf16[2,2,4,128,512]{4...) custom-call(s32[3]{0:T(128)} %pad_add_fusion.at, ...), custom_call_target="tpu_custom_call" | custom-call | flops 7247757312 | bytes 25165824 | tf_op jit(solution)/shard_map/pallas_call | solution.py:190
  104.4 0.7 copy-done.10
  105.1 1.8 %collective-permute-done.11.src_far = f32[8,384,128]{2,1,0:T(8,128)S(1)} collective-permute-done((f32[8,384,128]{2,1,0:T(8,128)S(1)}, f32[8,384,128]{2,1,0:T(8,128)S(1)}, u32[]{:S(2)}, u32[]{:S(2)}) %collective-permute-start.11) | collective-permute-done | bytes 1572896 | tf_op jit(solution)/shard_map/ppermute | solution.py:328
  106.9 0.3 copy-done.4
  107.1 0.4 copy-done.6
  107.6 4.7 %shard_map.69 = f32[8,384,128]{2,1,0:T(8,128)S(1)} custom-call(s32[4]{0:T(128)S(1)} %add_add_fusion.1.at, f32[2,384,512]{2,1,0:T(8,128)S(1)} %copy-done.6, f32[8,384,128]{2,1,0:T(8,128)S(1)} %collective-permute-done.11.src_far, f32[2,3,128,512]{3,2,1,0:T(8,128)S(1)} %collective-permute-done.10.src_near, bf16[2,384,512]{2,1,0:T(8,128)(2,1)S(1)} %copy-done, ...), custom_call_target="tpu_custom_call" | custom-call | flops 2415919104 | bytes 8388608 | tf_op jit(solution)/shard_map/pallas_call | solution.py:254
  112.5 4.7 %shard_map.68.a = f32[8,384,128]{2,1,0:T(8,128)S(1)} custom-call(s32[4]{0:T(128)S(1)} %add_add_fusion.at, f32[2,384,512]{2,1,0:T(8,128)S(1)} %copy-done.5, f32[8,384,128]{2,1,0:T(8,128)S(1)} %collective-permute-done.11.src_far, f32[2,3,128,512]{3,2,1,0:T(8,128)S(1)} %collective-permute-done.10.src_near, bf16[2,384,512]{2,1,0:T(8,128)(2,1)S(1)} %copy-done, ...), custom_call_target="tpu_custom_call" | custom-call | flops 2415919104 | bytes 8388608 | tf_op jit(solution)/shard_map/pallas_call | solution.py:254
  117.2 1.3 shard_map.70
  118.5 4.3 %all-to-all-start.1 = ((f32[8,384,128]{2,1,0:T(8,128)}), f32[8,384,128]{2,1,0:T(8,128)S(1)}, u32[]{:S(2)}, u32[]{:S(2)}) async-start(f32[8,384,128]{2,1,0:T(8,128)} %shard_map.70), calls=%async_computation.1 | async-start | bytes 3145728 | tf_op jit(solution)/shard_map/all_to_all | solution.py:350
  123.1 0.1 broadcast_in_dim.12.row
  123.3 21.0 %all-to-all-done.1.part = f32[8,384,128]{2,1,0:T(8,128)S(1)} async-done(((f32[8,384,128]{2,1,0:T(8,128)}), f32[8,384,128]{2,1,0:T(8,128)S(1)}, u32[]{:S(2)}, u32[]{:S(2)}) %all-to-all-start.1) | async-done | bytes 1572896 | tf_op jit(solution)/shard_map/all_to_all | solution.py:350
  144.3 0.9 shard_map.71
  (56 shorter events, 0.7 us)
Async XLA Ops:
  4.0 6.0 %copy-start.2 = (f32[4,32,8,512]{3,2,1,0:T(8,128)S(1)}, f32[4,32,8,512]{3,2,1,0:T(8,128)}, u32[]{:S(2)}) copy-start(f32[4,32,8,512]{3,2,1,0:T(8,128)} %src.2) | copy-start | bytes 6291460
  4.0 42.8 %all-to-all-start = ((f32[8,384,128]{2,1,0:T(8,128)}), f32[8,384,128]{2,1,0:T(8,128)}, u32[]{:S(2)}, u32[]{:S(2)}) async-start(f32[8,384,128]{2,1,0:T(8,128)} %shard_map.64), calls=%async_computation | async-start | bytes 3145728 | tf_op jit(solution)/shard_map/all_to_all | solution.py:330
  11.4 36.6 %copy-start.9 = (f32[2,128,512]{2,1,0:T(8,128)}, f32[2,128,512]{2,1,0:T(8,128)S(1)}, u32[]{:S(2)}) copy-start(f32[2,128,512]{2,1,0:T(8,128)S(1)} %get-tuple-element.33.refs_3_) | copy-start | bytes 1572868
  11.4 25.0 %collective-permute-start = (f32[2,128,512]{2,1,0:T(8,128)S(1)}, f32[2,128,512]{2,1,0:T(8,128)S(1)}, u32[]{:S(2)}, u32[]{:S(2)}) collective-permute-start(f32[2,128,512]{2,1,0:T(8,128)S(1)} %get-tuple-element.30), channel_id=1, source_target_pairs={{0,16},{1,25},{2,18},{3,27},{4,20},{5,29},{6,22},{7,31},{16,8},{17... | collective-permute-start | bytes 1572872 | tf_op jit(solution)/shard_map/ppermute | solution.py:328
  14.3 23.8 %collective-permute-start.1 = (f32[2,128,512]{2,1,0:T(8,128)S(1)}, f32[2,128,512]{2,1,0:T(8,128)S(1)}, u32[]{:S(2)}, u32[]{:S(2)}) collective-permute-start(f32[2,128,512]{2,1,0:T(8,128)S(1)} %get-tuple-element.31), channel_id=1, source_target_pairs={{0,24},{1,17},{2,26},{3,19},{4,28},{5,21},{6,30},{7,23},{16,0},{17... | collective-permute-start | bytes 1572872 | tf_op jit(solution)/shard_map/ppermute | solution.py:328
  14.3 25.3 %collective-permute-start.2 = (f32[2,128,512]{2,1,0:T(8,128)S(1)}, f32[2,128,512]{2,1,0:T(8,128)S(1)}, u32[]{:S(2)}, u32[]{:S(2)}) collective-permute-start(f32[2,128,512]{2,1,0:T(8,128)S(1)} %get-tuple-element.32), channel_id=1, source_target_pairs={{0,8},{1,9},{2,10},{3,11},{4,12},{5,13},{6,14},{7,15},{16,24},{17,... | collective-permute-start | bytes 1572872 | tf_op jit(solution)/shard_map/ppermute | solution.py:328
  15.9 23.6 %collective-permute-start.3 = (f32[2,128,512]{2,1,0:T(8,128)S(1)}, f32[2,128,512]{2,1,0:T(8,128)S(1)}, u32[]{:S(2)}, u32[]{:S(2)}) collective-permute-start(f32[2,128,512]{2,1,0:T(8,128)S(1)} %get-tuple-element.33.refs_3_), channel_id=1, source_target_pairs={{0,32},{1,97},{2,34},{3,99},{4,36},{5,101},{6,38},{7,103},{16,48},... | collective-permute-start | bytes 1572872 | tf_op jit(solution)/shard_map/ppermute | solution.py:327
  19.7 19.9 %collective-permute-start.4 = (f32[2,128,512]{2,1,0:T(8,128)S(1)}, f32[2,128,512]{2,1,0:T(8,128)S(1)}, u32[]{:S(2)}, u32[]{:S(2)}) collective-permute-start(f32[2,128,512]{2,1,0:T(8,128)S(1)} %get-tuple-element.33.refs_3_), channel_id=1, source_target_pairs={{0,64},{1,65},{2,66},{3,67},{4,68},{5,69},{6,70},{7,71},{16,80},{1... | collective-permute-start | bytes 1572872 | tf_op jit(solution)/shard_map/ppermute | solution.py:327
  36.5 10.3 %collective-permute-start.5 = (f32[2,128,512]{2,1,0:T(8,128)S(1)}, f32[2,128,512]{2,1,0:T(8,128)}, u32[]{:S(2)}, u32[]{:S(2)}) collective-permute-start(f32[2,128,512]{2,1,0:T(8,128)S(1)} %get-tuple-element.33.refs_3_), channel_id=1, source_target_pairs={{0,96},{1,33},{2,98},{3,35},{4,100},{5,37},{6,102},{7,39},{16,112}... | collective-permute-start | bytes 1572872 | tf_op jit(solution)/shard_map/ppermute | solution.py:327
  39.5 7.3 %copy-start.12 = (f32[2,128,512]{2,1,0:T(8,128)}, f32[2,128,512]{2,1,0:T(8,128)S(1)}, u32[]{:S(2)}) copy-start(f32[2,128,512]{2,1,0:T(8,128)S(1)} %collective-permute-done.2) | copy-start | bytes 1572868
  39.5 7.3 %copy-start.17 = (f32[2,128,512]{2,1,0:T(8,128)}, f32[2,128,512]{2,1,0:T(8,128)S(1)}, u32[]{:S(2)}) copy-start(f32[2,128,512]{2,1,0:T(8,128)S(1)} %collective-permute-done.3.refs_4_) | copy-start | bytes 1572868
  39.5 7.3 %copy-start.18 = (f32[2,128,512]{2,1,0:T(8,128)}, f32[2,128,512]{2,1,0:T(8,128)S(1)}, u32[]{:S(2)}) copy-start(f32[2,128,512]{2,1,0:T(8,128)S(1)} %collective-permute-done.4.refs_5_) | copy-start | bytes 1572868
  48.1 41.4 %copy-start.11 = (f32[2,3,128,512]{3,2,1,0:T(8,128)}, f32[2,3,128,512]{3,2,1,0:T(8,128)S(1)}, u32[]{:S(2)}) copy-start(f32[2,3,128,512]{3,2,1,0:T(8,128)S(1)} %pad_maximum_fusion.refs_7_) | copy-start | bytes 4718596
  48.1 36.4 %collective-permute-start.8 = (f32[2,3,128,512]{3,2,1,0:T(8,128)S(1)}, f32[2,3,128,512]{3,2,1,0:T(8,128)}, u32[]{:S(2)}, u32[]{:S(2)}) collective-permute-start(f32[2,3,128,512]{3,2,1,0:T(8,128)S(1)} %pad_maximum_fusion.refs_7_), channel_id=1, source_target_pairs={{0,32},{1,97},{2,34},{3,99},{4,36},{5,101},{6,38},{7,103},{16,48},... | collective-permute-start | bytes 4718600 | tf_op jit(solution)/shard_map/ppermute | solution.py:327
  49.6 36.6 %collective-permute-start.6 = (f32[8,384,128]{2,1,0:T(8,128)}, f32[8,384,128]{2,1,0:T(8,128)S(1)}, u32[]{:S(2)}, u32[]{:S(2)}) collective-permute-start(f32[8,384,128]{2,1,0:T(8,128)} %all-to-all-done.refs_0_), channel_id=1, source_target_pairs={{0,16},{1,25},{2,18},{3,27},{4,20},{5,29},{6,22},{7,31},{16,8},{17... | collective-permute-start | bytes 4718600 | tf_op jit(solution)/shard_map/ppermute | solution.py:328
  53.3 36.2 %collective-permute-start.9 = (f32[2,3,128,512]{3,2,1,0:T(8,128)S(1)}, f32[2,3,128,512]{3,2,1,0:T(8,128)}, u32[]{:S(2)}, u32[]{:S(2)}) collective-permute-start(f32[2,3,128,512]{3,2,1,0:T(8,128)S(1)} %pad_maximum_fusion.refs_7_), channel_id=1, source_target_pairs={{0,96},{1,33},{2,98},{3,35},{4,100},{5,37},{6,102},{7,39},{16,112}... | collective-permute-start | bytes 4718600 | tf_op jit(solution)/shard_map/ppermute | solution.py:327
  53.8 35.7 %collective-permute-start.7 = (f32[8,384,128]{2,1,0:T(8,128)}, f32[8,384,128]{2,1,0:T(8,128)}, u32[]{:S(2)}, u32[]{:S(2)}) collective-permute-start(f32[8,384,128]{2,1,0:T(8,128)} %all-to-all-done.refs_0_), channel_id=1, source_target_pairs={{0,24},{1,17},{2,26},{3,19},{4,28},{5,21},{6,30},{7,23},{16,0},{17... | collective-permute-start | bytes 4718600 | tf_op jit(solution)/shard_map/ppermute | solution.py:328
  84.5 20.6 %collective-permute-start.10 = (f32[2,3,128,512]{3,2,1,0:T(8,128)}, f32[2,3,128,512]{3,2,1,0:T(8,128)S(1)}, u32[]{:S(2)}, u32[]{:S(2)}) collective-permute-start(f32[2,3,128,512]{3,2,1,0:T(8,128)} %collective-permute-done.8.refs_8_), channel_id=1, source_target_pairs={{0,32},{1,97},{2,34},{3,99},{4,36},{5,101},{6,38},{7,103},{16,48},... | collective-permute-start | bytes 4718600 | tf_op jit(solution)/shard_map/ppermute | solution.py:327
  86.2 3.3 %copy-start.16 = (f32[8,384,128]{2,1,0:T(8,128)}, f32[8,384,128]{2,1,0:T(8,128)S(1)}, u32[]{:S(2)}) copy-start(f32[8,384,128]{2,1,0:T(8,128)S(1)} %collective-permute-done.6.refs_1_) | copy-start | bytes 4718596
  86.2 20.7 %collective-permute-start.11 = (f32[8,384,128]{2,1,0:T(8,128)S(1)}, f32[8,384,128]{2,1,0:T(8,128)S(1)}, u32[]{:S(2)}, u32[]{:S(2)}) collective-permute-start(f32[8,384,128]{2,1,0:T(8,128)S(1)} %collective-permute-done.6.refs_1_), channel_id=1, source_target_pairs={{0,16},{1,25},{2,18},{3,27},{4,20},{5,29},{6,22},{7,31},{16,8},{17... | collective-permute-start | bytes 4718600 | tf_op jit(solution)/shard_map/ppermute | solution.py:328
  105.0 1.8 %copy-start = (bf16[2,384,512]{2,1,0:T(8,128)(2,1)S(1)}, bf16[2,384,512]{2,1,0:T(8,128)(2,1)}, u32[]{:S(2)}) copy-start(bf16[2,384,512]{2,1,0:T(8,128)(2,1)} %get-tuple-element.45.src_own) | copy-start | bytes 2359300
  105.1 1.8 %copy-start.1 = (bf16[2,384,512]{2,1,0:T(8,128)(2,1)S(1)}, bf16[2,384,512]{2,1,0:T(8,128)(2,1)}, u32[]{:S(2)}) copy-start(bf16[2,384,512]{2,1,0:T(8,128)(2,1)} %get-tuple-element.46.src_other) | copy-start | bytes 2359300
  105.1 2.1 %copy-start.4 = (bf16[2,2,4,128,512]{4,3,2,1,0:T(8,128)(2,1)S(1)}, bf16[2,2,4,128,512]{4,3,2,1,0:T(8,128)(2,1)}, u32[]{:S(2)}) copy-start(bf16[2,2,4,128,512]{4,3,2,1,0:T(8,128)(2,1)} %get-tuple-element.50.src_b) | copy-start | bytes 6291460
  105.1 2.5 %copy-start.6 = (f32[2,384,512]{2,1,0:T(8,128)S(1)}, f32[2,384,512]{2,1,0:T(8,128)}, u32[]{:S(2)}) copy-start(f32[2,384,512]{2,1,0:T(8,128)} %get-tuple-element.49.src_sum) | copy-start | bytes 4718596
  107.6 4.9 %copy-start.3 = (bf16[2,2,4,128,512]{4,3,2,1,0:T(8,128)(2,1)S(1)}, bf16[2,2,4,128,512]{4,3,2,1,0:T(8,128)(2,1)}, u32[]{:S(2)}) copy-start(bf16[2,2,4,128,512]{4,3,2,1,0:T(8,128)(2,1)} %get-tuple-element.47.src_b) | copy-start | bytes 6291460
  107.6 4.9 %copy-start.5 = (f32[2,384,512]{2,1,0:T(8,128)S(1)}, f32[2,384,512]{2,1,0:T(8,128)}, u32[]{:S(2)}) copy-start(f32[2,384,512]{2,1,0:T(8,128)} %get-tuple-element.41.src_sum) | copy-start | bytes 4718596
  112.3 4.9 %collective-permute-start.12 = (f32[8,384,128]{2,1,0:T(8,128)S(1)}, f32[8,384,128]{2,1,0:T(8,128)S(1)}, u32[]{:S(2)}, u32[]{:S(2)}) collective-permute-start(f32[8,384,128]{2,1,0:T(8,128)S(1)} %shard_map.69), channel_id=1, source_target_pairs={{0,1},{1,0},{2,3},{3,2},{4,5},{5,4},{6,7},{7,6},{16,17},{17,16},{1... | collective-permute-start | bytes 4718600 | tf_op jit(solution)/shard_map/ppermute | solution.py:349
  118.5 4.3 %copy-start.13 = (f32[512]{0:T(512)S(1)}, f32[512]{0:T(512)}, u32[]{:S(2)}) copy-start(f32[512]{0:T(512)} %param.11) | copy-start | bytes 6148
  118.5 4.3 %copy-start.14 = (f32[8]{0:T(128)S(1)}, f32[8]{0:T(128)}, u32[]{:S(2)}) copy-start(f32[8]{0:T(128)} %param.10) | copy-start | bytes 100
  118.5 4.4 %copy-start.15 = (f32[6]{0:T(128)S(1)}, f32[6]{0:T(128)}, u32[]{:S(2)}) copy-start(f32[6]{0:T(128)} %param.9) | copy-start | bytes 76
  118.5 25.8 %copy-start.8 = (f32[384,256]{1,0:T(8,128)S(1)}, f32[384,256]{1,0:T(8,128)}, u32[]{:S(2)}) copy-start(f32[384,256]{1,0:T(8,128)} %given.1) | copy-start | bytes 1179652
  118.5 25.8 %all-to-all-start.1 = ((f32[8,384,128]{2,1,0:T(8,128)}), f32[8,384,128]{2,1,0:T(8,128)S(1)}, u32[]{:S(2)}, u32[]{:S(2)}) async-start(f32[8,384,128]{2,1,0:T(8,128)} %shard_map.70), calls=%async_computation.1 | async-start | bytes 3145728 | tf_op jit(solution)/shard_map/all_to_all | solution.py:350
  (2 other events, 2.1 us)

commit v4 on v3

--- a/solution.py
+++ b/solution.py
@@ -328,14 +328,11 @@
     on_y = lambda v, d: lax.ppermute(v, AXES, Y_ON[d])
     wave = lambda *v: list(lax.optimization_barrier(v))
     ints = lax.all_to_all(ints, ("x", "core"), 0, 0, tiled=True)
-    b = on_y(parts[1], 1)
-    own2 = on_z(parts[0], 2)
-    d = on_y(parts[2], 2)
-    own1 = on_z(parts[0], 1)
-    c = on_y(parts[3], 3)
-    own3 = on_z(parts[0], 3)
+    b, d, c = on_y(parts[1], 1), on_y(parts[2], 2), on_y(parts[3], 3)
+    own1, own3 = on_z(parts[0], 1), on_z(parts[0], 3)
+    own2 = on_z(own1, 1)
+    ints, own1, b, own3, d, c, own2 = wave(ints, own1, b, own3, d, c, own2)
     own = [parts[0], own1, own2, own3]
-    ints, b, c, d, *own[1:] = wave(ints, b, c, d, *own[1:])
     bcd = jnp.stack([b, c, d], axis=1)
     bcd1, bcd3 = on_z(bcd, 1), on_z(bcd, 3)
     ints1, ints3 = on_y(ints, 1), on_y(ints, 3)

time: 146 us -> 144 us (0.986)
  waiting for transfers between devices: 78.5 us -> 74.3 us
    ppermute x6, waiting for transfers between devices: 20.3 us -> 13.9 us  [shards(): on_y = lambda v, d: lax.ppermute(v, AXES, Y_ON[d])]
    ppermute x6, starting transfers between devices: 11.4 us -> 6.44 us  [shards(): on_y = lambda v, d: lax.ppermute(v, AXES, Y_ON[d])]
    ppermute x1, starting transfers between devices: 0.09 us -> 2.29 us  [shards(): mine = total_of(mine, lax.ppermute(other, AXES, SWAP))]
    ppermute x6, waiting for transfers between devices: 37.2 us -> 39.4 us  [shards(): on_z = lambda v, d: lax.ppermute(v, AXES, Z_ON[d])]
    ppermute x6, starting transfers between devices: 8.9 us -> 11 us  [shards(): on_z = lambda v, d: lax.ppermute(v, AXES, Z_ON[d])]
  transfers between devices with their start and end apart: 15 -> 15, of which waited for: 7 -> 8; matrix products, arithmetic and copies ran while one was open for 1% -> 1% of each run, Pallas kernels for 14% -> 15%
where the time goes in v4:
time: 144 us; the launch traced here: 143 us
  waiting for transfers between devices  74.3 us (52%)
  starting transfers between devices  30.9 us (21%)
  Pallas kernels  30.5 us (21%)
  local copies, waits for them, and re-layouts  4.42 us (3%)
  other arithmetic  2.22 us (2%)
    ppermute x6, waiting for transfers between devices, shards(): on_z = lambda v, d: lax.ppermute(v, AXES, Z_ON[d])  39.4 us
    all_to_all x1, waiting for transfers between devices, shards(): mine = lax.all_to_all(mine, ('yl', 'x'), 0, 0, tiled=True)  21.1 us
    pallas_call x1, Pallas kernels, first_products(): pl.pallas_call(body, in_specs=[SMALL] + [ANY] * 10, out_specs=[ANY] * 6 +...  14.8 us
    ppermute x6, waiting for transfers between devices, shards(): on_y = lambda v, d: lax.ppermute(v, AXES, Y_ON[d])  13.9 us
    ppermute x6, starting transfers between devices, shards(): on_z = lambda v, d: lax.ppermute(v, AXES, Z_ON[d])  11 us
    pallas_call x2, Pallas kernels, last_products(): pl.pallas_call(body, in_specs=[SMALL] + [ANY] * 7, out_specs=pl.BlockSpec...  9.4 us
    ppermute x6, starting transfers between devices, shards(): on_y = lambda v, d: lax.ppermute(v, AXES, Y_ON[d])  6.44 us
    all_to_all x1, starting transfers between devices, shards(): ints = lax.all_to_all(ints, ('x', 'core'), 0, 0, tiled=True)  5.93 us
  transfers between devices with their start and end apart: 15, of which 8 were waited for; matrix products, arithmetic and copies ran while one was open for 1% of the time, Pallas kernels for 15%

profile of v4, /device:TPU:1, one launch (start us, length us, event | category | flops | bytes accessed | tf_op | source)
XLA Modules:
  0.0 142.5 jit_solution(15658952282789524040)
XLA Ops:
  0.0 1.4 copy-done.7
  1.4 2.6 %shard_map.64 = f32[8,384,128]{2,1,0:T(8,128)} custom-call(s32[1]{0:T(128)} %constant.51.clone.1.unused, f32[384,1024]{1,0:T(8,128)S(1)} %copy-done.7), custom_call_target="tpu_custom_call" | custom-call | bytes 3145728 | tf_op jit(solution)/shard_map/pallas_call | solution.py:36
  4.0 5.9 %all-to-all-start = ((f32[8,384,128]{2,1,0:T(8,128)}), f32[8,384,128]{2,1,0:T(8,128)}, u32[]{:S(2)}, u32[]{:S(2)}) async-start(f32[8,384,128]{2,1,0:T(8,128)} %shard_map.64), calls=%async_computation | async-start | bytes 3145728 | tf_op jit(solution)/shard_map/all_to_all | solution.py:330
  10.0 1.4 %shard_map.65 = (f32[2,128,512]{2,1,0:T(8,128)S(1)}, f32[2,128,512]{2,1,0:T(8,128)S(1)}, f32[2,128,512]{2,1,0:T(8,128)S(1)}, f32[2,128,512]{2,1,0:T(8,128)S(1)}) custom-call(s32[4]{0:T(128)S(1)} %pad_add_fusion.1.target, f32[4,32,8,512]{3,2,1,0:T(8,128)S(1)} %copy-done.2), custom_call_target="tpu_custom_call" | custom-call | bytes 4194304 | tf_op jit(solution)/shard_map/pallas_call | solution.py:36
  11.4 3.8 %collective-permute-start = (f32[2,128,512]{2,1,0:T(8,128)S(1)}, f32[2,128,512]{2,1,0:T(8,128)S(1)}, u32[]{:S(2)}, u32[]{:S(2)}) collective-permute-start(f32[2,128,512]{2,1,0:T(8,128)S(1)} %get-tuple-element.30.refs_3_), channel_id=1, source_target_pairs={{0,32},{1,97},{2,34},{3,99},{4,36},{5,101},{6,38},{7,103},{16,48},... | collective-permute-start | bytes 1572872 | tf_op jit(solution)/shard_map/ppermute | solution.py:327
  15.3 2.7 %collective-permute-start.1 = (f32[2,128,512]{2,1,0:T(8,128)S(1)}, f32[2,128,512]{2,1,0:T(8,128)S(1)}, u32[]{:S(2)}, u32[]{:S(2)}) collective-permute-start(f32[2,128,512]{2,1,0:T(8,128)S(1)} %get-tuple-element.31), channel_id=1, source_target_pairs={{0,16},{1,25},{2,18},{3,27},{4,20},{5,29},{6,22},{7,31},{16,8},{17... | collective-permute-start | bytes 1572872 | tf_op jit(solution)/shard_map/ppermute | solution.py:328
  18.4 0.7 collective-permute-start.4
  19.1 7.4 %collective-permute-done.refs_4_ = f32[2,128,512]{2,1,0:T(8,128)S(1)} collective-permute-done((f32[2,128,512]{2,1,0:T(8,128)S(1)}, f32[2,128,512]{2,1,0:T(8,128)S(1)}, u32[]{:S(2)}, u32[]{:S(2)}) %collective-permute-start) | collective-permute-done | bytes 524320 | tf_op jit(solution)/shard_map/ppermute | solution.py:327
  26.4 3.4 %collective-permute-start.5 = (f32[2,128,512]{2,1,0:T(8,128)S(1)}, f32[2,128,512]{2,1,0:T(8,128)}, u32[]{:S(2)}, u32[]{:S(2)}) collective-permute-start(f32[2,128,512]{2,1,0:T(8,128)S(1)} %collective-permute-done.refs_4_), channel_id=1, source_target_pairs={{0,32},{1,97},{2,34},{3,99},{4,36},{5,101},{6,38},{7,103},{16,48},... | collective-permute-start | bytes 1572872 | tf_op jit(solution)/shard_map/ppermute | solution.py:327
  29.9 8.5 %collective-permute-done.1 = f32[2,128,512]{2,1,0:T(8,128)S(1)} collective-permute-done((f32[2,128,512]{2,1,0:T(8,128)S(1)}, f32[2,128,512]{2,1,0:T(8,128)S(1)}, u32[]{:S(2)}, u32[]{:S(2)}) %collective-permute-start.1) | collective-permute-done | bytes 524320 | tf_op jit(solution)/shard_map/ppermute | solution.py:328
  38.3 3.8 %collective-permute-done.4 = f32[2,128,512]{2,1,0:T(8,128)S(1)} collective-permute-done((f32[2,128,512]{2,1,0:T(8,128)S(1)}, f32[2,128,512]{2,1,0:T(8,128)S(1)}, u32[]{:S(2)}, u32[]{:S(2)}) %collective-permute-start.4) | collective-permute-done | bytes 524320 | tf_op jit(solution)/shard_map/ppermute | solution.py:328
  42.2 0.8 copy-done.12
  43.0 1.2 pad_maximum_fusion.refs_7_
  44.2 1.8 %collective-permute-start.8 = (f32[2,3,128,512]{3,2,1,0:T(8,128)S(1)}, f32[2,3,128,512]{3,2,1,0:T(8,128)}, u32[]{:S(2)}, u32[]{:S(2)}) collective-permute-start(f32[2,3,128,512]{3,2,1,0:T(8,128)S(1)} %pad_maximum_fusion.refs_7_), channel_id=1, source_target_pairs={{0,32},{1,97},{2,34},{3,99},{4,36},{5,101},{6,38},{7,103},{16,48},... | collective-permute-start | bytes 4718600 | tf_op jit(solution)/shard_map/ppermute | solution.py:327
  46.0 1.9 %collective-permute-start.6 = (f32[8,384,128]{2,1,0:T(8,128)}, f32[8,384,128]{2,1,0:T(8,128)S(1)}, u32[]{:S(2)}, u32[]{:S(2)}) collective-permute-start(f32[8,384,128]{2,1,0:T(8,128)} %all-to-all-done.refs_0_), channel_id=1, source_target_pairs={{0,16},{1,25},{2,18},{3,27},{4,20},{5,29},{6,22},{7,31},{16,8},{17... | collective-permute-start | bytes 4718600 | tf_op jit(solution)/shard_map/ppermute | solution.py:328
  47.9 0.7 pad_add_fusion.at
  48.6 30.3 %collective-permute-done.8.refs_8_ = f32[2,3,128,512]{3,2,1,0:T(8,128)} collective-permute-done((f32[2,3,128,512]{3,2,1,0:T(8,128)S(1)}, f32[2,3,128,512]{3,2,1,0:T(8,128)}, u32[]{:S(2)}, u32[]{:S(2)}) %collective-permute-start.8) | collective-permute-done | bytes 1572896 | tf_op jit(solution)/shard_map/ppermute | solution.py:327
  78.9 1.9 %collective-permute-start.10 = (f32[2,3,128,512]{3,2,1,0:T(8,128)}, f32[2,3,128,512]{3,2,1,0:T(8,128)S(1)}, u32[]{:S(2)}, u32[]{:S(2)}) collective-permute-start(f32[2,3,128,512]{3,2,1,0:T(8,128)} %collective-permute-done.8.refs_8_), channel_id=1, source_target_pairs={{0,32},{1,97},{2,34},{3,99},{4,36},{5,101},{6,38},{7,103},{16,48},... | collective-permute-start | bytes 4718600 | tf_op jit(solution)/shard_map/ppermute | solution.py:327
  80.9 0.8 collective-permute-start.11
  81.7 1.7 %collective-permute-done.9.refs_9_ = f32[2,3,128,512]{3,2,1,0:T(8,128)} collective-permute-done((f32[2,3,128,512]{3,2,1,0:T(8,128)S(1)}, f32[2,3,128,512]{3,2,1,0:T(8,128)}, u32[]{:S(2)}, u32[]{:S(2)}) %collective-permute-start.9) | collective-permute-done | bytes 1572896 | tf_op jit(solution)/shard_map/ppermute | solution.py:327
  83.6 14.8 %shard_map.66 = (bf16[2,384,512]{2,1,0:T(8,128)(2,1)}, bf16[2,384,512]{2,1,0:T(8,128)(2,1)}, bf16[2,2,4,128,512]{4,3,2,1,0:T(8,128)(2,1)}, bf16[2,2,4,128,512]{4...) custom-call(s32[3]{0:T(128)} %pad_add_fusion.at, ...), custom_call_target="tpu_custom_call" | custom-call | flops 7247757312 | bytes 25165824 | tf_op jit(solution)/shard_map/pallas_call | solution.py:190
  98.5 0.7 copy-done.10
  99.2 1.2 collective-permute-done.11.src_far
  100.5 0.7 copy-done.4
  101.2 0.4 copy-done.6
  101.7 4.7 %shard_map.69 = f32[8,384,128]{2,1,0:T(8,128)S(1)} custom-call(s32[4]{0:T(128)S(1)} %add_add_fusion.1.at, f32[2,384,512]{2,1,0:T(8,128)S(1)} %copy-done.6, f32[8,384,128]{2,1,0:T(8,128)S(1)} %collective-permute-done.11.src_far, f32[2,3,128,512]{3,2,1,0:T(8,128)S(1)} %collective-permute-done.10.src_near, bf16[2,384,512]{2,1,0:T(8,128)(2,1)S(1)} %copy-done, ...), custom_call_target="tpu_custom_call" | custom-call | flops 2415919104 | bytes 8388608 | tf_op jit(solution)/shard_map/pallas_call | solution.py:254
  106.4 2.3 %collective-permute-start.12 = (f32[8,384,128]{2,1,0:T(8,128)S(1)}, f32[8,384,128]{2,1,0:T(8,128)S(1)}, u32[]{:S(2)}, u32[]{:S(2)}) collective-permute-start(f32[8,384,128]{2,1,0:T(8,128)S(1)} %shard_map.69), channel_id=1, source_target_pairs={{0,1},{1,0},{2,3},{3,2},{4,5},{5,4},{6,7},{7,6},{16,17},{17,16},{1... | collective-permute-start | bytes 4718600 | tf_op jit(solution)/shard_map/ppermute | solution.py:346
  108.8 4.7 %shard_map.68.a = f32[8,384,128]{2,1,0:T(8,128)S(1)} custom-call(s32[4]{0:T(128)S(1)} %add_add_fusion.at, f32[2,384,512]{2,1,0:T(8,128)S(1)} %copy-done.5, f32[8,384,128]{2,1,0:T(8,128)S(1)} %collective-permute-done.11.src_far, f32[2,3,128,512]{3,2,1,0:T(8,128)S(1)} %collective-permute-done.10.src_near, bf16[2,384,512]{2,1,0:T(8,128)(2,1)S(1)} %copy-done, ...), custom_call_target="tpu_custom_call" | custom-call | flops 2415919104 | bytes 8388608 | tf_op jit(solution)/shard_map/pallas_call | solution.py:254
  113.5 1.3 shard_map.70
  114.8 5.2 %all-to-all-start.1 = ((f32[8,384,128]{2,1,0:T(8,128)}), f32[8,384,128]{2,1,0:T(8,128)S(1)}, u32[]{:S(2)}, u32[]{:S(2)}) async-start(f32[8,384,128]{2,1,0:T(8,128)} %shard_map.70), calls=%async_computation.1 | async-start | bytes 3145728 | tf_op jit(solution)/shard_map/all_to_all | solution.py:347
  120.5 21.1 %all-to-all-done.1.part = f32[8,384,128]{2,1,0:T(8,128)S(1)} async-done(((f32[8,384,128]{2,1,0:T(8,128)}), f32[8,384,128]{2,1,0:T(8,128)S(1)}, u32[]{:S(2)}, u32[]{:S(2)}) %all-to-all-start.1) | async-done | bytes 1572896 | tf_op jit(solution)/shard_map/all_to_all | solution.py:347
  141.6 0.9 shard_map.71
  (56 shorter events, 1.5 us)
Async XLA Ops:
  0.0 1.4 copy-start.7
  4.0 6.0 %copy-start.2 = (f32[4,32,8,512]{3,2,1,0:T(8,128)S(1)}, f32[4,32,8,512]{3,2,1,0:T(8,128)}, u32[]{:S(2)}) copy-start(f32[4,32,8,512]{3,2,1,0:T(8,128)} %src.2) | copy-start | bytes 6291460
  4.0 38.2 %all-to-all-start = ((f32[8,384,128]{2,1,0:T(8,128)}), f32[8,384,128]{2,1,0:T(8,128)}, u32[]{:S(2)}, u32[]{:S(2)}) async-start(f32[8,384,128]{2,1,0:T(8,128)} %shard_map.64), calls=%async_computation | async-start | bytes 3145728 | tf_op jit(solution)/shard_map/all_to_all | solution.py:330
  11.4 32.7 %copy-start.9 = (f32[2,128,512]{2,1,0:T(8,128)}, f32[2,128,512]{2,1,0:T(8,128)S(1)}, u32[]{:S(2)}) copy-start(f32[2,128,512]{2,1,0:T(8,128)S(1)} %get-tuple-element.30.refs_3_) | copy-start | bytes 1572868
  11.4 15.0 %collective-permute-start = (f32[2,128,512]{2,1,0:T(8,128)S(1)}, f32[2,128,512]{2,1,0:T(8,128)S(1)}, u32[]{:S(2)}, u32[]{:S(2)}) collective-permute-start(f32[2,128,512]{2,1,0:T(8,128)S(1)} %get-tuple-element.30.refs_3_), channel_id=1, source_target_pairs={{0,32},{1,97},{2,34},{3,99},{4,36},{5,101},{6,38},{7,103},{16,48},... | collective-permute-start | bytes 1572872 | tf_op jit(solution)/shard_map/ppermute | solution.py:327
  15.3 23.1 %collective-permute-start.2 = (f32[2,128,512]{2,1,0:T(8,128)S(1)}, f32[2,128,512]{2,1,0:T(8,128)S(1)}, u32[]{:S(2)}, u32[]{:S(2)}) collective-permute-start(f32[2,128,512]{2,1,0:T(8,128)S(1)} %get-tuple-element.30.refs_3_), channel_id=1, source_target_pairs={{0,96},{1,33},{2,98},{3,35},{4,100},{5,37},{6,102},{7,39},{16,112}... | collective-permute-start | bytes 1572872 | tf_op jit(solution)/shard_map/ppermute | solution.py:327
  15.3 23.1 %collective-permute-start.1 = (f32[2,128,512]{2,1,0:T(8,128)S(1)}, f32[2,128,512]{2,1,0:T(8,128)S(1)}, u32[]{:S(2)}, u32[]{:S(2)}) collective-permute-start(f32[2,128,512]{2,1,0:T(8,128)S(1)} %get-tuple-element.31), channel_id=1, source_target_pairs={{0,16},{1,25},{2,18},{3,27},{4,20},{5,29},{6,22},{7,31},{16,8},{17... | collective-permute-start | bytes 1572872 | tf_op jit(solution)/shard_map/ppermute | solution.py:328
  18.0 20.3 %collective-permute-start.3 = (f32[2,128,512]{2,1,0:T(8,128)S(1)}, f32[2,128,512]{2,1,0:T(8,128)S(1)}, u32[]{:S(2)}, u32[]{:S(2)}) collective-permute-start(f32[2,128,512]{2,1,0:T(8,128)S(1)} %get-tuple-element.32), channel_id=1, source_target_pairs={{0,8},{1,9},{2,10},{3,11},{4,12},{5,13},{6,14},{7,15},{16,24},{17,... | collective-permute-start | bytes 1572872 | tf_op jit(solution)/shard_map/ppermute | solution.py:328
  18.4 23.8 %collective-permute-start.4 = (f32[2,128,512]{2,1,0:T(8,128)S(1)}, f32[2,128,512]{2,1,0:T(8,128)S(1)}, u32[]{:S(2)}, u32[]{:S(2)}) collective-permute-start(f32[2,128,512]{2,1,0:T(8,128)S(1)} %get-tuple-element.33), channel_id=1, source_target_pairs={{0,24},{1,17},{2,26},{3,19},{4,28},{5,21},{6,30},{7,23},{16,0},{17... | collective-permute-start | bytes 1572872 | tf_op jit(solution)/shard_map/ppermute | solution.py:328
  26.4 15.7 %copy-start.17 = (f32[2,128,512]{2,1,0:T(8,128)}, f32[2,128,512]{2,1,0:T(8,128)S(1)}, u32[]{:S(2)}) copy-start(f32[2,128,512]{2,1,0:T(8,128)S(1)} %collective-permute-done.refs_4_) | copy-start | bytes 1572868
  26.4 15.7 %collective-permute-start.5 = (f32[2,128,512]{2,1,0:T(8,128)S(1)}, f32[2,128,512]{2,1,0:T(8,128)}, u32[]{:S(2)}, u32[]{:S(2)}) collective-permute-start(f32[2,128,512]{2,1,0:T(8,128)S(1)} %collective-permute-done.refs_4_), channel_id=1, source_target_pairs={{0,32},{1,97},{2,34},{3,99},{4,36},{5,101},{6,38},{7,103},{16,48},... | collective-permute-start | bytes 1572872 | tf_op jit(solution)/shard_map/ppermute | solution.py:327
  38.3 3.9 %copy-start.18 = (f32[2,128,512]{2,1,0:T(8,128)}, f32[2,128,512]{2,1,0:T(8,128)S(1)}, u32[]{:S(2)}) copy-start(f32[2,128,512]{2,1,0:T(8,128)S(1)} %collective-permute-done.2.refs_6_) | copy-start | bytes 1572868
  44.2 39.4 %copy-start.11 = (f32[2,3,128,512]{3,2,1,0:T(8,128)}, f32[2,3,128,512]{3,2,1,0:T(8,128)S(1)}, u32[]{:S(2)}) copy-start(f32[2,3,128,512]{3,2,1,0:T(8,128)S(1)} %pad_maximum_fusion.refs_7_) | copy-start | bytes 4718596
  44.2 34.7 %collective-permute-start.8 = (f32[2,3,128,512]{3,2,1,0:T(8,128)S(1)}, f32[2,3,128,512]{3,2,1,0:T(8,128)}, u32[]{:S(2)}, u32[]{:S(2)}) collective-permute-start(f32[2,3,128,512]{3,2,1,0:T(8,128)S(1)} %pad_maximum_fusion.refs_7_), channel_id=1, source_target_pairs={{0,32},{1,97},{2,34},{3,99},{4,36},{5,101},{6,38},{7,103},{16,48},... | collective-permute-start | bytes 4718600 | tf_op jit(solution)/shard_map/ppermute | solution.py:327
  46.0 34.8 %collective-permute-start.6 = (f32[8,384,128]{2,1,0:T(8,128)}, f32[8,384,128]{2,1,0:T(8,128)S(1)}, u32[]{:S(2)}, u32[]{:S(2)}) collective-permute-start(f32[8,384,128]{2,1,0:T(8,128)} %all-to-all-done.refs_0_), channel_id=1, source_target_pairs={{0,16},{1,25},{2,18},{3,27},{4,20},{5,29},{6,22},{7,31},{16,8},{17... | collective-permute-start | bytes 4718600 | tf_op jit(solution)/shard_map/ppermute | solution.py:328
  47.9 35.4 %collective-permute-start.9 = (f32[2,3,128,512]{3,2,1,0:T(8,128)S(1)}, f32[2,3,128,512]{3,2,1,0:T(8,128)}, u32[]{:S(2)}, u32[]{:S(2)}) collective-permute-start(f32[2,3,128,512]{3,2,1,0:T(8,128)S(1)} %pad_maximum_fusion.refs_7_), channel_id=1, source_target_pairs={{0,96},{1,33},{2,98},{3,35},{4,100},{5,37},{6,102},{7,39},{16,112}... | collective-permute-start | bytes 4718600 | tf_op jit(solution)/shard_map/ppermute | solution.py:327
  47.9 35.7 %collective-permute-start.7 = (f32[8,384,128]{2,1,0:T(8,128)}, f32[8,384,128]{2,1,0:T(8,128)}, u32[]{:S(2)}, u32[]{:S(2)}) collective-permute-start(f32[8,384,128]{2,1,0:T(8,128)} %all-to-all-done.refs_0_), channel_id=1, source_target_pairs={{0,24},{1,17},{2,26},{3,19},{4,28},{5,21},{6,30},{7,23},{16,0},{17... | collective-permute-start | bytes 4718600 | tf_op jit(solution)/shard_map/ppermute | solution.py:328
  78.9 20.2 %collective-permute-start.10 = (f32[2,3,128,512]{3,2,1,0:T(8,128)}, f32[2,3,128,512]{3,2,1,0:T(8,128)S(1)}, u32[]{:S(2)}, u32[]{:S(2)}) collective-permute-start(f32[2,3,128,512]{3,2,1,0:T(8,128)} %collective-permute-done.8.refs_8_), channel_id=1, source_target_pairs={{0,32},{1,97},{2,34},{3,99},{4,36},{5,101},{6,38},{7,103},{16,48},... | collective-permute-start | bytes 4718600 | tf_op jit(solution)/shard_map/ppermute | solution.py:327
  80.9 2.8 %copy-start.16 = (f32[8,384,128]{2,1,0:T(8,128)}, f32[8,384,128]{2,1,0:T(8,128)S(1)}, u32[]{:S(2)}) copy-start(f32[8,384,128]{2,1,0:T(8,128)S(1)} %collective-permute-done.6.refs_1_) | copy-start | bytes 4718596
  80.9 19.6 %collective-permute-start.11 = (f32[8,384,128]{2,1,0:T(8,128)S(1)}, f32[8,384,128]{2,1,0:T(8,128)S(1)}, u32[]{:S(2)}, u32[]{:S(2)}) collective-permute-start(f32[8,384,128]{2,1,0:T(8,128)S(1)} %collective-permute-done.6.refs_1_), channel_id=1, source_target_pairs={{0,16},{1,25},{2,18},{3,27},{4,20},{5,29},{6,22},{7,31},{16,8},{17... | collective-permute-start | bytes 4718600 | tf_op jit(solution)/shard_map/ppermute | solution.py:328
  99.1 1.3 copy-start
  99.1 1.4 copy-start.1
  99.1 2.1 %copy-start.4 = (bf16[2,2,4,128,512]{4,3,2,1,0:T(8,128)(2,1)S(1)}, bf16[2,2,4,128,512]{4,3,2,1,0:T(8,128)(2,1)}, u32[]{:S(2)}) copy-start(bf16[2,2,4,128,512]{4,3,2,1,0:T(8,128)(2,1)} %get-tuple-element.50.src_b) | copy-start | bytes 6291460
  99.1 2.5 %copy-start.6 = (f32[2,384,512]{2,1,0:T(8,128)S(1)}, f32[2,384,512]{2,1,0:T(8,128)}, u32[]{:S(2)}) copy-start(f32[2,384,512]{2,1,0:T(8,128)} %get-tuple-element.49.src_sum) | copy-start | bytes 4718596
  101.7 7.1 %copy-start.3 = (bf16[2,2,4,128,512]{4,3,2,1,0:T(8,128)(2,1)S(1)}, bf16[2,2,4,128,512]{4,3,2,1,0:T(8,128)(2,1)}, u32[]{:S(2)}) copy-start(bf16[2,2,4,128,512]{4,3,2,1,0:T(8,128)(2,1)} %get-tuple-element.47.src_b) | copy-start | bytes 6291460
  101.7 7.1 %copy-start.5 = (f32[2,384,512]{2,1,0:T(8,128)S(1)}, f32[2,384,512]{2,1,0:T(8,128)}, u32[]{:S(2)}) copy-start(f32[2,384,512]{2,1,0:T(8,128)} %get-tuple-element.41.src_sum) | copy-start | bytes 4718596
  106.4 7.1 %collective-permute-start.12 = (f32[8,384,128]{2,1,0:T(8,128)S(1)}, f32[8,384,128]{2,1,0:T(8,128)S(1)}, u32[]{:S(2)}, u32[]{:S(2)}) collective-permute-start(f32[8,384,128]{2,1,0:T(8,128)S(1)} %shard_map.69), channel_id=1, source_target_pairs={{0,1},{1,0},{2,3},{3,2},{4,5},{5,4},{6,7},{7,6},{16,17},{17,16},{1... | collective-permute-start | bytes 4718600 | tf_op jit(solution)/shard_map/ppermute | solution.py:346
  114.8 5.2 %copy-start.13 = (f32[512]{0:T(512)S(1)}, f32[512]{0:T(512)}, u32[]{:S(2)}) copy-start(f32[512]{0:T(512)} %param.11) | copy-start | bytes 6148
  114.8 5.2 %copy-start.14 = (f32[8]{0:T(128)S(1)}, f32[8]{0:T(128)}, u32[]{:S(2)}) copy-start(f32[8]{0:T(128)} %param.10) | copy-start | bytes 100
  114.8 5.3 %copy-start.15 = (f32[6]{0:T(128)S(1)}, f32[6]{0:T(128)}, u32[]{:S(2)}) copy-start(f32[6]{0:T(128)} %param.9) | copy-start | bytes 76
  114.8 26.8 %copy-start.8 = (f32[384,256]{1,0:T(8,128)S(1)}, f32[384,256]{1,0:T(8,128)}, u32[]{:S(2)}) copy-start(f32[384,256]{1,0:T(8,128)} %given.1) | copy-start | bytes 1179652
  114.8 26.7 %all-to-all-start.1 = ((f32[8,384,128]{2,1,0:T(8,128)}), f32[8,384,128]{2,1,0:T(8,128)S(1)}, u32[]{:S(2)}, u32[]{:S(2)}) async-start(f32[8,384,128]{2,1,0:T(8,128)} %shard_map.70), calls=%async_computation.1 | async-start | bytes 3145728 | tf_op jit(solution)/shard_map/all_to_all | solution.py:347
  (2 other events, 1.5 us)

commit v5 on v4

--- a/solution.py
+++ b/solution.py
@@ -329,9 +329,10 @@
     wave = lambda *v: list(lax.optimization_barrier(v))
     ints = lax.all_to_all(ints, ("x", "core"), 0, 0, tiled=True)
     b, d, c = on_y(parts[1], 1), on_y(parts[2], 2), on_y(parts[3], 3)
-    own1, own3 = on_z(parts[0], 1), on_z(parts[0], 3)
+    own1 = on_z(parts[0], 1)
+    own3 = on_z(wave(parts[0], own1)[0], 3)
     own2 = on_z(own1, 1)
-    ints, own1, b, own3, d, c, own2 = wave(ints, own1, b, own3, d, c, own2)
+    ints, b, own1, d, own3, c, own2 = wave(ints, b, own1, d, own3, c, own2)
     own = [parts[0], own1, own2, own3]
     bcd = jnp.stack([b, c, d], axis=1)
     bcd1, bcd3 = on_z(bcd, 1), on_z(bcd, 3)

time: 144 us -> 143 us (level)
  waiting for transfers between devices: 74.3 us -> 70.1 us
  starting transfers between devices: 30.9 us -> 33.9 us
    ppermute x6, waiting for transfers between devices: 39.4 us -> 31.5 us  [shards(): on_z = lambda v, d: lax.ppermute(v, AXES, Z_ON[d])]
    ppermute x6, waiting for transfers between devices: 13.9 us -> 17.5 us  [shards(): on_y = lambda v, d: lax.ppermute(v, AXES, Y_ON[d])]
    ppermute x6, starting transfers between devices: 11 us -> 13.9 us  [shards(): on_z = lambda v, d: lax.ppermute(v, AXES, Z_ON[d])]
  transfers between devices with their start and end apart: 15 -> 15, of which waited for: 8 -> 7; matrix products, arithmetic and copies ran while one was open for 1% -> 1% of each run, Pallas kernels for 15% -> 15%
where the time goes in v5:
time: 143 us
  waiting for transfers between devices  70.1 us (49%)
  starting transfers between devices  33.9 us (24%)
  Pallas kernels  30.5 us (21%)
  local copies, waits for them, and re-layouts  5.85 us (4%)
  other arithmetic  2.22 us (2%)
    ppermute x6, waiting for transfers between devices, shards(): on_z = lambda v, d: lax.ppermute(v, AXES, Z_ON[d])  31.5 us
    all_to_all x1, waiting for transfers between devices, shards(): mine = lax.all_to_all(mine, ('yl', 'x'), 0, 0, tiled=True)  21.1 us
    ppermute x6, waiting for transfers between devices, shards(): on_y = lambda v, d: lax.ppermute(v, AXES, Y_ON[d])  17.5 us
    pallas_call x1, Pallas kernels, first_products(): pl.pallas_call(body, in_specs=[SMALL] + [ANY] * 10, out_specs=[ANY] * 6 +...  14.8 us
    ppermute x6, starting transfers between devices, shards(): on_z = lambda v, d: lax.ppermute(v, AXES, Z_ON[d])  13.9 us
    pallas_call x2, Pallas kernels, last_products(): pl.pallas_call(body, in_specs=[SMALL] + [ANY] * 7, out_specs=pl.BlockSpec...  9.4 us
    ppermute x6, starting transfers between devices, shards(): on_y = lambda v, d: lax.ppermute(v, AXES, Y_ON[d])  6.37 us
    all_to_all x1, starting transfers between devices, shards(): ints = lax.all_to_all(ints, ('x', 'core'), 0, 0, tiled=True)  5.93 us
  transfers between devices with their start and end apart: 15, of which 7 were waited for; matrix products, arithmetic and copies ran while one was open for 1% of the time, Pallas kernels for 15%

profile of v5, /device:TPU:1, one launch (start us, length us, event | category | flops | bytes accessed | tf_op | source)
XLA Modules:
  0.0 142.8 jit_solution(5927920264179793811)
XLA Ops:
  0.0 1.4 copy-done.7
  1.4 2.6 %shard_map.64 = f32[8,384,128]{2,1,0:T(8,128)} custom-call(s32[1]{0:T(128)} %constant.51.clone.1.unused, f32[384,1024]{1,0:T(8,128)S(1)} %copy-done.7), custom_call_target="tpu_custom_call" | custom-call | bytes 3145728 | tf_op jit(solution)/shard_map/pallas_call | solution.py:36
  4.0 5.9 %all-to-all-start = ((f32[8,384,128]{2,1,0:T(8,128)}), f32[8,384,128]{2,1,0:T(8,128)}, u32[]{:S(2)}, u32[]{:S(2)}) async-start(f32[8,384,128]{2,1,0:T(8,128)} %shard_map.64), calls=%async_computation | async-start | bytes 3145728 | tf_op jit(solution)/shard_map/all_to_all | solution.py:330
  10.0 1.4 %shard_map.65 = (f32[2,128,512]{2,1,0:T(8,128)S(1)}, f32[2,128,512]{2,1,0:T(8,128)S(1)}, f32[2,128,512]{2,1,0:T(8,128)S(1)}, f32[2,128,512]{2,1,0:T(8,128)S(1)}) custom-call(s32[4]{0:T(128)S(1)} %pad_add_fusion.1.target, f32[4,32,8,512]{3,2,1,0:T(8,128)S(1)} %copy-done.2), custom_call_target="tpu_custom_call" | custom-call | bytes 4194304 | tf_op jit(solution)/shard_map/pallas_call | solution.py:36
  11.4 3.8 %collective-permute-start.1 = (f32[2,128,512]{2,1,0:T(8,128)S(1)}, f32[2,128,512]{2,1,0:T(8,128)S(1)}, u32[]{:S(2)}, u32[]{:S(2)}) collective-permute-start(f32[2,128,512]{2,1,0:T(8,128)S(1)} %get-tuple-element.34.refs_3_), channel_id=1, source_target_pairs={{0,32},{1,97},{2,34},{3,99},{4,36},{5,101},{6,38},{7,103},{16,48},... | collective-permute-start | bytes 1572872 | tf_op jit(solution)/shard_map/ppermute | solution.py:327
  15.3 2.7 %collective-permute-start = (f32[2,128,512]{2,1,0:T(8,128)S(1)}, f32[2,128,512]{2,1,0:T(8,128)S(1)}, u32[]{:S(2)}, u32[]{:S(2)}) collective-permute-start(f32[2,128,512]{2,1,0:T(8,128)S(1)} %get-tuple-element.31), channel_id=1, source_target_pairs={{0,16},{1,25},{2,18},{3,27},{4,20},{5,29},{6,22},{7,31},{16,8},{17... | collective-permute-start | bytes 1572872 | tf_op jit(solution)/shard_map/ppermute | solution.py:328
  18.4 0.7 collective-permute-start.4
  19.0 2.3 %collective-permute-done.1.refs_4_ = f32[2,128,512]{2,1,0:T(8,128)S(1)} collective-permute-done((f32[2,128,512]{2,1,0:T(8,128)S(1)}, f32[2,128,512]{2,1,0:T(8,128)S(1)}, u32[]{:S(2)}, u32[]{:S(2)}) %collective-permute-start.1) | collective-permute-done | bytes 524320 | tf_op jit(solution)/shard_map/ppermute | solution.py:327
  21.8 3.2 %collective-permute-start.5 = (f32[2,128,512]{2,1,0:T(8,128)S(1)}, f32[2,128,512]{2,1,0:T(8,128)}, u32[]{:S(2)}, u32[]{:S(2)}) collective-permute-start(f32[2,128,512]{2,1,0:T(8,128)S(1)} %collective-permute-done.1.refs_4_), channel_id=1, source_target_pairs={{0,32},{1,97},{2,34},{3,99},{4,36},{5,101},{6,38},{7,103},{16,48},... | collective-permute-start | bytes 1572872 | tf_op jit(solution)/shard_map/ppermute | solution.py:327
  24.9 14.7 %collective-permute-done = f32[2,128,512]{2,1,0:T(8,128)S(1)} collective-permute-done((f32[2,128,512]{2,1,0:T(8,128)S(1)}, f32[2,128,512]{2,1,0:T(8,128)S(1)}, u32[]{:S(2)}, u32[]{:S(2)}) %collective-permute-start) | collective-permute-done | bytes 524320 | tf_op jit(solution)/shard_map/ppermute | solution.py:328
  40.1 0.8 copy-done.12
  41.1 1.2 pad_maximum_fusion.refs_7_
  42.3 2.3 %collective-permute-start.8 = (f32[2,3,128,512]{3,2,1,0:T(8,128)S(1)}, f32[2,3,128,512]{3,2,1,0:T(8,128)}, u32[]{:S(2)}, u32[]{:S(2)}) collective-permute-start(f32[2,3,128,512]{3,2,1,0:T(8,128)S(1)} %pad_maximum_fusion.refs_7_), channel_id=1, source_target_pairs={{0,32},{1,97},{2,34},{3,99},{4,36},{5,101},{6,38},{7,103},{16,48},... | collective-permute-start | bytes 4718600 | tf_op jit(solution)/shard_map/ppermute | solution.py:327
  44.5 1.6 %collective-permute-start.6 = (f32[8,384,128]{2,1,0:T(8,128)}, f32[8,384,128]{2,1,0:T(8,128)S(1)}, u32[]{:S(2)}, u32[]{:S(2)}) collective-permute-start(f32[8,384,128]{2,1,0:T(8,128)} %all-to-all-done.refs_0_), channel_id=1, source_target_pairs={{0,16},{1,25},{2,18},{3,27},{4,20},{5,29},{6,22},{7,31},{16,8},{17... | collective-permute-start | bytes 4718600 | tf_op jit(solution)/shard_map/ppermute | solution.py:328
  46.1 0.8 collective-permute-start.9
  46.9 0.7 pad_add_fusion.at
  47.7 27.7 %collective-permute-done.8.refs_8_ = f32[2,3,128,512]{3,2,1,0:T(8,128)} collective-permute-done((f32[2,3,128,512]{3,2,1,0:T(8,128)S(1)}, f32[2,3,128,512]{3,2,1,0:T(8,128)}, u32[]{:S(2)}, u32[]{:S(2)}) %collective-permute-start.8) | collective-permute-done | bytes 1572896 | tf_op jit(solution)/shard_map/ppermute | solution.py:327
  75.4 3.5 %collective-permute-start.10 = (f32[2,3,128,512]{3,2,1,0:T(8,128)}, f32[2,3,128,512]{3,2,1,0:T(8,128)S(1)}, u32[]{:S(2)}, u32[]{:S(2)}) collective-permute-start(f32[2,3,128,512]{3,2,1,0:T(8,128)} %collective-permute-done.8.refs_8_), channel_id=1, source_target_pairs={{0,32},{1,97},{2,34},{3,99},{4,36},{5,101},{6,38},{7,103},{16,48},... | collective-permute-start | bytes 4718600 | tf_op jit(solution)/shard_map/ppermute | solution.py:327
  78.9 1.0 collective-permute-start.11
  79.9 1.5 %collective-permute-done.9.refs_9_ = f32[2,3,128,512]{3,2,1,0:T(8,128)} collective-permute-done((f32[2,3,128,512]{3,2,1,0:T(8,128)S(1)}, f32[2,3,128,512]{3,2,1,0:T(8,128)}, u32[]{:S(2)}, u32[]{:S(2)}) %collective-permute-start.9) | collective-permute-done | bytes 1572896 | tf_op jit(solution)/shard_map/ppermute | solution.py:327
  81.3 2.4 %collective-permute-done.7.refs_2_ = f32[8,384,128]{2,1,0:T(8,128)} collective-permute-done((f32[8,384,128]{2,1,0:T(8,128)}, f32[8,384,128]{2,1,0:T(8,128)}, u32[]{:S(2)}, u32[]{:S(2)}) %collective-permute-start.7) | collective-permute-done | bytes 1572896 | tf_op jit(solution)/shard_map/ppermute | solution.py:328
  83.7 14.8 %shard_map.66 = (bf16[2,384,512]{2,1,0:T(8,128)(2,1)}, bf16[2,384,512]{2,1,0:T(8,128)(2,1)}, bf16[2,2,4,128,512]{4,3,2,1,0:T(8,128)(2,1)}, bf16[2,2,4,128,512]{4...) custom-call(s32[3]{0:T(128)} %pad_add_fusion.at, ...), custom_call_target="tpu_custom_call" | custom-call | flops 7247757312 | bytes 25165824 | tf_op jit(solution)/shard_map/pallas_call | solution.py:190
  98.6 0.7 copy-done.10
  99.3 1.1 copy-done
  100.6 0.7 copy-done.4
  101.8 4.7 %shard_map.69 = f32[8,384,128]{2,1,0:T(8,128)S(1)} custom-call(s32[4]{0:T(128)S(1)} %add_add_fusion.1.at, f32[2,384,512]{2,1,0:T(8,128)S(1)} %copy-done.6, f32[8,384,128]{2,1,0:T(8,128)S(1)} %collective-permute-done.11.src_far, f32[2,3,128,512]{3,2,1,0:T(8,128)S(1)} %collective-permute-done.10.src_near, bf16[2,384,512]{2,1,0:T(8,128)(2,1)S(1)} %copy-done, ...), custom_call_target="tpu_custom_call" | custom-call | flops 2415919104 | bytes 8388608 | tf_op jit(solution)/shard_map/pallas_call | solution.py:254
  106.5 3.5 %collective-permute-start.12 = (f32[8,384,128]{2,1,0:T(8,128)S(1)}, f32[8,384,128]{2,1,0:T(8,128)S(1)}, u32[]{:S(2)}, u32[]{:S(2)}) collective-permute-start(f32[8,384,128]{2,1,0:T(8,128)S(1)} %shard_map.69), channel_id=1, source_target_pairs={{0,1},{1,0},{2,3},{3,2},{4,5},{5,4},{6,7},{7,6},{16,17},{17,16},{1... | collective-permute-start | bytes 4718600 | tf_op jit(solution)/shard_map/ppermute | solution.py:347
  110.0 4.7 %shard_map.68.a = f32[8,384,128]{2,1,0:T(8,128)S(1)} custom-call(s32[4]{0:T(128)S(1)} %add_add_fusion.at, f32[2,384,512]{2,1,0:T(8,128)S(1)} %copy-done.5, f32[8,384,128]{2,1,0:T(8,128)S(1)} %collective-permute-done.11.src_far, f32[2,3,128,512]{3,2,1,0:T(8,128)S(1)} %collective-permute-done.10.src_near, bf16[2,384,512]{2,1,0:T(8,128)(2,1)S(1)} %copy-done, ...), custom_call_target="tpu_custom_call" | custom-call | flops 2415919104 | bytes 8388608 | tf_op jit(solution)/shard_map/pallas_call | solution.py:254
  114.8 1.3 shard_map.70
  116.1 4.3 %all-to-all-start.1 = ((f32[8,384,128]{2,1,0:T(8,128)}), f32[8,384,128]{2,1,0:T(8,128)S(1)}, u32[]{:S(2)}, u32[]{:S(2)}) async-start(f32[8,384,128]{2,1,0:T(8,128)} %shard_map.70), calls=%async_computation.1 | async-start | bytes 3145728 | tf_op jit(solution)/shard_map/all_to_all | solution.py:348
  120.8 21.1 %all-to-all-done.1.part = f32[8,384,128]{2,1,0:T(8,128)S(1)} async-done(((f32[8,384,128]{2,1,0:T(8,128)}), f32[8,384,128]{2,1,0:T(8,128)S(1)}, u32[]{:S(2)}, u32[]{:S(2)}) %all-to-all-start.1) | async-done | bytes 1572896 | tf_op jit(solution)/shard_map/all_to_all | solution.py:348
  141.9 0.9 shard_map.71
  (56 shorter events, 2.8 us)
Async XLA Ops:
  0.0 1.4 copy-start.7
  4.0 6.0 %copy-start.2 = (f32[4,32,8,512]{3,2,1,0:T(8,128)S(1)}, f32[4,32,8,512]{3,2,1,0:T(8,128)}, u32[]{:S(2)}) copy-start(f32[4,32,8,512]{3,2,1,0:T(8,128)} %src.2) | copy-start | bytes 6291460
  4.0 36.1 %all-to-all-start = ((f32[8,384,128]{2,1,0:T(8,128)}), f32[8,384,128]{2,1,0:T(8,128)}, u32[]{:S(2)}, u32[]{:S(2)}) async-start(f32[8,384,128]{2,1,0:T(8,128)} %shard_map.64), calls=%async_computation | async-start | bytes 3145728 | tf_op jit(solution)/shard_map/all_to_all | solution.py:330
  11.4 30.8 %copy-start.9 = (f32[2,128,512]{2,1,0:T(8,128)}, f32[2,128,512]{2,1,0:T(8,128)S(1)}, u32[]{:S(2)}) copy-start(f32[2,128,512]{2,1,0:T(8,128)S(1)} %get-tuple-element.34.refs_3_) | copy-start | bytes 1572868
  11.4 10.0 %collective-permute-start.1 = (f32[2,128,512]{2,1,0:T(8,128)S(1)}, f32[2,128,512]{2,1,0:T(8,128)S(1)}, u32[]{:S(2)}, u32[]{:S(2)}) collective-permute-start(f32[2,128,512]{2,1,0:T(8,128)S(1)} %get-tuple-element.34.refs_3_), channel_id=1, source_target_pairs={{0,32},{1,97},{2,34},{3,99},{4,36},{5,101},{6,38},{7,103},{16,48},... | collective-permute-start | bytes 1572872 | tf_op jit(solution)/shard_map/ppermute | solution.py:327
  15.3 24.3 %collective-permute-start = (f32[2,128,512]{2,1,0:T(8,128)S(1)}, f32[2,128,512]{2,1,0:T(8,128)S(1)}, u32[]{:S(2)}, u32[]{:S(2)}) collective-permute-start(f32[2,128,512]{2,1,0:T(8,128)S(1)} %get-tuple-element.31), channel_id=1, source_target_pairs={{0,16},{1,25},{2,18},{3,27},{4,20},{5,29},{6,22},{7,31},{16,8},{17... | collective-permute-start | bytes 1572872 | tf_op jit(solution)/shard_map/ppermute | solution.py:328
  18.0 21.6 %collective-permute-start.2 = (f32[2,128,512]{2,1,0:T(8,128)S(1)}, f32[2,128,512]{2,1,0:T(8,128)S(1)}, u32[]{:S(2)}, u32[]{:S(2)}) collective-permute-start(f32[2,128,512]{2,1,0:T(8,128)S(1)} %get-tuple-element.33), channel_id=1, source_target_pairs={{0,8},{1,9},{2,10},{3,11},{4,12},{5,13},{6,14},{7,15},{16,24},{17,... | collective-permute-start | bytes 1572872 | tf_op jit(solution)/shard_map/ppermute | solution.py:328
  18.4 21.7 %collective-permute-start.4 = (f32[2,128,512]{2,1,0:T(8,128)S(1)}, f32[2,128,512]{2,1,0:T(8,128)S(1)}, u32[]{:S(2)}, u32[]{:S(2)}) collective-permute-start(f32[2,128,512]{2,1,0:T(8,128)S(1)} %get-tuple-element.35), channel_id=1, source_target_pairs={{0,24},{1,17},{2,26},{3,19},{4,28},{5,21},{6,30},{7,23},{16,0},{17... | collective-permute-start | bytes 1572872 | tf_op jit(solution)/shard_map/ppermute | solution.py:328
  21.4 18.7 %copy-start.17 = (f32[2,128,512]{2,1,0:T(8,128)}, f32[2,128,512]{2,1,0:T(8,128)S(1)}, u32[]{:S(2)}) copy-start(f32[2,128,512]{2,1,0:T(8,128)S(1)} %collective-permute-done.1.refs_4_) | copy-start | bytes 1572868
  21.4 18.7 %collective-permute-start.3 = (f32[2,128,512]{2,1,0:T(8,128)S(1)}, f32[2,128,512]{2,1,0:T(8,128)S(1)}, u32[]{:S(2)}, u32[]{:S(2)}) collective-permute-start(f32[2,128,512]{2,1,0:T(8,128)S(1)} %get-tuple-element.34.refs_3_), channel_id=1, source_target_pairs={{0,96},{1,33},{2,98},{3,35},{4,100},{5,37},{6,102},{7,39},{16,112}... | collective-permute-start | bytes 1572872 | tf_op jit(solution)/shard_map/ppermute | solution.py:327
  21.8 18.3 %collective-permute-start.5 = (f32[2,128,512]{2,1,0:T(8,128)S(1)}, f32[2,128,512]{2,1,0:T(8,128)}, u32[]{:S(2)}, u32[]{:S(2)}) collective-permute-start(f32[2,128,512]{2,1,0:T(8,128)S(1)} %collective-permute-done.1.refs_4_), channel_id=1, source_target_pairs={{0,32},{1,97},{2,34},{3,99},{4,36},{5,101},{6,38},{7,103},{16,48},... | collective-permute-start | bytes 1572872 | tf_op jit(solution)/shard_map/ppermute | solution.py:327
  40.1 1.0 copy-start.18
  42.3 41.5 %copy-start.11 = (f32[2,3,128,512]{3,2,1,0:T(8,128)}, f32[2,3,128,512]{3,2,1,0:T(8,128)S(1)}, u32[]{:S(2)}) copy-start(f32[2,3,128,512]{3,2,1,0:T(8,128)S(1)} %pad_maximum_fusion.refs_7_) | copy-start | bytes 4718596
  42.3 33.1 %collective-permute-start.8 = (f32[2,3,128,512]{3,2,1,0:T(8,128)S(1)}, f32[2,3,128,512]{3,2,1,0:T(8,128)}, u32[]{:S(2)}, u32[]{:S(2)}) collective-permute-start(f32[2,3,128,512]{3,2,1,0:T(8,128)S(1)} %pad_maximum_fusion.refs_7_), channel_id=1, source_target_pairs={{0,32},{1,97},{2,34},{3,99},{4,36},{5,101},{6,38},{7,103},{16,48},... | collective-permute-start | bytes 4718600 | tf_op jit(solution)/shard_map/ppermute | solution.py:327
  44.5 34.3 %collective-permute-start.6 = (f32[8,384,128]{2,1,0:T(8,128)}, f32[8,384,128]{2,1,0:T(8,128)S(1)}, u32[]{:S(2)}, u32[]{:S(2)}) collective-permute-start(f32[8,384,128]{2,1,0:T(8,128)} %all-to-all-done.refs_0_), channel_id=1, source_target_pairs={{0,16},{1,25},{2,18},{3,27},{4,20},{5,29},{6,22},{7,31},{16,8},{17... | collective-permute-start | bytes 4718600 | tf_op jit(solution)/shard_map/ppermute | solution.py:328
  46.1 35.2 %collective-permute-start.9 = (f32[2,3,128,512]{3,2,1,0:T(8,128)S(1)}, f32[2,3,128,512]{3,2,1,0:T(8,128)}, u32[]{:S(2)}, u32[]{:S(2)}) collective-permute-start(f32[2,3,128,512]{3,2,1,0:T(8,128)S(1)} %pad_maximum_fusion.refs_7_), channel_id=1, source_target_pairs={{0,96},{1,33},{2,98},{3,35},{4,100},{5,37},{6,102},{7,39},{16,112}... | collective-permute-start | bytes 4718600 | tf_op jit(solution)/shard_map/ppermute | solution.py:327
  46.9 36.8 %collective-permute-start.7 = (f32[8,384,128]{2,1,0:T(8,128)}, f32[8,384,128]{2,1,0:T(8,128)}, u32[]{:S(2)}, u32[]{:S(2)}) collective-permute-start(f32[8,384,128]{2,1,0:T(8,128)} %all-to-all-done.refs_0_), channel_id=1, source_target_pairs={{0,24},{1,17},{2,26},{3,19},{4,28},{5,21},{6,30},{7,23},{16,0},{17... | collective-permute-start | bytes 4718600 | tf_op jit(solution)/shard_map/ppermute | solution.py:328
  75.4 23.9 %collective-permute-start.10 = (f32[2,3,128,512]{3,2,1,0:T(8,128)}, f32[2,3,128,512]{3,2,1,0:T(8,128)S(1)}, u32[]{:S(2)}, u32[]{:S(2)}) collective-permute-start(f32[2,3,128,512]{3,2,1,0:T(8,128)} %collective-permute-done.8.refs_8_), channel_id=1, source_target_pairs={{0,32},{1,97},{2,34},{3,99},{4,36},{5,101},{6,38},{7,103},{16,48},... | collective-permute-start | bytes 4718600 | tf_op jit(solution)/shard_map/ppermute | solution.py:327
  78.9 4.9 %copy-start.16 = (f32[8,384,128]{2,1,0:T(8,128)}, f32[8,384,128]{2,1,0:T(8,128)S(1)}, u32[]{:S(2)}) copy-start(f32[8,384,128]{2,1,0:T(8,128)S(1)} %collective-permute-done.6.refs_1_) | copy-start | bytes 4718596
  78.9 20.4 %collective-permute-start.11 = (f32[8,384,128]{2,1,0:T(8,128)S(1)}, f32[8,384,128]{2,1,0:T(8,128)S(1)}, u32[]{:S(2)}, u32[]{:S(2)}) collective-permute-start(f32[8,384,128]{2,1,0:T(8,128)S(1)} %collective-permute-done.6.refs_1_), channel_id=1, source_target_pairs={{0,16},{1,25},{2,18},{3,27},{4,20},{5,29},{6,22},{7,31},{16,8},{17... | collective-permute-start | bytes 4718600 | tf_op jit(solution)/shard_map/ppermute | solution.py:328
  99.3 1.1 copy-start
  99.3 1.4 copy-start.1
  99.3 2.1 %copy-start.4 = (bf16[2,2,4,128,512]{4,3,2,1,0:T(8,128)(2,1)S(1)}, bf16[2,2,4,128,512]{4,3,2,1,0:T(8,128)(2,1)}, u32[]{:S(2)}) copy-start(bf16[2,2,4,128,512]{4,3,2,1,0:T(8,128)(2,1)} %get-tuple-element.52.src_b) | copy-start | bytes 6291460
  99.3 2.5 %copy-start.6 = (f32[2,384,512]{2,1,0:T(8,128)S(1)}, f32[2,384,512]{2,1,0:T(8,128)}, u32[]{:S(2)}) copy-start(f32[2,384,512]{2,1,0:T(8,128)} %get-tuple-element.51.src_sum) | copy-start | bytes 4718596
  101.8 8.2 %copy-start.3 = (bf16[2,2,4,128,512]{4,3,2,1,0:T(8,128)(2,1)S(1)}, bf16[2,2,4,128,512]{4,3,2,1,0:T(8,128)(2,1)}, u32[]{:S(2)}) copy-start(bf16[2,2,4,128,512]{4,3,2,1,0:T(8,128)(2,1)} %get-tuple-element.49.src_b) | copy-start | bytes 6291460
  101.8 8.2 %copy-start.5 = (f32[2,384,512]{2,1,0:T(8,128)S(1)}, f32[2,384,512]{2,1,0:T(8,128)}, u32[]{:S(2)}) copy-start(f32[2,384,512]{2,1,0:T(8,128)} %get-tuple-element.43.src_sum) | copy-start | bytes 4718596
  106.5 8.3 %collective-permute-start.12 = (f32[8,384,128]{2,1,0:T(8,128)S(1)}, f32[8,384,128]{2,1,0:T(8,128)S(1)}, u32[]{:S(2)}, u32[]{:S(2)}) collective-permute-start(f32[8,384,128]{2,1,0:T(8,128)S(1)} %shard_map.69), channel_id=1, source_target_pairs={{0,1},{1,0},{2,3},{3,2},{4,5},{5,4},{6,7},{7,6},{16,17},{17,16},{1... | collective-permute-start | bytes 4718600 | tf_op jit(solution)/shard_map/ppermute | solution.py:347
  116.1 4.3 %copy-start.13 = (f32[512]{0:T(512)S(1)}, f32[512]{0:T(512)}, u32[]{:S(2)}) copy-start(f32[512]{0:T(512)} %param.11) | copy-start | bytes 6148
  116.1 4.3 %copy-start.14 = (f32[8]{0:T(128)S(1)}, f32[8]{0:T(128)}, u32[]{:S(2)}) copy-start(f32[8]{0:T(128)} %param.10) | copy-start | bytes 100
  116.1 4.4 %copy-start.15 = (f32[6]{0:T(128)S(1)}, f32[6]{0:T(128)}, u32[]{:S(2)}) copy-start(f32[6]{0:T(128)} %param.9) | copy-start | bytes 76
  116.1 25.8 %copy-start.8 = (f32[384,256]{1,0:T(8,128)S(1)}, f32[384,256]{1,0:T(8,128)}, u32[]{:S(2)}) copy-start(f32[384,256]{1,0:T(8,128)} %given.1) | copy-start | bytes 1179652
  116.1 25.8 %all-to-all-start.1 = ((f32[8,384,128]{2,1,0:T(8,128)}), f32[8,384,128]{2,1,0:T(8,128)S(1)}, u32[]{:S(2)}, u32[]{:S(2)}) async-start(f32[8,384,128]{2,1,0:T(8,128)} %shard_map.70), calls=%async_computation.1 | async-start | bytes 3145728 | tf_op jit(solution)/shard_map/all_to_all | solution.py:348
  (2 other events, 1.5 us)

commit v6 on v5

--- a/solution.py
+++ b/solution.py
@@ -7,8 +7,8 @@
 from jax.experimental.pallas import tpu as pltpu
 from jax.sharding import Mesh, PartitionSpec as P
 
-AXES = ("z", "yl", "yh", "x", "core")
-SIZES = (4, 2, 2, 4, 2)
+AXES = ("z", "yl", "yh", "xh", "xl", "core")
+SIZES = (4, 2, 2, 2, 2, 2)
 F32, BF16 = jnp.float32, jnp.bfloat16
 
 
@@ -238,7 +238,7 @@
             copy.wait()
         value = total[1 - yl] + product(other[0], other[1], bh, bl)
         for x in range(4):
-            out[(1 - yl) * 4 + x] = value[:, x * 128 : x * 128 + 128]
+            out[(1 - yl) * 4 + x % 2 * 2 + x // 2] = value[:, x * 128 : x * 128 + 128]
 
         @pl.when(yh != zh)
         def _():
@@ -249,7 +249,7 @@
         for k in range(2):
             value = value + product(far[k, 0], far[k, 1], *(b[k, p].reshape(512, 512) for p in range(2)))
         for x in range(4):
-            out[yl * 4 + x] = value[:, x * 128 : x * 128 + 128]
+            out[yl * 4 + x % 2 * 2 + x // 2] = value[:, x * 128 : x * 128 + 128]
 
     return pl.pallas_call(
         body,
@@ -315,7 +315,8 @@
 
 
 def shards(integrals, amplitudes, driver, occ_rows, occ_cols, virtual):
-    z, yl, yh, x, core = (lax.axis_index(axis) for axis in AXES)
+    z, yl, yh, xh, xl, core = (lax.axis_index(axis) for axis in AXES)
+    x = xh * 2 + xl
     y = yh * 2 + yl
     way = 1 - 2 * core
     rows = driver.shape[0]
@@ -327,7 +328,7 @@
     on_z = lambda v, d: lax.ppermute(v, AXES, Z_ON[d])
     on_y = lambda v, d: lax.ppermute(v, AXES, Y_ON[d])
     wave = lambda *v: list(lax.optimization_barrier(v))
-    ints = lax.all_to_all(ints, ("x", "core"), 0, 0, tiled=True)
+    ints = lax.all_to_all(ints, ("xh", "xl", "core"), 0, 0, tiled=True)
     b, d, c = on_y(parts[1], 1), on_y(parts[2], 2), on_y(parts[3], 3)
     own1 = on_z(parts[0], 1)
     own3 = on_z(wave(parts[0], own1)[0], 3)
@@ -345,7 +346,7 @@
     other = last_products(number(1 - core, z, y, core), sum_other, ints2, bcd2, own_a, other_a, far_other, ended)
     mine = last_products(number(core, z, y, core), sum_mine, ints2, bcd2, own_a, other_a, far_mine, ended)
     mine = total_of(mine, lax.ppermute(other, AXES, SWAP))
-    mine = lax.all_to_all(mine, ("yl", "x"), 0, 0, tiled=True)
+    mine = lax.all_to_all(mine, ("yl", "xl", "xh"), 0, 0, tiled=True)
     row_energy = (occ_rows[:, None] - virtual[None, :]).reshape(-1)
     col_energy = (occ_cols[:, None] - virtual[None, :]).reshape(-1)
     row_part = lax.dynamic_slice_in_dim(row_energy, (z * 2 + yl) * rows, rows, 0)
@@ -355,6 +356,6 @@
 
 def solution(mesh):
     fine = Mesh(mesh.devices.reshape(SIZES), AXES)
-    row, col = ("z", "yl"), ("yh", "x", "core")
+    row, col = ("z", "yl"), ("yh", "xh", "xl", "core")
     in_specs = (P(row, col), P(row, col, None, None), P(row, col), P(), P(), P())
     return jax.shard_map(shards, mesh=fine, in_specs=in_specs, out_specs=P(row, col), check_vma=False)

time: 143 us -> 143 us (level)
  no operation moved by 1% of the time
where the time goes in v6:
time: 143 us
  waiting for transfers between devices  70.1 us (49%)
  starting transfers between devices  33.9 us (24%)
  Pallas kernels  30.5 us (21%)
  local copies, waits for them, and re-layouts  5.85 us (4%)
  other arithmetic  2.22 us (2%)
    ppermute x6, waiting for transfers between devices, shards(): on_z = lambda v, d: lax.ppermute(v, AXES, Z_ON[d])  31.5 us
    all_to_all x1, waiting for transfers between devices, shards(): mine = lax.all_to_all(mine, ('yl', 'xl', 'xh'), 0, 0, tiled=True)  21.1 us
    ppermute x6, waiting for transfers between devices, shards(): on_y = lambda v, d: lax.ppermute(v, AXES, Y_ON[d])  17.5 us
    pallas_call x1, Pallas kernels, first_products(): pl.pallas_call(body, in_specs=[SMALL] + [ANY] * 10, out_specs=[ANY] * 6 +...  14.8 us
    ppermute x6, starting transfers between devices, shards(): on_z = lambda v, d: lax.ppermute(v, AXES, Z_ON[d])  13.9 us
    pallas_call x2, Pallas kernels, last_products(): pl.pallas_call(body, in_specs=[SMALL] + [ANY] * 7, out_specs=pl.BlockSpec...  9.4 us
    ppermute x6, starting transfers between devices, shards(): on_y = lambda v, d: lax.ppermute(v, AXES, Y_ON[d])  6.37 us
    all_to_all x1, starting transfers between devices, shards(): ints = lax.all_to_all(ints, ('xh', 'xl', 'core'), 0, 0, tiled=True)  5.93 us
  transfers between devices with their start and end apart: 15, of which 7 were waited for; matrix products, arithmetic and copies ran while one was open for 1% of the time, Pallas kernels for 15%

profile of v6, /device:TPU:1, one launch (start us, length us, event | category | flops | bytes accessed | tf_op | source)
XLA Modules:
  0.0 142.8 jit_solution(2413193281256750834)
XLA Ops:
  0.0 1.4 copy-done.7
  1.4 2.6 %shard_map.64 = f32[8,384,128]{2,1,0:T(8,128)} custom-call(s32[1]{0:T(128)} %constant.53.clone.1.unused, f32[384,1024]{1,0:T(8,128)S(1)} %copy-done.7), custom_call_target="tpu_custom_call" | custom-call | bytes 3145728 | tf_op jit(solution)/shard_map/pallas_call | solution.py:36
  4.0 5.9 %all-to-all-start = ((f32[8,384,128]{2,1,0:T(8,128)}), f32[8,384,128]{2,1,0:T(8,128)}, u32[]{:S(2)}, u32[]{:S(2)}) async-start(f32[8,384,128]{2,1,0:T(8,128)} %shard_map.64), calls=%async_computation | async-start | bytes 3145728 | tf_op jit(solution)/shard_map/all_to_all | solution.py:331
  10.0 1.4 %shard_map.65 = (f32[2,128,512]{2,1,0:T(8,128)S(1)}, f32[2,128,512]{2,1,0:T(8,128)S(1)}, f32[2,128,512]{2,1,0:T(8,128)S(1)}, f32[2,128,512]{2,1,0:T(8,128)S(1)}) custom-call(s32[4]{0:T(128)S(1)} %pad_add_fusion.1.target, f32[4,32,8,512]{3,2,1,0:T(8,128)S(1)} %copy-done.2), custom_call_target="tpu_custom_call" | custom-call | bytes 4194304 | tf_op jit(solution)/shard_map/pallas_call | solution.py:36
  11.4 3.8 %collective-permute-start.1 = (f32[2,128,512]{2,1,0:T(8,128)S(1)}, f32[2,128,512]{2,1,0:T(8,128)S(1)}, u32[]{:S(2)}, u32[]{:S(2)}) collective-permute-start(f32[2,128,512]{2,1,0:T(8,128)S(1)} %get-tuple-element.34.refs_3_), channel_id=1, source_target_pairs={{0,32},{1,97},{2,34},{3,99},{4,36},{5,101},{6,38},{7,103},{16,48},... | collective-permute-start | bytes 1572872 | tf_op jit(solution)/shard_map/ppermute | solution.py:328
  15.3 2.7 %collective-permute-start = (f32[2,128,512]{2,1,0:T(8,128)S(1)}, f32[2,128,512]{2,1,0:T(8,128)S(1)}, u32[]{:S(2)}, u32[]{:S(2)}) collective-permute-start(f32[2,128,512]{2,1,0:T(8,128)S(1)} %get-tuple-element.31), channel_id=1, source_target_pairs={{0,16},{1,25},{2,18},{3,27},{4,20},{5,29},{6,22},{7,31},{16,8},{17... | collective-permute-start | bytes 1572872 | tf_op jit(solution)/shard_map/ppermute | solution.py:329
  18.4 0.7 collective-permute-start.4
  19.0 2.3 %collective-permute-done.1.refs_4_ = f32[2,128,512]{2,1,0:T(8,128)S(1)} collective-permute-done((f32[2,128,512]{2,1,0:T(8,128)S(1)}, f32[2,128,512]{2,1,0:T(8,128)S(1)}, u32[]{:S(2)}, u32[]{:S(2)}) %collective-permute-start.1) | collective-permute-done | bytes 524320 | tf_op jit(solution)/shard_map/ppermute | solution.py:328
  21.8 3.2 %collective-permute-start.5 = (f32[2,128,512]{2,1,0:T(8,128)S(1)}, f32[2,128,512]{2,1,0:T(8,128)}, u32[]{:S(2)}, u32[]{:S(2)}) collective-permute-start(f32[2,128,512]{2,1,0:T(8,128)S(1)} %collective-permute-done.1.refs_4_), channel_id=1, source_target_pairs={{0,32},{1,97},{2,34},{3,99},{4,36},{5,101},{6,38},{7,103},{16,48},... | collective-permute-start | bytes 1572872 | tf_op jit(solution)/shard_map/ppermute | solution.py:328
  24.9 14.7 %collective-permute-done = f32[2,128,512]{2,1,0:T(8,128)S(1)} collective-permute-done((f32[2,128,512]{2,1,0:T(8,128)S(1)}, f32[2,128,512]{2,1,0:T(8,128)S(1)}, u32[]{:S(2)}, u32[]{:S(2)}) %collective-permute-start) | collective-permute-done | bytes 524320 | tf_op jit(solution)/shard_map/ppermute | solution.py:329
  40.1 0.8 copy-done.12
  41.1 1.2 pad_maximum_fusion.refs_7_
  42.3 2.3 %collective-permute-start.8 = (f32[2,3,128,512]{3,2,1,0:T(8,128)S(1)}, f32[2,3,128,512]{3,2,1,0:T(8,128)}, u32[]{:S(2)}, u32[]{:S(2)}) collective-permute-start(f32[2,3,128,512]{3,2,1,0:T(8,128)S(1)} %pad_maximum_fusion.refs_7_), channel_id=1, source_target_pairs={{0,32},{1,97},{2,34},{3,99},{4,36},{5,101},{6,38},{7,103},{16,48},... | collective-permute-start | bytes 4718600 | tf_op jit(solution)/shard_map/ppermute | solution.py:328
  44.5 1.6 %collective-permute-start.6 = (f32[8,384,128]{2,1,0:T(8,128)}, f32[8,384,128]{2,1,0:T(8,128)S(1)}, u32[]{:S(2)}, u32[]{:S(2)}) collective-permute-start(f32[8,384,128]{2,1,0:T(8,128)} %all-to-all-done.refs_0_), channel_id=1, source_target_pairs={{0,16},{1,25},{2,18},{3,27},{4,20},{5,29},{6,22},{7,31},{16,8},{17... | collective-permute-start | bytes 4718600 | tf_op jit(solution)/shard_map/ppermute | solution.py:329
  46.1 0.8 collective-permute-start.9
  46.9 0.7 pad_add_fusion.at
  47.7 27.7 %collective-permute-done.8.refs_8_ = f32[2,3,128,512]{3,2,1,0:T(8,128)} collective-permute-done((f32[2,3,128,512]{3,2,1,0:T(8,128)S(1)}, f32[2,3,128,512]{3,2,1,0:T(8,128)}, u32[]{:S(2)}, u32[]{:S(2)}) %collective-permute-start.8) | collective-permute-done | bytes 1572896 | tf_op jit(solution)/shard_map/ppermute | solution.py:328
  75.4 3.5 %collective-permute-start.10 = (f32[2,3,128,512]{3,2,1,0:T(8,128)}, f32[2,3,128,512]{3,2,1,0:T(8,128)S(1)}, u32[]{:S(2)}, u32[]{:S(2)}) collective-permute-start(f32[2,3,128,512]{3,2,1,0:T(8,128)} %collective-permute-done.8.refs_8_), channel_id=1, source_target_pairs={{0,32},{1,97},{2,34},{3,99},{4,36},{5,101},{6,38},{7,103},{16,48},... | collective-permute-start | bytes 4718600 | tf_op jit(solution)/shard_map/ppermute | solution.py:328
  78.9 1.0 collective-permute-start.11
  79.9 1.5 %collective-permute-done.9.refs_9_ = f32[2,3,128,512]{3,2,1,0:T(8,128)} collective-permute-done((f32[2,3,128,512]{3,2,1,0:T(8,128)S(1)}, f32[2,3,128,512]{3,2,1,0:T(8,128)}, u32[]{:S(2)}, u32[]{:S(2)}) %collective-permute-start.9) | collective-permute-done | bytes 1572896 | tf_op jit(solution)/shard_map/ppermute | solution.py:328
  81.3 2.4 %collective-permute-done.7.refs_2_ = f32[8,384,128]{2,1,0:T(8,128)} collective-permute-done((f32[8,384,128]{2,1,0:T(8,128)}, f32[8,384,128]{2,1,0:T(8,128)}, u32[]{:S(2)}, u32[]{:S(2)}) %collective-permute-start.7) | collective-permute-done | bytes 1572896 | tf_op jit(solution)/shard_map/ppermute | solution.py:329
  83.7 14.8 %shard_map.66 = (bf16[2,384,512]{2,1,0:T(8,128)(2,1)}, bf16[2,384,512]{2,1,0:T(8,128)(2,1)}, bf16[2,2,4,128,512]{4,3,2,1,0:T(8,128)(2,1)}, bf16[2,2,4,128,512]{4...) custom-call(s32[3]{0:T(128)} %pad_add_fusion.at, ...), custom_call_target="tpu_custom_call" | custom-call | flops 7247757312 | bytes 25165824 | tf_op jit(solution)/shard_map/pallas_call | solution.py:190
  98.6 0.7 copy-done.10
  99.3 1.1 copy-done
  100.6 0.7 copy-done.4
  101.8 4.7 %shard_map.69 = f32[8,384,128]{2,1,0:T(8,128)S(1)} custom-call(s32[4]{0:T(128)S(1)} %add_add_fusion.1.at, f32[2,384,512]{2,1,0:T(8,128)S(1)} %copy-done.6, f32[8,384,128]{2,1,0:T(8,128)S(1)} %collective-permute-done.11.src_far, f32[2,3,128,512]{3,2,1,0:T(8,128)S(1)} %collective-permute-done.10.src_near, bf16[2,384,512]{2,1,0:T(8,128)(2,1)S(1)} %copy-done, ...), custom_call_target="tpu_custom_call" | custom-call | flops 2415919104 | bytes 8388608 | tf_op jit(solution)/shard_map/pallas_call | solution.py:254
  106.5 3.5 %collective-permute-start.12 = (f32[8,384,128]{2,1,0:T(8,128)S(1)}, f32[8,384,128]{2,1,0:T(8,128)S(1)}, u32[]{:S(2)}, u32[]{:S(2)}) collective-permute-start(f32[8,384,128]{2,1,0:T(8,128)S(1)} %shard_map.69), channel_id=1, source_target_pairs={{0,1},{1,0},{2,3},{3,2},{4,5},{5,4},{6,7},{7,6},{16,17},{17,16},{1... | collective-permute-start | bytes 4718600 | tf_op jit(solution)/shard_map/ppermute | solution.py:348
  110.0 4.7 %shard_map.68.a = f32[8,384,128]{2,1,0:T(8,128)S(1)} custom-call(s32[4]{0:T(128)S(1)} %add_add_fusion.at, f32[2,384,512]{2,1,0:T(8,128)S(1)} %copy-done.5, f32[8,384,128]{2,1,0:T(8,128)S(1)} %collective-permute-done.11.src_far, f32[2,3,128,512]{3,2,1,0:T(8,128)S(1)} %collective-permute-done.10.src_near, bf16[2,384,512]{2,1,0:T(8,128)(2,1)S(1)} %copy-done, ...), custom_call_target="tpu_custom_call" | custom-call | flops 2415919104 | bytes 8388608 | tf_op jit(solution)/shard_map/pallas_call | solution.py:254
  114.8 1.3 shard_map.70
  116.1 4.3 %all-to-all-start.1 = ((f32[8,384,128]{2,1,0:T(8,128)}), f32[8,384,128]{2,1,0:T(8,128)S(1)}, u32[]{:S(2)}, u32[]{:S(2)}) async-start(f32[8,384,128]{2,1,0:T(8,128)} %shard_map.70), calls=%async_computation.1 | async-start | bytes 3145728 | tf_op jit(solution)/shard_map/all_to_all | solution.py:349
  120.8 21.1 %all-to-all-done.1.part = f32[8,384,128]{2,1,0:T(8,128)S(1)} async-done(((f32[8,384,128]{2,1,0:T(8,128)}), f32[8,384,128]{2,1,0:T(8,128)S(1)}, u32[]{:S(2)}, u32[]{:S(2)}) %all-to-all-start.1) | async-done | bytes 1572896 | tf_op jit(solution)/shard_map/all_to_all | solution.py:349
  141.9 0.9 shard_map.71
  (56 shorter events, 2.8 us)
Async XLA Ops:
  0.0 1.4 copy-start.7
  4.0 6.0 %copy-start.2 = (f32[4,32,8,512]{3,2,1,0:T(8,128)S(1)}, f32[4,32,8,512]{3,2,1,0:T(8,128)}, u32[]{:S(2)}) copy-start(f32[4,32,8,512]{3,2,1,0:T(8,128)} %src.2) | copy-start | bytes 6291460
  4.0 36.1 %all-to-all-start = ((f32[8,384,128]{2,1,0:T(8,128)}), f32[8,384,128]{2,1,0:T(8,128)}, u32[]{:S(2)}, u32[]{:S(2)}) async-start(f32[8,384,128]{2,1,0:T(8,128)} %shard_map.64), calls=%async_computation | async-start | bytes 3145728 | tf_op jit(solution)/shard_map/all_to_all | solution.py:331
  11.4 30.8 %copy-start.9 = (f32[2,128,512]{2,1,0:T(8,128)}, f32[2,128,512]{2,1,0:T(8,128)S(1)}, u32[]{:S(2)}) copy-start(f32[2,128,512]{2,1,0:T(8,128)S(1)} %get-tuple-element.34.refs_3_) | copy-start | bytes 1572868
  11.4 10.0 %collective-permute-start.1 = (f32[2,128,512]{2,1,0:T(8,128)S(1)}, f32[2,128,512]{2,1,0:T(8,128)S(1)}, u32[]{:S(2)}, u32[]{:S(2)}) collective-permute-start(f32[2,128,512]{2,1,0:T(8,128)S(1)} %get-tuple-element.34.refs_3_), channel_id=1, source_target_pairs={{0,32},{1,97},{2,34},{3,99},{4,36},{5,101},{6,38},{7,103},{16,48},... | collective-permute-start | bytes 1572872 | tf_op jit(solution)/shard_map/ppermute | solution.py:328
  15.3 24.3 %collective-permute-start = (f32[2,128,512]{2,1,0:T(8,128)S(1)}, f32[2,128,512]{2,1,0:T(8,128)S(1)}, u32[]{:S(2)}, u32[]{:S(2)}) collective-permute-start(f32[2,128,512]{2,1,0:T(8,128)S(1)} %get-tuple-element.31), channel_id=1, source_target_pairs={{0,16},{1,25},{2,18},{3,27},{4,20},{5,29},{6,22},{7,31},{16,8},{17... | collective-permute-start | bytes 1572872 | tf_op jit(solution)/shard_map/ppermute | solution.py:329
  18.0 21.6 %collective-permute-start.2 = (f32[2,128,512]{2,1,0:T(8,128)S(1)}, f32[2,128,512]{2,1,0:T(8,128)S(1)}, u32[]{:S(2)}, u32[]{:S(2)}) collective-permute-start(f32[2,128,512]{2,1,0:T(8,128)S(1)} %get-tuple-element.33), channel_id=1, source_target_pairs={{0,8},{1,9},{2,10},{3,11},{4,12},{5,13},{6,14},{7,15},{16,24},{17,... | collective-permute-start | bytes 1572872 | tf_op jit(solution)/shard_map/ppermute | solution.py:329
  18.4 21.7 %collective-permute-start.4 = (f32[2,128,512]{2,1,0:T(8,128)S(1)}, f32[2,128,512]{2,1,0:T(8,128)S(1)}, u32[]{:S(2)}, u32[]{:S(2)}) collective-permute-start(f32[2,128,512]{2,1,0:T(8,128)S(1)} %get-tuple-element.35), channel_id=1, source_target_pairs={{0,24},{1,17},{2,26},{3,19},{4,28},{5,21},{6,30},{7,23},{16,0},{17... | collective-permute-start | bytes 1572872 | tf_op jit(solution)/shard_map/ppermute | solution.py:329
  21.4 18.7 %copy-start.17 = (f32[2,128,512]{2,1,0:T(8,128)}, f32[2,128,512]{2,1,0:T(8,128)S(1)}, u32[]{:S(2)}) copy-start(f32[2,128,512]{2,1,0:T(8,128)S(1)} %collective-permute-done.1.refs_4_) | copy-start | bytes 1572868
  21.4 18.7 %collective-permute-start.3 = (f32[2,128,512]{2,1,0:T(8,128)S(1)}, f32[2,128,512]{2,1,0:T(8,128)S(1)}, u32[]{:S(2)}, u32[]{:S(2)}) collective-permute-start(f32[2,128,512]{2,1,0:T(8,128)S(1)} %get-tuple-element.34.refs_3_), channel_id=1, source_target_pairs={{0,96},{1,33},{2,98},{3,35},{4,100},{5,37},{6,102},{7,39},{16,112}... | collective-permute-start | bytes 1572872 | tf_op jit(solution)/shard_map/ppermute | solution.py:328
  21.8 18.3 %collective-permute-start.5 = (f32[2,128,512]{2,1,0:T(8,128)S(1)}, f32[2,128,512]{2,1,0:T(8,128)}, u32[]{:S(2)}, u32[]{:S(2)}) collective-permute-start(f32[2,128,512]{2,1,0:T(8,128)S(1)} %collective-permute-done.1.refs_4_), channel_id=1, source_target_pairs={{0,32},{1,97},{2,34},{3,99},{4,36},{5,101},{6,38},{7,103},{16,48},... | collective-permute-start | bytes 1572872 | tf_op jit(solution)/shard_map/ppermute | solution.py:328
  40.1 1.0 copy-start.18
  42.3 41.5 %copy-start.11 = (f32[2,3,128,512]{3,2,1,0:T(8,128)}, f32[2,3,128,512]{3,2,1,0:T(8,128)S(1)}, u32[]{:S(2)}) copy-start(f32[2,3,128,512]{3,2,1,0:T(8,128)S(1)} %pad_maximum_fusion.refs_7_) | copy-start | bytes 4718596
  42.3 33.1 %collective-permute-start.8 = (f32[2,3,128,512]{3,2,1,0:T(8,128)S(1)}, f32[2,3,128,512]{3,2,1,0:T(8,128)}, u32[]{:S(2)}, u32[]{:S(2)}) collective-permute-start(f32[2,3,128,512]{3,2,1,0:T(8,128)S(1)} %pad_maximum_fusion.refs_7_), channel_id=1, source_target_pairs={{0,32},{1,97},{2,34},{3,99},{4,36},{5,101},{6,38},{7,103},{16,48},... | collective-permute-start | bytes 4718600 | tf_op jit(solution)/shard_map/ppermute | solution.py:328
  44.5 34.3 %collective-permute-start.6 = (f32[8,384,128]{2,1,0:T(8,128)}, f32[8,384,128]{2,1,0:T(8,128)S(1)}, u32[]{:S(2)}, u32[]{:S(2)}) collective-permute-start(f32[8,384,128]{2,1,0:T(8,128)} %all-to-all-done.refs_0_), channel_id=1, source_target_pairs={{0,16},{1,25},{2,18},{3,27},{4,20},{5,29},{6,22},{7,31},{16,8},{17... | collective-permute-start | bytes 4718600 | tf_op jit(solution)/shard_map/ppermute | solution.py:329
  46.1 35.2 %collective-permute-start.9 = (f32[2,3,128,512]{3,2,1,0:T(8,128)S(1)}, f32[2,3,128,512]{3,2,1,0:T(8,128)}, u32[]{:S(2)}, u32[]{:S(2)}) collective-permute-start(f32[2,3,128,512]{3,2,1,0:T(8,128)S(1)} %pad_maximum_fusion.refs_7_), channel_id=1, source_target_pairs={{0,96},{1,33},{2,98},{3,35},{4,100},{5,37},{6,102},{7,39},{16,112}... | collective-permute-start | bytes 4718600 | tf_op jit(solution)/shard_map/ppermute | solution.py:328
  46.9 36.8 %collective-permute-start.7 = (f32[8,384,128]{2,1,0:T(8,128)}, f32[8,384,128]{2,1,0:T(8,128)}, u32[]{:S(2)}, u32[]{:S(2)}) collective-permute-start(f32[8,384,128]{2,1,0:T(8,128)} %all-to-all-done.refs_0_), channel_id=1, source_target_pairs={{0,24},{1,17},{2,26},{3,19},{4,28},{5,21},{6,30},{7,23},{16,0},{17... | collective-permute-start | bytes 4718600 | tf_op jit(solution)/shard_map/ppermute | solution.py:329
  75.4 23.9 %collective-permute-start.10 = (f32[2,3,128,512]{3,2,1,0:T(8,128)}, f32[2,3,128,512]{3,2,1,0:T(8,128)S(1)}, u32[]{:S(2)}, u32[]{:S(2)}) collective-permute-start(f32[2,3,128,512]{3,2,1,0:T(8,128)} %collective-permute-done.8.refs_8_), channel_id=1, source_target_pairs={{0,32},{1,97},{2,34},{3,99},{4,36},{5,101},{6,38},{7,103},{16,48},... | collective-permute-start | bytes 4718600 | tf_op jit(solution)/shard_map/ppermute | solution.py:328
  78.9 4.9 %copy-start.16 = (f32[8,384,128]{2,1,0:T(8,128)}, f32[8,384,128]{2,1,0:T(8,128)S(1)}, u32[]{:S(2)}) copy-start(f32[8,384,128]{2,1,0:T(8,128)S(1)} %collective-permute-done.6.refs_1_) | copy-start | bytes 4718596
  78.9 20.4 %collective-permute-start.11 = (f32[8,384,128]{2,1,0:T(8,128)S(1)}, f32[8,384,128]{2,1,0:T(8,128)S(1)}, u32[]{:S(2)}, u32[]{:S(2)}) collective-permute-start(f32[8,384,128]{2,1,0:T(8,128)S(1)} %collective-permute-done.6.refs_1_), channel_id=1, source_target_pairs={{0,16},{1,25},{2,18},{3,27},{4,20},{5,29},{6,22},{7,31},{16,8},{17... | collective-permute-start | bytes 4718600 | tf_op jit(solution)/shard_map/ppermute | solution.py:329
  99.3 1.1 copy-start
  99.3 1.4 copy-start.1
  99.3 2.1 %copy-start.4 = (bf16[2,2,4,128,512]{4,3,2,1,0:T(8,128)(2,1)S(1)}, bf16[2,2,4,128,512]{4,3,2,1,0:T(8,128)(2,1)}, u32[]{:S(2)}) copy-start(bf16[2,2,4,128,512]{4,3,2,1,0:T(8,128)(2,1)} %get-tuple-element.52.src_b) | copy-start | bytes 6291460
  99.3 2.5 %copy-start.6 = (f32[2,384,512]{2,1,0:T(8,128)S(1)}, f32[2,384,512]{2,1,0:T(8,128)}, u32[]{:S(2)}) copy-start(f32[2,384,512]{2,1,0:T(8,128)} %get-tuple-element.51.src_sum) | copy-start | bytes 4718596
  101.8 8.2 %copy-start.3 = (bf16[2,2,4,128,512]{4,3,2,1,0:T(8,128)(2,1)S(1)}, bf16[2,2,4,128,512]{4,3,2,1,0:T(8,128)(2,1)}, u32[]{:S(2)}) copy-start(bf16[2,2,4,128,512]{4,3,2,1,0:T(8,128)(2,1)} %get-tuple-element.49.src_b) | copy-start | bytes 6291460
  101.8 8.2 %copy-start.5 = (f32[2,384,512]{2,1,0:T(8,128)S(1)}, f32[2,384,512]{2,1,0:T(8,128)}, u32[]{:S(2)}) copy-start(f32[2,384,512]{2,1,0:T(8,128)} %get-tuple-element.43.src_sum) | copy-start | bytes 4718596
  106.5 8.3 %collective-permute-start.12 = (f32[8,384,128]{2,1,0:T(8,128)S(1)}, f32[8,384,128]{2,1,0:T(8,128)S(1)}, u32[]{:S(2)}, u32[]{:S(2)}) collective-permute-start(f32[8,384,128]{2,1,0:T(8,128)S(1)} %shard_map.69), channel_id=1, source_target_pairs={{0,1},{1,0},{2,3},{3,2},{4,5},{5,4},{6,7},{7,6},{16,17},{17,16},{1... | collective-permute-start | bytes 4718600 | tf_op jit(solution)/shard_map/ppermute | solution.py:348
  116.1 4.3 %copy-start.13 = (f32[512]{0:T(512)S(1)}, f32[512]{0:T(512)}, u32[]{:S(2)}) copy-start(f32[512]{0:T(512)} %param.11) | copy-start | bytes 6148
  116.1 4.3 %copy-start.14 = (f32[8]{0:T(128)S(1)}, f32[8]{0:T(128)}, u32[]{:S(2)}) copy-start(f32[8]{0:T(128)} %param.10) | copy-start | bytes 100
  116.1 4.4 %copy-start.15 = (f32[6]{0:T(128)S(1)}, f32[6]{0:T(128)}, u32[]{:S(2)}) copy-start(f32[6]{0:T(128)} %param.9) | copy-start | bytes 76
  116.1 25.8 %copy-start.8 = (f32[384,256]{1,0:T(8,128)S(1)}, f32[384,256]{1,0:T(8,128)}, u32[]{:S(2)}) copy-start(f32[384,256]{1,0:T(8,128)} %given.1) | copy-start | bytes 1179652
  116.1 25.8 %all-to-all-start.1 = ((f32[8,384,128]{2,1,0:T(8,128)}), f32[8,384,128]{2,1,0:T(8,128)S(1)}, u32[]{:S(2)}, u32[]{:S(2)}) async-start(f32[8,384,128]{2,1,0:T(8,128)} %shard_map.70), calls=%async_computation.1 | async-start | bytes 3145728 | tf_op jit(solution)/shard_map/all_to_all | solution.py:349
  (2 other events, 1.5 us)
